TPU v7x, 32 devices: a whole 2x2x4 slice. The times are simulated.
32 devices in a mesh: gx: 4 (over z), gz: 4 (over y, x), gy: 2 (over core).
Axes of the slice: x: 2, y: 2, z: 4, core: 2. Of those that a mesh axis runs over, the one named last changes fastest.
Arguments:
- velocity: float32 [3, 128, 192, 512], P(None, ('gx', 'gy'), None, 'gz'), may hold values from -6 to 6
- metric_x: float32 [128], P(('gx', 'gy')), may hold values from 0.5 to 2
- metric_y: float32 [192], replicated, may hold values from 0.5 to 2
- metric_z: float32 [512], P('gz'), may hold values from 0.5 to 2
- x_inverse: float32 [128, 16], P(('gx', 'gy')), may hold values from -5 to 5, as said below
- y_inverse: float32 [192, 192], replicated, may hold values from -5 to 5, as said below
- z_inverse: float32 [512, 128], P('gz'), may hold values from -5 to 5, as said below
Outputs:
- gradient: float32 [3, 3, 128, 192, 512], P(None, None, ('gx', 'gy'), None, 'gz')
- convection: float32 [3, 128, 192, 512], P(None, ('gx', 'gy'), None, 'gz')
Inputs may be any that keep to these rules, and one draw needn't show every extreme that they name: Rows b * 16 to b * 16 + 15 of x_inverse hold the inverse of a 16 x 16 tridiagonal matrix with unit diagonal whose row r has one value between 0.2 and 0.4 on both sides of the diagonal (where they exist), drawn afresh for each row and block. y_inverse holds the inverse of such a 192 x 192 matrix. Likewise for z_inverse with blocks of 128 rows.
All inputs are finite; a program needn't handle non-finite values.
Results may differ from a plain program's by a relative error of at most 0.0003.
Values sent between devices are 32-bit elements; how exact they have to be, the bound alone decides.
No kernel may reach another device: no remote copies, remote signals or barrier semaphores. Data moves between devices by JAX's collectives and lax.ppermute only.
A program may use at most 192 MiB of HBM per device.

v0:
```python
import functools

import jax
import jax.numpy as jnp
from jax import lax
from jax.experimental import pallas as pl
from jax.experimental.pallas import tpu as pltpu
from jax.sharding import PartitionSpec as P

COUPLING = 1.0 / 3.0
NEAR = 7.0 / 9.0
FAR = 1.0 / 36.0
F32 = jnp.float32
BF16 = jnp.bfloat16
SMEM = pltpu.SMEM
VMEM_LIMIT = 20 * 1024 * 1024
GROUP = 4


def split(values):
    high = values.astype(BF16)
    low = (values - high.astype(F32)).astype(BF16)
    return high, low


def dot(a, b):
    return lax.dot_general(a, b, (((1,), (0,)), ((), ())), preferred_element_type=F32)


def dot_nt(a, b):
    return lax.dot_general(a, b, (((1,), (1,)), ((), ())), preferred_element_type=F32)


def params():
    return pltpu.CompilerParams(vmem_limit_bytes=VMEM_LIMIT)


def six(velocity, direction):
    return list(velocity) + [velocity[i] * velocity[direction] for i in range(3)]


def times_stencil(inverse):
    rows, length = inverse.shape
    zeros = jnp.zeros((rows, 2), F32)
    wide = jnp.concatenate([zeros, inverse, zeros], axis=1)

    def column(offset):
        return wide[:, 2 + offset : 2 + offset + length]

    return NEAR * (column(-1) - column(1)) + FAR * (column(-2) - column(2))


def in_vmem(*shape):
    return pltpu.VMEM(shape, F32)


ANY = pl.BlockSpec(memory_space=pl.ANY)
WHOLE = pl.BlockSpec(memory_space=pltpu.VMEM)
SCALARS = pl.BlockSpec(memory_space=SMEM)


def cost(array, passes):
    return pl.CostEstimate(flops=passes, bytes_accessed=passes, transcendentals=0)


def layer_shape(*shape):
    return jax.ShapeDtypeStruct(shape, F32)


class Ends:
    def __init__(self, n):
        self.first = lax.axis_index("gy") == 0
        self.n = n
        self.o = jnp.where(self.first, 0, n - 1)
        self.o1 = jnp.where(self.first, 1, n - 2)
        self.q = jnp.where(self.first, n - 1, 0)
        self.q1 = jnp.where(self.first, n - 2, 1)
        self.sign_o = jnp.where(self.first, -1.0, 1.0).astype(F32)
        self.sign_q = -self.sign_o


class Table:
    def __init__(self, n):
        self.source, self.forward, self.backward = 0, n, 2 * n
        self.send, self.last = 3 * n, 4 * n + 2
        self.oo, self.oo1, self.qo, self.qo1, self.qq = range(5 * n + 4, 5 * n + 9)
        self.size = 5 * n + 9


def prepare_kernel(
    n, ny, xi_ref, mx_ref, yi_ref, my_ref, zi_ref, mz_ref, v_ref,
    own_ref, halo_ref, table_ref, y_ref, y_metric_ref, z_ref, z_metric_ref, x_ref, m_ref, sem,
):
    ends = Ends(n)
    nz = v_ref.shape[3]
    small = [pltpu.make_async_copy(xi_ref, x_ref, sem.at[9]), pltpu.make_async_copy(mx_ref, m_ref, sem.at[10])]
    copies = []
    for i in range(3):
        copies.append(pltpu.make_async_copy(v_ref.at[i, ends.o], own_ref.at[pl.ds(i * ny, ny)], sem.at[3 * i]))
        for j in range(2):
            plane = jnp.where(ends.first, n - 2 + j, j)
            copies.append(
                pltpu.make_async_copy(
                    v_ref.at[i, plane], halo_ref.at[pl.ds((2 * i + j) * ny, ny)], sem.at[3 * i + 1 + j]
                )
            )
    copies.append(pltpu.make_async_copy(zi_ref, z_ref, sem.at[11]))
    copies.append(pltpu.make_async_copy(mz_ref, z_metric_ref, sem.at[12]))
    copies.append(pltpu.make_async_copy(yi_ref, y_ref, sem.at[13]))
    copies.append(pltpu.make_async_copy(my_ref, y_metric_ref, sem.at[14]))
    for copy in small + copies:
        copy.start()
    for copy in small:
        copy.wait()

    wide = jnp.concatenate([x_ref[...], jnp.zeros((n, nz - n), F32)], axis=1)
    own_ref[3 * ny : 3 * ny + n, :] = wide
    halo_ref[6 * ny : 6 * ny + n, :] = wide

    table = Table(n)
    first = ends.first

    def spread(value):
        return jnp.broadcast_to(value, (8, nz))

    def entry(i, j):
        return spread(x_ref[i : i + 1, j : j + 1])

    metric = [spread(m_ref[0:1, k : k + 1]) for k in range(n)]
    above = [entry(i, i + 1) for i in range(n - 1)]
    diagonal = [entry(i, i) for i in range(n)]
    ratio = [-above[i] / diagonal[i + 1] for i in range(n - 1)]
    ratio.append(-entry(n - 1, n - 2) / diagonal[n - 2] * diagonal[n - 1])
    for k in range(n):
        if k == 0:
            source = metric[k]
        elif k == n - 1:
            source = diagonal[k] * metric[k]
        else:
            source = (1.0 + ratio[k] * ratio[k - 1]) * metric[k]
        table_ref[table.source + k] = FAR * source
        table_ref[table.forward + k] = ratio[k] * metric[k] / metric[k - 1] if k > 0 else metric[k]
        table_ref[table.backward + k] = ratio[k] * metric[k] / metric[k + 1] if k < n - 1 else metric[k]

    top = [entry(0, k) for k in range(n)]
    bottom = [entry(n - 1, k) for k in range(n)]
    outer = [jnp.where(first, top[k], bottom[k]) for k in range(n)]
    inner = [jnp.where(first, bottom[k], top[k]) for k in range(n)]
    sign_o, sign_q = ends.sign_o, ends.sign_q
    for base, row, factor in ((table.send, outer, -COUPLING), (table.last, inner, 1.0)):

        def at(k):
            return row[k] if 0 <= k < n else jnp.zeros_like(row[0])

        for k in range(n):
            value = factor * (NEAR * (at(k - 1) - at(k + 1)) + FAR * (at(k - 2) - at(k + 2)))
            if base == table.send:
                if k == 0:
                    value = value + jnp.where(first, NEAR, 0.0)
                elif k == 1:
                    value = value + jnp.where(first, FAR, 0.0)
                elif k == n - 2:
                    value = value - jnp.where(first, 0.0, FAR)
                elif k == n - 1:
                    value = value - jnp.where(first, 0.0, NEAR)
            table_ref[base + k] = value
        at_q = jnp.where(first, row[n - 1], row[0])
        at_q1 = jnp.where(first, row[n - 2], row[1])
        near = factor * sign_q * (NEAR * at_q + FAR * at_q1)
        far = factor * sign_q * FAR * at_q
        table_ref[base + n] = jnp.where(first, near, far)
        table_ref[base + n + 1] = jnp.where(first, far, near)
    table_ref[table.oo] = jnp.where(first, outer[0], outer[n - 1])
    table_ref[table.oo1] = jnp.where(first, outer[1], outer[n - 2])
    table_ref[table.qo] = jnp.where(first, inner[0], inner[n - 1])
    table_ref[table.qo1] = jnp.where(first, inner[1], inner[n - 2])
    table_ref[table.qq] = jnp.where(first, inner[n - 1], inner[0])
    for copy in copies:
        copy.wait()


def prepare(x_inverse, metric_x, y_inverse, metric_y, z_inverse, metric_z, velocity):
    _, n, ny, nz = velocity.shape
    inputs = (x_inverse, metric_x, y_inverse, metric_y, z_inverse, metric_z, velocity)
    return pl.pallas_call(
        functools.partial(prepare_kernel, n, ny),
        in_specs=[ANY] * 7,
        out_specs=[WHOLE] * 7,
        out_shape=[
            layer_shape(3 * ny + n, nz),
            layer_shape(6 * ny + n, nz),
            in_vmem(Table(n).size, 8, nz),
            in_vmem(ny, ny),
            in_vmem(1, ny),
            in_vmem(nz, nz),
            in_vmem(1, nz),
        ],
        scratch_shapes=[pltpu.VMEM((n, n), F32), pltpu.VMEM((1, n), F32), pltpu.SemaphoreType.DMA((15,))],
        compiler_params=params(),
        name="prepare",
    )(*(pltpu.with_memory_space_constraint(value, pltpu.HBM) for value in inputs))


def x_ends_kernel(n, ny, table_ref, v_ref, halo_ref, w_ref, l_ref):
    table = Table(n)

    def tile(index, carry):
        start = pl.multiple_of(index * 8, 8)
        rows = pl.ds(start, 8)
        w = [None] * 6
        l = [None] * 6
        for k in range(n + 2):
            if k < n:
                fields = six([v_ref[i, k, rows, :] for i in range(3)], 0)
            else:
                fields = six([halo_ref[pl.ds((2 * i + k - n) * ny + start, 8), :] for i in range(3)], 0)
            a, b = table_ref[table.send + k], table_ref[table.last + k]
            for f in range(6):
                w[f] = a * fields[f] if k == 0 else w[f] + a * fields[f]
                l[f] = b * fields[f] if k == 0 else l[f] + b * fields[f]
        for f in range(6):
            w_ref[f, rows, :] = w[f]
            l_ref[f, rows, :] = l[f]
        return carry

    lax.fori_loop(0, ny // 8, tile, 0)


def x_ends(table, velocity, halo):
    _, n, ny, nz = velocity.shape
    return pl.pallas_call(
        functools.partial(x_ends_kernel, n, ny),
        in_specs=[WHOLE] * 3,
        out_specs=[WHOLE, WHOLE],
        out_shape=[layer_shape(6, ny, nz), layer_shape(6, ny, nz)],
        compiler_params=params(),
        cost_estimate=cost(velocity, 3),
        name="x_ends",
    )(table, velocity, halo)


def x_face_kernel(n, ny, table_ref, wr_ref, ws_ref, l_ref, own_ref, near_ref, after_ref, w_ref, e_ref):
    ends = Ends(n)
    table = Table(n)
    shape = (8, wr_ref.shape[2])

    def corner(i, j):
        row = 3 * ny + i
        return jnp.broadcast_to(near_ref[row : row + 1, j : j + 1], shape)

    p_oo = jnp.where(ends.first, corner(n - 1, n - 1), corner(0, 0))
    p_oo1 = jnp.where(ends.first, corner(n - 1, n - 2), corner(0, 1))
    x_qo = table_ref[table.qo]
    inverse_den = 1.0 / (1.0 - COUPLING * COUPLING * table_ref[table.oo] * p_oo)
    sent_weight = COUPLING * p_oo
    own_weight = COUPLING * FAR * ends.sign_o * p_oo1
    near_weight = COUPLING * FAR * ends.sign_o * COUPLING * table_ref[table.oo1] * p_oo
    end_weight = ends.sign_o * FAR * table_ref[table.qo1]

    def tile(index, carry):
        start = pl.multiple_of(index * 8, 8)
        rows = pl.ds(start, 8)
        own = six([own_ref[pl.ds(i * ny + start, 8), :] for i in range(3)], 0)
        near = six([near_ref[pl.ds(i * ny + start, 8), :] for i in range(3)], 0)
        for f in range(6):
            w = wr_ref[f, rows, :] - sent_weight * ws_ref[f, rows, :]
            w = (w + own_weight * own[f] + near_weight * near[f]) * inverse_den
            w_ref[f, rows, :] = 36.0 * w
            e_ref[f, rows, :] = l_ref[f, rows, :] + x_qo * w + end_weight * near[f]
        return carry

    lax.fori_loop(0, ny // 8, tile, 0)


def x_face(table, received, sent, partial, own, near, after, n):
    _, ny, _ = received.shape
    layer = layer_shape(*received.shape)
    return pl.pallas_call(
        functools.partial(x_face_kernel, n, ny),
        in_specs=[WHOLE] * 6 + [ANY],
        out_specs=[WHOLE, WHOLE],
        out_shape=[layer, layer],
        compiler_params=params(),
        cost_estimate=cost(received, 1),
        name="x_face",
    )(table, received, sent, partial, own, near, after)


def x_solve_kernel(
    n, ny, table_ref, v_ref, near_ref, halo_ref, w_ref, e_ref, r_ref, part_ref, held_ref, gradient_ref, convection_ref,
    g_ref, c_ref, sem,
):
    ends = Ends(n)
    table = Table(n)
    nz = v_ref.shape[3]
    parts = sem.shape[1]
    share = ny // parts

    def corner(i):
        row = 6 * ny + i
        return jnp.broadcast_to(halo_ref[row : row + 1, i : i + 1], (8, nz))

    p_qq = jnp.where(ends.first, corner(0), corner(n - 1))
    weight = COUPLING * p_qq
    scale = -36.0 * COUPLING / (1.0 - COUPLING * COUPLING * table_ref[table.qq] * p_qq)
    near_first = jnp.where(ends.first, 28.0 * ends.sign_q, ends.sign_q)
    near_second = jnp.where(ends.first, ends.sign_q, 28.0 * ends.sign_q)
    far_first = jnp.where(ends.first, ends.sign_q, 0.0)
    far_second = jnp.where(ends.first, 0.0, ends.sign_q)

    def tile(index, carry):
        start = pl.multiple_of(index * 8, 8)
        rows = pl.ds(start, 8)
        near = six([near_ref[pl.ds(i * ny + start, 8), :] for i in range(3)], 0)
        halo_a = six([halo_ref[pl.ds(2 * i * ny + start, 8), :] for i in range(3)], 0)
        halo_b = six([halo_ref[pl.ds((2 * i + 1) * ny + start, 8), :] for i in range(3)], 0)
        for f in range(6):
            if f < 3:
                line = [v_ref[f, k, rows, :] for k in range(n)]
            else:
                line = [v_ref[f - 3, k, rows, :] * v_ref[0, k, rows, :] for k in range(n)]
            outer_0 = w_ref[f, rows, :]
            outer_1 = ends.sign_o * near[f]
            inner_0 = near_first * halo_a[f] + near_second * halo_b[f]
            inner_0 = inner_0 + scale * (r_ref[f, rows, :] - weight * e_ref[f, rows, :])
            inner_1 = far_first * halo_a[f] + far_second * halo_b[f]
            added = {
                0: jnp.where(ends.first, outer_0, inner_0),
                1: jnp.where(ends.first, outer_1, inner_1),
                n - 1: jnp.where(ends.first, inner_0, outer_0),
                n - 2: jnp.where(ends.first, inner_1, outer_1),
            }
            forward = []
            for k in range(n):
                if k == 0:
                    source = 28.0 * line[1] + line[2]
                elif k == 1:
                    source = 28.0 * (line[2] - line[0]) + line[3]
                elif k == n - 1:
                    source = -28.0 * line[n - 2] - line[n - 3]
                elif k == n - 2:
                    source = 28.0 * (line[n - 1] - line[n - 3]) - line[n - 4]
                else:
                    source = 28.0 * (line[k + 1] - line[k - 1]) + (line[k + 2] - line[k - 2])
                if k in added:
                    source = source + added[k]
                value = table_ref[table.source + k] * source
                if k > 0:
                    value = value - table_ref[table.forward + k] * forward[k - 1]
                forward.append(value)
            solved = None
            for k in reversed(range(n)):
                solved = forward[k] if k == n - 1 else forward[k] - table_ref[table.backward + k] * solved
                if f < 3:
                    g_ref[f, k, rows, :] = solved
                else:
                    c_ref[f - 3, k, rows, :] = solved + part_ref[f - 3, k, rows, :]
        return carry

    def copies(part):
        rows = pl.ds(pl.multiple_of(part * share, 8), share)
        return (
            pltpu.make_async_copy(g_ref.at[:, :, rows], gradient_ref.at[:, 0, :, rows], sem.at[0, part]),
            pltpu.make_async_copy(c_ref.at[:, :, rows], convection_ref.at[:, :, rows], sem.at[1, part]),
        )

    def step(part, carry):
        lax.fori_loop(part * (share // 8), (part + 1) * (share // 8), tile, 0)
        for copy in copies(part):
            copy.start()
        return carry

    lax.fori_loop(0, parts, step, 0)

    def drain(part, carry):
        for copy in copies(part):
            copy.wait()
        return carry

    lax.fori_loop(0, parts, drain, 0)


def x_solve(table, velocity, near, halo, outer, ends, received, partial, gradient, parts=6):
    _, n, ny, nz = velocity.shape
    return pl.pallas_call(
        functools.partial(x_solve_kernel, n, ny),
        in_specs=[WHOLE] * 8 + [ANY],
        out_specs=[ANY, ANY],
        out_shape=[layer_shape(*gradient.shape), layer_shape(3, n, ny, nz)],
        scratch_shapes=[
            pltpu.VMEM((3, n, ny, nz), F32),
            pltpu.VMEM((3, n, ny, nz), F32),
            pltpu.SemaphoreType.DMA((2, parts)),
        ],
        input_output_aliases={8: 0},
        compiler_params=params(),
        cost_estimate=cost(velocity, 5),
        name="x_solve",
    )(table, velocity, near, halo, outer, ends, received, partial, gradient)


def y_kernel(n, inv_ref, m_ref, v_ref, part_ref, after_ref, gradient_ref, c_ref, high_ref, low_ref, out_ref, sem):
    ny = inv_ref.shape[0]
    nz = v_ref.shape[3]
    row = lax.broadcasted_iota(jnp.int32, (ny, ny), 0)
    column = lax.broadcasted_iota(jnp.int32, (ny, ny), 1)
    metric = jnp.sum(jnp.where(row == column, m_ref[...], 0.0), axis=1, keepdims=True)
    high, low = split(times_stencil(inv_ref[...]) * metric)
    high_ref[...] = high
    low_ref[...] = low

    def copy(group):
        planes = pl.ds(group * GROUP, GROUP)
        return pltpu.make_async_copy(out_ref.at[:, planes], gradient_ref.at[:, 1, planes], sem.at[group])

    def step(group, carry):
        for u in range(GROUP):
            p = group * GROUP + u
            fields = six([v_ref[i, p] for i in range(3)], 1)
            for a in (0, 2, 4):
                high, low = split(jnp.concatenate(fields[a : a + 2], axis=1))
                result = dot(high_ref[...], high) + dot(low_ref[...], high) + dot(high_ref[...], low)
                for j in range(2):
                    f = a + j
                    value = result[:, j * nz : (j + 1) * nz]
                    if f < 3:
                        out_ref[f, p] = value
                    else:
                        c_ref[f - 3, p] = value + part_ref[f - 3, p]
        copy(group).start()
        return carry

    lax.fori_loop(0, n // GROUP, step, 0)

    def drain(group, carry):
        copy(group).wait()
        return carry

    lax.fori_loop(0, n // GROUP, drain, 0)


def y_solve(y_inverse, metric, velocity, partial, after):
    _, n, ny, nz = velocity.shape
    return pl.pallas_call(
        functools.partial(y_kernel, n),
        in_specs=[WHOLE] * 4 + [ANY],
        out_specs=[ANY, WHOLE],
        out_shape=[layer_shape(3, 3, n, ny, nz), in_vmem(3, n, ny, nz)],
        scratch_shapes=[
            pltpu.VMEM((ny, ny), BF16),
            pltpu.VMEM((ny, ny), BF16),
            pltpu.VMEM((3, n, ny, nz), F32),
            pltpu.SemaphoreType.DMA((n // GROUP,)),
        ],
        input_output_aliases={3: 1},
        compiler_params=params(),
        cost_estimate=cost(velocity, 4),
        name="y_solve",
    )(y_inverse, metric, velocity, partial, after)


LINES = 128


def z_own_kernel(
    n, inv_ref, m_ref, v_ref, after_ref, g_ref, c_ref, right_ref, left_ref, right_2_ref, left_2_ref, main_ref
):
    nz = inv_ref.shape[0]
    ny = v_ref.shape[2]
    high, low = split(times_stencil(inv_ref[...]).T * m_ref[...])
    both = jnp.concatenate([high, low], axis=1)
    main_ref[...] = jnp.concatenate([both, both], axis=0)
    first_scale = 1.0 / m_ref[0:1, 0:1]
    last_scale = 1.0 / m_ref[0:1, nz - 1 : nz]
    lane = lax.broadcasted_iota(jnp.int32, (ny, nz), 1)

    def corner(i, j):
        return jnp.broadcast_to(inv_ref[i : i + 1, j : j + 1], (1, LINES))

    m = nz - 1
    corners_right = [corner(m, m), corner(m, m - 1), corner(m, 0), corner(m, 1)]
    corners_left = [corner(0, 0), corner(0, 1), corner(0, m), corner(0, m - 1)]

    def step(group, carry):
        gathered = []
        for u in range(GROUP):
            p = group * GROUP + u
            velocities = [v_ref[i, p] for i in range(3)]
            columns = jnp.zeros((ny, nz), F32)
            for f, field in enumerate(six(velocities, 2)):
                high, low = split(field)
                both = dot(jnp.concatenate([high, low], axis=1), main_ref[...])
                value = both[:, :nz] + both[:, nz:]
                if f < 3:
                    g_ref[f, p] = value
                else:
                    c_ref[f - 3, p] = value
                columns = jnp.where(lane // 2 == f, pltpu.roll(value, 1 + 2 * f, axis=1), columns)
            for i in range(3):
                columns = jnp.where(lane // 4 == 3 + i, pltpu.roll(velocities[i], 14 + 4 * i, axis=1), columns)
            gathered.append(columns)
        lines = jnp.concatenate(gathered, axis=0)
        for j in range(GROUP * ny // LINES):
            turned = lines[j * LINES : (j + 1) * LINES].T

            def row(index):
                return turned[index : index + 1]

            def block(ends, scale, column, corners):
                rows = [row(ends + 2 * f) * scale for f in range(6)] + corners[0:2]
                rows = rows + [row(12 + 4 * i + column) for i in range(3)] + corners[2:3]
                rows = rows + [row(13 + 4 * i + column) for i in range(3)] + corners[3:4]
                return jnp.concatenate(rows, axis=0)

            index = group * (GROUP * ny // LINES) + j
            to_right = block(0, last_scale, 0, corners_right)
            to_left = block(1, first_scale, 2, corners_left)
            right_ref[index] = to_right
            left_ref[index] = to_left
            right_2_ref[index] = to_right[8:16]
            left_2_ref[index] = to_left[8:16]
        return carry

    lax.fori_loop(0, n // GROUP, step, 0)


def z_own(z_inverse, metric, velocity, after):
    _, n, ny, nz = velocity.shape
    return pl.pallas_call(
        functools.partial(z_own_kernel, n),
        in_specs=[WHOLE, WHOLE, WHOLE, ANY],
        out_specs=[WHOLE] * 6,
        out_shape=[in_vmem(3, n, ny, nz)] * 2
        + [layer_shape(n * ny // LINES, 16, LINES)] * 2
        + [layer_shape(n * ny // LINES, 8, LINES)] * 2,
        scratch_shapes=[pltpu.VMEM((2 * nz, 2 * nz), BF16)],
        compiler_params=params(),
        cost_estimate=cost(velocity, 3),
        name="z_own",
    )(z_inverse, metric, velocity, after)


def z_side(own_right, own_left, left, right, left_2, right_2):
    index = lax.broadcasted_iota(jnp.int32, (8, LINES), 0)

    def row(values, i):
        return jnp.broadcast_to(values[i : i + 1], (8, LINES))

    def fields(velocities):
        products = velocities * row(velocities, 2)
        return jnp.where(index < 3, velocities, pltpu.roll(products, 3, axis=0))

    def pair(velocities):
        return fields(velocities), fields(pltpu.roll(velocities, 4, axis=0))

    def from_left(velocities):
        far, near = pair(velocities)
        return -NEAR * near - FAR * far, -FAR * near

    def from_right(velocities):
        near, far = pair(velocities)
        return NEAR * near + FAR * far, FAR * near

    def first_value(values, at_left, at_right):
        return (
            values[0:8]
            + row(values, 6) * at_left[0]
            + row(values, 7) * at_left[1]
            + row(values, 11) * at_right[0]
            + row(values, 15) * at_right[1]
        )

    def last_value(values, at_left, at_right):
        return (
            values[0:8]
            + row(values, 11) * at_left[0]
            + row(values, 15) * at_left[1]
            + row(values, 6) * at_right[0]
            + row(values, 7) * at_right[1]
        )

    at_left, at_right = from_left(left[8:16]), from_right(right[8:16])
    own_first = first_value(own_left, at_left, at_right)
    own_last = last_value(own_right, at_left, at_right)
    left_value = last_value(left, from_left(left_2), from_right(own_left[8:16]))
    right_value = first_value(right, from_left(own_right[8:16]), from_right(right_2))
    left_tail, right_head = row(left, 6), row(right, 6)
    left_final = (left_value - COUPLING * left_tail * own_first) / (
        1.0 - COUPLING * COUPLING * left_tail * row(own_left, 6)
    )
    right_start = (right_value - COUPLING * right_head * own_last) / (
        1.0 - COUPLING * COUPLING * right_head * row(own_right, 6)
    )
    return jnp.concatenate(
        [at_left[0] - COUPLING * left_final, at_left[1], at_right[0] - COUPLING * right_start, at_right[1]], axis=0
    )


def z_join_kernel(
    n, inv_ref, m_ref, g_ref, part_ref, own_right_ref, own_left_ref, left_ref, right_ref, left_2_ref, right_2_ref, held_ref,
    gradient_ref, c_ref, side_ref, out_ref, sem,
):
    nz = inv_ref.shape[0]
    ny = g_ref.shape[2]
    columns = inv_ref[...].T * m_ref[...]
    index = lax.broadcasted_iota(jnp.int32, (32, nz), 0)
    kind = index // 8
    picked = jnp.where(
        kind == 0,
        columns[0:1],
        jnp.where(kind == 1, columns[1:2], jnp.where(kind == 2, columns[nz - 1 : nz], columns[nz - 2 : nz - 1])),
    )
    wide = jnp.concatenate([jnp.where(index % 8 == f, picked, 0.0) for f in range(6)], axis=1)
    high, low = split(wide)
    side_ref[...] = jnp.concatenate([high, high, low], axis=0)
    blocks = GROUP * ny // LINES

    def copy(group):
        planes = pl.ds(group * GROUP, GROUP)
        return pltpu.make_async_copy(out_ref.at[:, planes], gradient_ref.at[:, 2, planes], sem.at[group])

    def step(group, carry):
        sides = []
        for j in range(blocks):
            lines = (own_right_ref, own_left_ref, left_ref, right_ref, left_2_ref, right_2_ref)
            high, low = split(z_side(*(ref[group * blocks + j] for ref in lines)).T)
            sides.append(jnp.concatenate([high, low, high], axis=1))
        for pair in range(GROUP // 2):
            half = blocks // (GROUP // 2)
            lines = jnp.concatenate(sides[pair * half : (pair + 1) * half], axis=0)
            for f in range(0, 6, 2):
                added = dot(lines, side_ref[:, f * nz : (f + 2) * nz])
                for u in range(2):
                    p = group * GROUP + 2 * pair + u
                    for j in range(2):
                        value = added[u * ny : (u + 1) * ny, j * nz : (j + 1) * nz]
                        if f + j < 3:
                            out_ref[f + j, p] = value + g_ref[f + j, p]
                        else:
                            c_ref[f + j - 3, p] = value + part_ref[f + j - 3, p]
        copy(group).start()
        return carry

    lax.fori_loop(0, n // GROUP, step, 0)

    def drain(group, carry):
        copy(group).wait()
        return carry

    lax.fori_loop(0, n // GROUP, drain, 0)


def z_join(z_inverse, metric, own, partial, lines, gradient):
    _, n, ny, nz = own.shape
    return pl.pallas_call(
        functools.partial(z_join_kernel, n),
        in_specs=[WHOLE] * 10 + [ANY],
        out_specs=[ANY, WHOLE],
        out_shape=[layer_shape(*gradient.shape), in_vmem(3, n, ny, nz)],
        scratch_shapes=[
            pltpu.VMEM((96, 6 * nz), BF16),
            pltpu.VMEM((3, n, ny, nz), F32),
            pltpu.SemaphoreType.DMA((n // GROUP,)),
        ],
        input_output_aliases={10: 0, 3: 1},
        compiler_params=params(),
        cost_estimate=cost(own, 3),
        name="z_join",
    )(z_inverse, metric, own, partial, *lines, gradient)


def on_device(mesh, velocity, metric_x, metric_y, metric_z, x_inverse, y_inverse, z_inverse):
    n = velocity.shape[1]
    blocks = mesh.shape["gx"] * 2
    across = [(i, (i + 1) % blocks) for i in range(1, blocks, 2)]
    across = across + [(j, i) for i, j in across]
    beside = [(0, 1), (1, 0)]
    count = mesh.shape["gz"]

    def shift(by):
        return [(i, (i + by) % count) for i in range(count)]

    own, inner, table, y_inverse, metric_y, z_inverse, metric_z = prepare(
        x_inverse, metric_x[None], y_inverse, metric_y[None], z_inverse, metric_z[None], velocity
    )
    near = lax.ppermute(own, ("gx", "gy"), across)
    halo = lax.ppermute(inner, "gy", beside)
    held = pltpu.with_memory_space_constraint(velocity, pltpu.VMEM)

    x_sent, x_partial = x_ends(table, held, halo)
    x_received = lax.ppermute(x_sent, ("gx", "gy"), across)

    z_gradient, convection, to_right, to_left, to_right_2, to_left_2 = z_own(z_inverse, metric_z, held, x_sent)
    z_lines = (
        to_right,
        to_left,
        lax.ppermute(to_right, "gz", shift(1)),
        lax.ppermute(to_left, "gz", shift(-1)),
        lax.ppermute(to_right_2, "gz", shift(2)),
        lax.ppermute(to_left_2, "gz", shift(-2)),
    )

    gradient, convection = y_solve(y_inverse, metric_y, held, convection, to_right)
    gradient, convection = z_join(z_inverse, metric_z, z_gradient, convection, z_lines, gradient)

    outer, x_end = x_face(table, x_received, x_sent, x_partial, own, near, convection, n)
    x_other = lax.ppermute(x_end, "gy", beside)
    return tuple(x_solve(table, held, near, halo, outer, x_end, x_other, convection, gradient))


def solution(mesh):
    return jax.shard_map(
        functools.partial(on_device, mesh),
        mesh=mesh,
        in_specs=(
            P(None, ("gx", "gy"), None, "gz"),
            P(("gx", "gy")),
            P(),
            P("gz"),
            P(("gx", "gy"), None),
            P(),
            P("gz", None),
        ),
        out_specs=(P(None, None, ("gx", "gy"), None, "gz"), P(None, ("gx", "gy"), None, "gz")),
        check_vma=False,
    )
```

profile of v0, /device:TPU:0, one launch (start us, length us, event | category | flops | bytes accessed | tf_op | source)
XLA Modules:
  0.0 45.1 jit_solution(1304471466211564969)
XLA Ops:
  0.6 0.0 copy-start
  0.6 1.6 %prepare.1 = (f32[592,128]{1,0:T(8,128)S(1)}, f32[1168,128]{1,0:T(8,128)S(1)}, f32[89,8,128]{2,1,0:T(8,128)S(1)}, f32[192,192]{1,0:T(8,128)S(1)}, f32[1,192]{1,0...) custom-call(f32[16,16]{1,0:T(8,128)} %xi_ref.1, f32[1,16]{1,0:T(1,128)} %bitcast.4, f32[192,192]{1,0:T(8,128)} %yi_ref.1, ...), custom_call_target="tpu_custom_call" | custom-call | tf_op jit(solution)/shard_map/prepare/pallas_call | solution.py:185
  2.3 0.5 %collective-permute-start.1 = (f32[1168,128]{1,0:T(8,128)S(1)}, f32[1168,128]{1,0:T(8,128)S(1)}, u32[]{:S(2)}, u32[]{:S(2)}) collective-permute-start(f32[1168,128]{1,0:T(8,128)S(1)} %get-tuple-element.25), channel_id=1, source_target_pairs={{0,1},{1,0},{2,3},{3,2},{4,5},{5,4},{6,7},{7,6},{8,9},{9,8},{10,11... | collective-permute-start | bytes 1794056 | tf_op jit(solution)/shard_map/ppermute | solution.py:687
  2.8 1.6 %collective-permute-done.1.halo_ref = f32[1168,128]{1,0:T(8,128)S(1)} collective-permute-done((f32[1168,128]{1,0:T(8,128)S(1)}, f32[1168,128]{1,0:T(8,128)S(1)}, u32[]{:S(2)}, u32[]{:S(2)}) %collective-permute-start.1) | collective-permute-done | bytes 598048 | tf_op jit(solution)/shard_map/ppermute | solution.py:687
  4.5 0.0 copy-done
  4.5 2.2 %x_ends.1 = (f32[6,192,128]{2,1,0:T(8,128)S(1)}, f32[6,192,128]{2,1,0:T(8,128)S(1)}) custom-call(f32[89,8,128]{2,1,0:T(8,128)S(1)} %get-tuple-element.23.table_ref, f32[3,16,192,128]{3,2,1,0:T(8,128)S(1)} %copy-done, f32[1168,128]{1,0:T(8,128)S(1)} %collective-permute-done.1.halo_ref), custom_call_target="tpu_custom_call" | custom-call | flops 3 | bytes 3 | tf_op jit(solution)/shard_map/x_ends/pallas_call | solution.py:231
  6.6 4.8 %collective-permute-start.2 = (f32[6,192,128]{2,1,0:T(8,128)S(1)}, f32[6,192,128]{2,1,0:T(8,128)S(1)}, u32[]{:S(2)}, u32[]{:S(2)}) collective-permute-start(f32[6,192,128]{2,1,0:T(8,128)S(1)} %get-tuple-element.26.after_ref.ws_ref), channel_id=1, source_target_pairs={{1,8},{9,16},{17,24},{25,0},{8,1},{16,9},{24,17},{0,25},{3,10},{11... | collective-permute-start | bytes 1769480 | tf_op jit(solution)/shard_map/ppermute | solution.py:691
  11.4 0.1 collective-permute-start
  11.5 5.1 %z_own.1 = (f32[3,16,192,128]{3,2,1,0:T(8,128)S(1)}, f32[3,16,192,128]{3,2,1,0:T(8,128)S(1)}, f32[24,16,128]{2,1,0:T(8,128)S(1)}, f32[24,16,128]{2,1,0:T(8,128)S...) custom-call(f32[128,128]{1,0:T(8,128)S(1)} %get-tuple-element.28.inv_ref, ...), custom_call_target="tpu_custom_call" | custom-call | flops 3 | bytes 3 | tf_op jit(solution)/shard_map/z_own/pallas_call | solution.py:529
  16.6 1.7 %collective-permute-start.5 = (f32[24,8,128]{2,1,0:T(8,128)S(1)}, f32[24,8,128]{2,1,0:T(8,128)S(1)}, u32[]{:S(2)}, u32[]{:S(2)}) collective-permute-start(f32[24,8,128]{2,1,0:T(8,128)S(1)} %get-tuple-element.37), channel_id=1, source_target_pairs={{0,4},{2,6},{4,0},{6,2},{1,5},{3,7},{5,1},{7,3},{8,12},{10,14},{12... | collective-permute-start | bytes 294920 | tf_op jit(solution)/shard_map/ppermute | solution.py:699
  18.3 1.5 %collective-permute-start.3 = (f32[24,16,128]{2,1,0:T(8,128)S(1)}, f32[24,16,128]{2,1,0:T(8,128)S(1)}, u32[]{:S(2)}, u32[]{:S(2)}) collective-permute-start(f32[24,16,128]{2,1,0:T(8,128)S(1)} %get-tuple-element.34.after_ref.own_right_ref), channel_id=1, source_target_pairs={{0,2},{2,4},{4,6},{6,0},{1,3},{3,5},{5,7},{7,1},{8,10},{10,12},{12... | collective-permute-start | bytes 589832 | tf_op jit(solution)/shard_map/ppermute | solution.py:697
  19.8 1.4 %collective-permute-start.4 = (f32[24,16,128]{2,1,0:T(8,128)S(1)}, f32[24,16,128]{2,1,0:T(8,128)S(1)}, u32[]{:S(2)}, u32[]{:S(2)}) collective-permute-start(f32[24,16,128]{2,1,0:T(8,128)S(1)} %get-tuple-element.36.own_left_ref), channel_id=1, source_target_pairs={{0,6},{2,0},{4,2},{6,4},{1,7},{3,1},{5,3},{7,5},{8,14},{10,8},{12,... | collective-permute-start | bytes 589832 | tf_op jit(solution)/shard_map/ppermute | solution.py:698
  21.2 3.9 %collective-permute-done.5.left_2_ref = f32[24,8,128]{2,1,0:T(8,128)S(1)} collective-permute-done((f32[24,8,128]{2,1,0:T(8,128)S(1)}, f32[24,8,128]{2,1,0:T(8,128)S(1)}, u32[]{:S(2)}, u32[]{:S(2)}) %collective-permute-start.5) | collective-permute-done | bytes 98336 | tf_op jit(solution)/shard_map/ppermute | solution.py:699
  25.1 0.0 collective-permute-start.6
  25.1 6.2 %y_solve.1 = (f32[3,3,16,192,128]{4,3,2,1,0:T(8,128)}, f32[3,16,192,128]{3,2,1,0:T(8,128)S(1)}) custom-call(f32[192,192]{1,0:T(8,128)S(1)} %get-tuple-element.31.inv_ref, f32[1,192]{1,0:T(1,128)S(1)} %get-tuple-element.32.m_ref, f32[3,16,192,128]{3,2,1,0:T(8,128)S(1)} %copy-done, ...), custom_call_target="tpu_custom_call", output_to_operand_aliasing={{1}: (3, {})} | custom-call | flops 4 | bytes 4 | tf_op jit(solution)/shard_map/y_solve/pallas_call | solution.py:444
  31.4 0.0 collective-permute-done.6.right_2_ref
  31.4 0.0 collective-permute-done.3.left_ref
  31.4 0.0 collective-permute-done.4.right_ref
  31.4 4.6 %z_join.1 = (f32[3,3,16,192,128]{4,3,2,1,0:T(8,128)}, f32[3,16,192,128]{3,2,1,0:T(8,128)S(1)}) custom-call(f32[128,128]{1,0:T(8,128)S(1)} %get-tuple-element.28.inv_ref, f32[1,128]{1,0:T(1,128)S(1)} %get-tuple-element.29.m_ref, f32[3,16,192,128]{3,2,1,0:T(8,128)S(1)} %get-tuple-element.30.g_ref, ...), custom_call_target="tpu_custom_call", output_to_operand_aliasing={{0}: (10, {}), {1}: (3, {})} | custom-call | flops 3 | bytes 3 | tf_op jit(solution)/shard_map/z_join/pallas_call | solution.py:655
  36.0 0.0 collective-permute-done.near_ref
  36.0 0.0 collective-permute-done.2.wr_ref
  36.0 0.6 %x_face.1 = (f32[6,192,128]{2,1,0:T(8,128)S(1)}, f32[6,192,128]{2,1,0:T(8,128)S(1)}) custom-call(f32[89,8,128]{2,1,0:T(8,128)S(1)} %get-tuple-element.23.table_ref, f32[6,192,128]{2,1,0:T(8,128)S(1)} %collective-permute-done.2.wr_ref, f32[6,192,128]{2,1,0:T(8,128)S(1)} %get-tuple-element.26.after_ref.ws_ref, f32[6,192,128]{2,1,0:T(8,128)S(1)} %get-tuple-element.27.l_ref, ...), custom_call_target="tpu_custom_call" | custom-call | flops 1 | bytes 1 | tf_op jit(solution)/shard_map/x_face/pallas_call | solution.py:278
  36.6 0.1 collective-permute-start.7
  36.7 2.0 %collective-permute-done.7.r_ref = f32[6,192,128]{2,1,0:T(8,128)S(1)} collective-permute-done((f32[6,192,128]{2,1,0:T(8,128)S(1)}, f32[6,192,128]{2,1,0:T(8,128)S(1)}, u32[]{:S(2)}, u32[]{:S(2)}) %collective-permute-start.7) | collective-permute-done | bytes 589856 | tf_op jit(solution)/shard_map/ppermute | solution.py:707
  38.7 6.4 %x_solve.1 = (f32[3,3,16,192,128]{4,3,2,1,0:T(8,128)}, f32[3,16,192,128]{3,2,1,0:T(8,128)}) custom-call(f32[89,8,128]{2,1,0:T(8,128)S(1)} %get-tuple-element.23.table_ref, f32[3,16,192,128]{3,2,1,0:T(8,128)S(1)} %copy-done, f32[592,128]{1,0:T(8,128)S(1)} %collective-permute-done.near_ref, ...), custom_call_target="tpu_custom_call", output_to_operand_aliasing={{0}: (8, {})} | custom-call | flops 5 | bytes 5 | tf_op jit(solution)/shard_map/x_solve/pallas_call | solution.py:385
Async XLA Ops:
  0.6 3.8 %copy-start = (f32[3,16,192,128]{3,2,1,0:T(8,128)S(1)}, f32[3,16,192,128]{3,2,1,0:T(8,128)}, u32[]{:S(2)}) copy-start(f32[3,16,192,128]{3,2,1,0:T(8,128)} %v_ref.9) | copy-start | bytes 14155780
  2.3 2.2 %collective-permute-start.1 = (f32[1168,128]{1,0:T(8,128)S(1)}, f32[1168,128]{1,0:T(8,128)S(1)}, u32[]{:S(2)}, u32[]{:S(2)}) collective-permute-start(f32[1168,128]{1,0:T(8,128)S(1)} %get-tuple-element.25), channel_id=1, source_target_pairs={{0,1},{1,0},{2,3},{3,2},{4,5},{5,4},{6,7},{7,6},{8,9},{9,8},{10,11... | collective-permute-start | bytes 1794056 | tf_op jit(solution)/shard_map/ppermute | solution.py:687
  6.6 29.4 %collective-permute-start.2 = (f32[6,192,128]{2,1,0:T(8,128)S(1)}, f32[6,192,128]{2,1,0:T(8,128)S(1)}, u32[]{:S(2)}, u32[]{:S(2)}) collective-permute-start(f32[6,192,128]{2,1,0:T(8,128)S(1)} %get-tuple-element.26.after_ref.ws_ref), channel_id=1, source_target_pairs={{1,8},{9,16},{17,24},{25,0},{8,1},{16,9},{24,17},{0,25},{3,10},{11... | collective-permute-start | bytes 1769480 | tf_op jit(solution)/shard_map/ppermute | solution.py:691
  11.4 24.6 %collective-permute-start = (f32[592,128]{1,0:T(8,128)S(1)}, f32[592,128]{1,0:T(8,128)S(1)}, u32[]{:S(2)}, u32[]{:S(2)}) collective-permute-start(f32[592,128]{1,0:T(8,128)S(1)} %get-tuple-element.24.own_ref), channel_id=1, source_target_pairs={{1,8},{9,16},{17,24},{25,0},{8,1},{16,9},{24,17},{0,25},{3,10},{11... | collective-permute-start | bytes 909320 | tf_op jit(solution)/shard_map/ppermute | solution.py:686
  16.6 8.5 %collective-permute-start.5 = (f32[24,8,128]{2,1,0:T(8,128)S(1)}, f32[24,8,128]{2,1,0:T(8,128)S(1)}, u32[]{:S(2)}, u32[]{:S(2)}) collective-permute-start(f32[24,8,128]{2,1,0:T(8,128)S(1)} %get-tuple-element.37), channel_id=1, source_target_pairs={{0,4},{2,6},{4,0},{6,2},{1,5},{3,7},{5,1},{7,3},{8,12},{10,14},{12... | collective-permute-start | bytes 294920 | tf_op jit(solution)/shard_map/ppermute | solution.py:699
  18.3 13.1 %collective-permute-start.3 = (f32[24,16,128]{2,1,0:T(8,128)S(1)}, f32[24,16,128]{2,1,0:T(8,128)S(1)}, u32[]{:S(2)}, u32[]{:S(2)}) collective-permute-start(f32[24,16,128]{2,1,0:T(8,128)S(1)} %get-tuple-element.34.after_ref.own_right_ref), channel_id=1, source_target_pairs={{0,2},{2,4},{4,6},{6,0},{1,3},{3,5},{5,7},{7,1},{8,10},{10,12},{12... | collective-permute-start | bytes 589832 | tf_op jit(solution)/shard_map/ppermute | solution.py:697
  19.8 11.6 %collective-permute-start.4 = (f32[24,16,128]{2,1,0:T(8,128)S(1)}, f32[24,16,128]{2,1,0:T(8,128)S(1)}, u32[]{:S(2)}, u32[]{:S(2)}) collective-permute-start(f32[24,16,128]{2,1,0:T(8,128)S(1)} %get-tuple-element.36.own_left_ref), channel_id=1, source_target_pairs={{0,6},{2,0},{4,2},{6,4},{1,7},{3,1},{5,3},{7,5},{8,14},{10,8},{12,... | collective-permute-start | bytes 589832 | tf_op jit(solution)/shard_map/ppermute | solution.py:698
  25.1 6.2 %collective-permute-start.6 = (f32[24,8,128]{2,1,0:T(8,128)S(1)}, f32[24,8,128]{2,1,0:T(8,128)S(1)}, u32[]{:S(2)}, u32[]{:S(2)}) collective-permute-start(f32[24,8,128]{2,1,0:T(8,128)S(1)} %get-tuple-element.38), channel_id=1, source_target_pairs={{0,4},{2,6},{4,0},{6,2},{1,5},{3,7},{5,1},{7,3},{8,12},{10,14},{12... | collective-permute-start | bytes 294920 | tf_op jit(solution)/shard_map/ppermute | solution.py:700
  36.6 2.1 %collective-permute-start.7 = (f32[6,192,128]{2,1,0:T(8,128)S(1)}, f32[6,192,128]{2,1,0:T(8,128)S(1)}, u32[]{:S(2)}, u32[]{:S(2)}) collective-permute-start(f32[6,192,128]{2,1,0:T(8,128)S(1)} %get-tuple-element.42.e_ref), channel_id=1, source_target_pairs={{0,1},{1,0},{2,3},{3,2},{4,5},{5,4},{6,7},{7,6},{8,9},{9,8},{10,11... | collective-permute-start | bytes 1769480 | tf_op jit(solution)/shard_map/ppermute | solution.py:707
where the time goes:
time: 45.6 us; the launch traced here: 45.1 us
  Pallas kernels  26.7 us (59%)
  starting transfers between devices  10.1 us (22%)
  waiting for transfers between devices  7.55 us (17%)
  between operations  0.74 us (2%)
    pallas_call x1, Pallas kernels, x_solve(): pl.pallas_call(functools.partial(x_solve_kernel, n, ny), in_specs=[WHOLE]...  6.38 us
    pallas_call x1, Pallas kernels, y_solve(): pl.pallas_call(functools.partial(y_kernel, n), in_specs=[WHOLE] * 4 + [AN...  6.23 us
    pallas_call x1, Pallas kernels, z_own(): pl.pallas_call(functools.partial(z_own_kernel, n), in_specs=[WHOLE, WHOLE...  5.1 us
    ppermute x1, starting transfers between devices, on_device(): x_received = lax.ppermute(x_sent, ('gx', 'gy'), across)  4.78 us
    pallas_call x1, Pallas kernels, z_join(): pl.pallas_call(functools.partial(z_join_kernel, n), in_specs=[WHOLE] * 10...  4.63 us
    ppermute x1, waiting for transfers between devices, on_device(): lax.ppermute(to_right_2, 'gz', shift(2))  3.9 us
    pallas_call x1, Pallas kernels, x_ends(): pl.pallas_call(functools.partial(x_ends_kernel, n, ny), in_specs=[WHOLE]...  2.17 us
    ppermute x1, waiting for transfers between devices, on_device(): x_other = lax.ppermute(x_end, 'gy', beside)  1.99 us
  transfers between devices with their start and end apart: 8, of which 3 were waited for; matrix products, arithmetic and copies ran while one was open for 0% of the time, Pallas kernels for 35%

commit v1 on v0

--- a/solution.py
+++ b/solution.py
@@ -15,6 +15,8 @@
 SMEM = pltpu.SMEM
 VMEM_LIMIT = 20 * 1024 * 1024
 GROUP = 4
+Y_COST = 20_000_000_000
+Z_COST = 20_000_000_000
 
 
 def split(values):
@@ -399,7 +401,7 @@
     )(table, velocity, near, halo, outer, ends, received, partial, gradient)
 
 
-def y_kernel(n, inv_ref, m_ref, v_ref, part_ref, after_ref, gradient_ref, c_ref, high_ref, low_ref, out_ref, sem):
+def y_kernel(n, inv_ref, m_ref, v_ref, part_ref, after_ref, g_ref, c_ref, high_ref, low_ref):
     ny = inv_ref.shape[0]
     nz = v_ref.shape[3]
     row = lax.broadcasted_iota(jnp.int32, (ny, ny), 0)
@@ -408,10 +410,6 @@
     high, low = split(times_stencil(inv_ref[...]) * metric)
     high_ref[...] = high
     low_ref[...] = low
-
-    def copy(group):
-        planes = pl.ds(group * GROUP, GROUP)
-        return pltpu.make_async_copy(out_ref.at[:, planes], gradient_ref.at[:, 1, planes], sem.at[group])
 
     def step(group, carry):
         for u in range(GROUP):
@@ -424,19 +422,12 @@
                     f = a + j
                     value = result[:, j * nz : (j + 1) * nz]
                     if f < 3:
-                        out_ref[f, p] = value
+                        g_ref[f, p] = value
                     else:
                         c_ref[f - 3, p] = value + part_ref[f - 3, p]
-        copy(group).start()
         return carry
 
     lax.fori_loop(0, n // GROUP, step, 0)
-
-    def drain(group, carry):
-        copy(group).wait()
-        return carry
-
-    lax.fori_loop(0, n // GROUP, drain, 0)
 
 
 def y_solve(y_inverse, metric, velocity, partial, after):
@@ -444,17 +435,12 @@
     return pl.pallas_call(
         functools.partial(y_kernel, n),
         in_specs=[WHOLE] * 4 + [ANY],
-        out_specs=[ANY, WHOLE],
-        out_shape=[layer_shape(3, 3, n, ny, nz), in_vmem(3, n, ny, nz)],
-        scratch_shapes=[
-            pltpu.VMEM((ny, ny), BF16),
-            pltpu.VMEM((ny, ny), BF16),
-            pltpu.VMEM((3, n, ny, nz), F32),
-            pltpu.SemaphoreType.DMA((n // GROUP,)),
-        ],
+        out_specs=[WHOLE, WHOLE],
+        out_shape=[in_vmem(3, n, ny, nz), in_vmem(3, n, ny, nz)],
+        scratch_shapes=[pltpu.VMEM((ny, ny), BF16), pltpu.VMEM((ny, ny), BF16)],
         input_output_aliases={3: 1},
         compiler_params=params(),
-        cost_estimate=cost(velocity, 4),
+        cost_estimate=cost(velocity, Y_COST),
         name="y_solve",
     )(y_inverse, metric, velocity, partial, after)
 
@@ -463,7 +449,7 @@
 
 
 def z_own_kernel(
-    n, inv_ref, m_ref, v_ref, after_ref, g_ref, c_ref, right_ref, left_ref, right_2_ref, left_2_ref, main_ref
+    n, inv_ref, m_ref, v_ref, after_ref, g_ref, c_ref, right_ref, left_ref, far_ref, main_ref
 ):
     nz = inv_ref.shape[0]
     ny = v_ref.shape[2]
@@ -517,8 +503,7 @@
             to_left = block(1, first_scale, 2, corners_left)
             right_ref[index] = to_right
             left_ref[index] = to_left
-            right_2_ref[index] = to_right[8:16]
-            left_2_ref[index] = to_left[8:16]
+            far_ref[index] = jnp.concatenate([to_right[8:16], to_left[8:16]], axis=0)
         return carry
 
     lax.fori_loop(0, n // GROUP, step, 0)
@@ -529,10 +514,8 @@
     return pl.pallas_call(
         functools.partial(z_own_kernel, n),
         in_specs=[WHOLE, WHOLE, WHOLE, ANY],
-        out_specs=[WHOLE] * 6,
-        out_shape=[in_vmem(3, n, ny, nz)] * 2
-        + [layer_shape(n * ny // LINES, 16, LINES)] * 2
-        + [layer_shape(n * ny // LINES, 8, LINES)] * 2,
+        out_specs=[WHOLE] * 5,
+        out_shape=[in_vmem(3, n, ny, nz)] * 2 + [layer_shape(n * ny // LINES, 16, LINES)] * 3,
         scratch_shapes=[pltpu.VMEM((2 * nz, 2 * nz), BF16)],
         compiler_params=params(),
         cost_estimate=cost(velocity, 3),
@@ -582,8 +565,8 @@
     at_left, at_right = from_left(left[8:16]), from_right(right[8:16])
     own_first = first_value(own_left, at_left, at_right)
     own_last = last_value(own_right, at_left, at_right)
-    left_value = last_value(left, from_left(left_2), from_right(own_left[8:16]))
-    right_value = first_value(right, from_left(own_right[8:16]), from_right(right_2))
+    left_value = last_value(left, from_left(left_2[0:8]), from_right(own_left[8:16]))
+    right_value = first_value(right, from_left(own_right[8:16]), from_right(right_2[8:16]))
     left_tail, right_head = row(left, 6), row(right, 6)
     left_final = (left_value - COUPLING * left_tail * own_first) / (
         1.0 - COUPLING * COUPLING * left_tail * row(own_left, 6)
@@ -597,8 +580,8 @@
 
 
 def z_join_kernel(
-    n, inv_ref, m_ref, g_ref, part_ref, own_right_ref, own_left_ref, left_ref, right_ref, left_2_ref, right_2_ref, held_ref,
-    gradient_ref, c_ref, side_ref, out_ref, sem,
+    n, inv_ref, m_ref, g_ref, part_ref, own_right_ref, own_left_ref, left_ref, right_ref, left_2_ref, right_2_ref, y_ref,
+    after_ref, gradient_ref, c_ref, side_ref, out_ref, sem,
 ):
     nz = inv_ref.shape[0]
     ny = g_ref.shape[2]
@@ -614,6 +597,8 @@
     high, low = split(wide)
     side_ref[...] = jnp.concatenate([high, high, low], axis=0)
     blocks = GROUP * ny // LINES
+    y_copy = pltpu.make_async_copy(y_ref, gradient_ref.at[:, 1], sem.at[n // GROUP])
+    y_copy.start()
 
     def copy(group):
         planes = pl.ds(group * GROUP, GROUP)
@@ -648,25 +633,26 @@
         return carry
 
     lax.fori_loop(0, n // GROUP, drain, 0)
-
-
-def z_join(z_inverse, metric, own, partial, lines, gradient):
+    y_copy.wait()
+
+
+def z_join(z_inverse, metric, own, partial, lines, y_gradient, after):
     _, n, ny, nz = own.shape
     return pl.pallas_call(
         functools.partial(z_join_kernel, n),
-        in_specs=[WHOLE] * 10 + [ANY],
+        in_specs=[WHOLE] * 11 + [ANY],
         out_specs=[ANY, WHOLE],
-        out_shape=[layer_shape(*gradient.shape), in_vmem(3, n, ny, nz)],
+        out_shape=[layer_shape(3, 3, n, ny, nz), in_vmem(3, n, ny, nz)],
         scratch_shapes=[
             pltpu.VMEM((96, 6 * nz), BF16),
             pltpu.VMEM((3, n, ny, nz), F32),
-            pltpu.SemaphoreType.DMA((n // GROUP,)),
+            pltpu.SemaphoreType.DMA((n // GROUP + 1,)),
         ],
-        input_output_aliases={10: 0, 3: 1},
+        input_output_aliases={3: 1},
         compiler_params=params(),
-        cost_estimate=cost(own, 3),
+        cost_estimate=cost(own, Z_COST),
         name="z_join",
-    )(z_inverse, metric, own, partial, *lines, gradient)
+    )(z_inverse, metric, own, partial, *lines, y_gradient, after)
 
 
 def on_device(mesh, velocity, metric_x, metric_y, metric_z, x_inverse, y_inverse, z_inverse):
@@ -690,21 +676,23 @@
     x_sent, x_partial = x_ends(table, held, halo)
     x_received = lax.ppermute(x_sent, ("gx", "gy"), across)
 
-    z_gradient, convection, to_right, to_left, to_right_2, to_left_2 = z_own(z_inverse, metric_z, held, x_sent)
+    z_gradient, convection, to_right, to_left, to_far = z_own(z_inverse, metric_z, held, x_sent)
+    left_far = lax.ppermute(to_far, "gz", shift(2))
+    right_far = left_far if shift(2) == shift(-2) else lax.ppermute(to_far, "gz", shift(-2))
     z_lines = (
         to_right,
         to_left,
         lax.ppermute(to_right, "gz", shift(1)),
         lax.ppermute(to_left, "gz", shift(-1)),
-        lax.ppermute(to_right_2, "gz", shift(2)),
-        lax.ppermute(to_left_2, "gz", shift(-2)),
+        left_far,
+        right_far,
     )
 
-    gradient, convection = y_solve(y_inverse, metric_y, held, convection, to_right)
-    gradient, convection = z_join(z_inverse, metric_z, z_gradient, convection, z_lines, gradient)
-
+    y_gradient, convection = y_solve(y_inverse, metric_y, held, convection, near)
     outer, x_end = x_face(table, x_received, x_sent, x_partial, own, near, convection, n)
     x_other = lax.ppermute(x_end, "gy", beside)
+
+    gradient, convection = z_join(z_inverse, metric_z, z_gradient, convection, z_lines, y_gradient, x_end)
     return tuple(x_solve(table, held, near, halo, outer, x_end, x_other, convection, gradient))
 
 

time: 45.6 us -> 39.2 us (0.86)
  waiting for transfers between devices: 7.55 us -> 1.05 us
  starting transfers between devices: 10.1 us -> 11.5 us
  Pallas kernels: 26.7 us -> 25.7 us
    ppermute x1, starting transfers between devices: 0.08 us -> 4.71 us  [on_device(): near = lax.ppermute(own, ('gx', 'gy'), across)]
    ppermute x2 -> x1, waiting for transfers between devices: 3.9 us -> 0.01 us  [on_device(): left_far = lax.ppermute(to_far, 'gz', shift(2))]
    ppermute x1, starting transfers between devices: 4.78 us -> 1.7 us  [on_device(): x_received = lax.ppermute(x_sent, ('gx', 'gy'), across)]
    ppermute x1, waiting for transfers between devices: 1.99 us -> 0.01 us  [on_device(): x_other = lax.ppermute(x_end, 'gy', beside)]
    ppermute x1, waiting for transfers between devices: 1.64 us -> 0.01 us  [on_device(): halo = lax.ppermute(inner, 'gy', beside)]
    pallas_call x1, Pallas kernels: 6.23 us -> 5.19 us  [y_solve(): pl.pallas_call(functools.partial(y_kernel, n), in_specs=[WHOLE] * 4 + [AN...]
    ppermute x1, waiting for transfers between devices: 0.01 us -> 1.04 us  [on_device(): x_received = lax.ppermute(x_sent, ('gx', 'gy'), across)]
    ppermute x2 -> x1, starting transfers between devices: 1.7 us -> 1.58 us  [on_device(): left_far = lax.ppermute(to_far, 'gz', shift(2))]
  transfers between devices with their start and end apart: 8 -> 7, of which waited for: 3 -> 1; matrix products, arithmetic and copies ran while one was open for 0% -> 0% of each run, Pallas kernels for 35% -> 45%
where the time goes in v1:
time: 39.2 us; the launch traced here: 39 us
  Pallas kernels  25.7 us (66%)
  starting transfers between devices  11.5 us (29%)
  waiting for transfers between devices  1.05 us (3%)
  between operations  0.73 us (2%)
    pallas_call x1, Pallas kernels, x_solve(): pl.pallas_call(functools.partial(x_solve_kernel, n, ny), in_specs=[WHOLE]...  6.39 us
    pallas_call x1, Pallas kernels, y_solve(): pl.pallas_call(functools.partial(y_kernel, n), in_specs=[WHOLE] * 4 + [AN...  5.19 us
    pallas_call x1, Pallas kernels, z_own(): pl.pallas_call(functools.partial(z_own_kernel, n), in_specs=[WHOLE, WHOLE...  5.1 us
    ppermute x1, starting transfers between devices, on_device(): near = lax.ppermute(own, ('gx', 'gy'), across)  4.71 us
    pallas_call x1, Pallas kernels, z_join(): pl.pallas_call(functools.partial(z_join_kernel, n), in_specs=[WHOLE] * 11...  4.64 us
    pallas_call x1, Pallas kernels, x_ends(): pl.pallas_call(functools.partial(x_ends_kernel, n, ny), in_specs=[WHOLE]...  2.18 us
    ppermute x1, starting transfers between devices, on_device(): x_received = lax.ppermute(x_sent, ('gx', 'gy'), across)  1.7 us
    pallas_call x1, Pallas kernels, prepare(): pl.pallas_call(functools.partial(prepare_kernel, n, ny), in_specs=[ANY] *...  1.64 us
  transfers between devices with their start and end apart: 7, of which 1 were waited for; matrix products, arithmetic and copies ran while one was open for 0% of the time, Pallas kernels for 45%

profile of v1, /device:TPU:0, one launch (start us, length us, event | category | flops | bytes accessed | tf_op | source)
XLA Modules:
  0.0 39.0 jit_solution(2110296257897651718)
XLA Ops:
  0.6 0.0 copy-start
  0.6 1.6 %prepare.1 = (f32[592,128]{1,0:T(8,128)S(1)}, f32[1168,128]{1,0:T(8,128)S(1)}, f32[89,8,128]{2,1,0:T(8,128)S(1)}, f32[192,192]{1,0:T(8,128)S(1)}, f32[1,192]{1,0...) custom-call(f32[16,16]{1,0:T(8,128)} %xi_ref.1, f32[1,16]{1,0:T(1,128)} %bitcast.4, f32[192,192]{1,0:T(8,128)} %yi_ref.1, ...), custom_call_target="tpu_custom_call" | custom-call | tf_op jit(solution)/shard_map/prepare/pallas_call | solution.py:187
  2.3 0.5 %collective-permute-start.1 = (f32[1168,128]{1,0:T(8,128)S(1)}, f32[1168,128]{1,0:T(8,128)S(1)}, u32[]{:S(2)}, u32[]{:S(2)}) collective-permute-start(f32[1168,128]{1,0:T(8,128)S(1)} %get-tuple-element.24), channel_id=1, source_target_pairs={{0,1},{1,0},{2,3},{3,2},{4,5},{5,4},{6,7},{7,6},{8,9},{9,8},{10,11... | collective-permute-start | bytes 1794056 | tf_op jit(solution)/shard_map/ppermute | solution.py:673
  2.8 4.7 %collective-permute-start = (f32[592,128]{1,0:T(8,128)S(1)}, f32[592,128]{1,0:T(8,128)S(1)}, u32[]{:S(2)}, u32[]{:S(2)}) collective-permute-start(f32[592,128]{1,0:T(8,128)S(1)} %get-tuple-element.23.own_ref), channel_id=1, source_target_pairs={{1,8},{9,16},{17,24},{25,0},{8,1},{16,9},{24,17},{0,25},{3,10},{11... | collective-permute-start | bytes 909320 | tf_op jit(solution)/shard_map/ppermute | solution.py:672
  7.5 0.0 collective-permute-done.1.halo_ref
  7.5 0.0 copy-done
  7.5 2.2 %x_ends.1 = (f32[6,192,128]{2,1,0:T(8,128)S(1)}, f32[6,192,128]{2,1,0:T(8,128)S(1)}) custom-call(f32[89,8,128]{2,1,0:T(8,128)S(1)} %get-tuple-element.22.table_ref, f32[3,16,192,128]{3,2,1,0:T(8,128)S(1)} %copy-done, f32[1168,128]{1,0:T(8,128)S(1)} %collective-permute-done.1.halo_ref), custom_call_target="tpu_custom_call" | custom-call | flops 3 | bytes 3 | tf_op jit(solution)/shard_map/x_ends/pallas_call | solution.py:233
  9.7 1.7 %collective-permute-start.2 = (f32[6,192,128]{2,1,0:T(8,128)S(1)}, f32[6,192,128]{2,1,0:T(8,128)S(1)}, u32[]{:S(2)}, u32[]{:S(2)}) collective-permute-start(f32[6,192,128]{2,1,0:T(8,128)S(1)} %get-tuple-element.25.after_ref.ws_ref), channel_id=1, source_target_pairs={{1,8},{9,16},{17,24},{25,0},{8,1},{16,9},{24,17},{0,25},{3,10},{11... | collective-permute-start | bytes 1769480 | tf_op jit(solution)/shard_map/ppermute | solution.py:677
  11.4 5.1 %z_own.1 = (f32[3,16,192,128]{3,2,1,0:T(8,128)S(1)}, f32[3,16,192,128]{3,2,1,0:T(8,128)S(1)}, f32[24,16,128]{2,1,0:T(8,128)S(1)}, f32[24,16,128]{2,1,0:T(8,128)S(1)}, f32[24,16,128]{2,1,0:T(8,128)S(1)}) custom-call(f32[128,128]{1,0:T(8,128)S(1)} %get-tuple-element.29.inv_ref, f32[1,128]{1,0:T(1,128)S(1)} %get-tuple-element.30.m_ref, ...), custom_call_target="tpu_custom_call" | custom-call | flops 3 | bytes 3 | tf_op jit(solution)/shard_map/z_own/pallas_call | solution.py:514
  16.5 1.6 %collective-permute-start.6 = (f32[24,16,128]{2,1,0:T(8,128)S(1)}, f32[24,16,128]{2,1,0:T(8,128)S(1)}, u32[]{:S(2)}, u32[]{:S(2)}) collective-permute-start(f32[24,16,128]{2,1,0:T(8,128)S(1)} %get-tuple-element.38), channel_id=1, source_target_pairs={{0,4},{2,6},{4,0},{6,2},{1,5},{3,7},{5,1},{7,3},{8,12},{10,14},{12... | collective-permute-start | bytes 589832 | tf_op jit(solution)/shard_map/ppermute | solution.py:680
  18.1 1.5 %collective-permute-start.4 = (f32[24,16,128]{2,1,0:T(8,128)S(1)}, f32[24,16,128]{2,1,0:T(8,128)S(1)}, u32[]{:S(2)}, u32[]{:S(2)}) collective-permute-start(f32[24,16,128]{2,1,0:T(8,128)S(1)} %get-tuple-element.36.own_right_ref), channel_id=1, source_target_pairs={{0,2},{2,4},{4,6},{6,0},{1,3},{3,5},{5,7},{7,1},{8,10},{10,12},{12... | collective-permute-start | bytes 589832 | tf_op jit(solution)/shard_map/ppermute | solution.py:685
  19.6 1.4 %collective-permute-start.5 = (f32[24,16,128]{2,1,0:T(8,128)S(1)}, f32[24,16,128]{2,1,0:T(8,128)S(1)}, u32[]{:S(2)}, u32[]{:S(2)}) collective-permute-start(f32[24,16,128]{2,1,0:T(8,128)S(1)} %get-tuple-element.37.own_left_ref), channel_id=1, source_target_pairs={{0,6},{2,0},{4,2},{6,4},{1,7},{3,1},{5,3},{7,5},{8,14},{10,8},{12,... | collective-permute-start | bytes 589832 | tf_op jit(solution)/shard_map/ppermute | solution.py:686
  21.0 0.0 collective-permute-done.after_ref.near_ref
  21.0 5.2 %y_solve.1 = (f32[3,16,192,128]{3,2,1,0:T(8,128)S(1)}, f32[3,16,192,128]{3,2,1,0:T(8,128)S(1)}) custom-call(f32[192,192]{1,0:T(8,128)S(1)} %get-tuple-element.27.inv_ref, f32[1,192]{1,0:T(1,128)S(1)} %get-tuple-element.28.m_ref, f32[3,16,192,128]{3,2,1,0:T(8,128)S(1)} %copy-done, ...), custom_call_target="tpu_custom_call", output_to_operand_aliasing={{1}: (3, {})} | custom-call | flops 20000000000 | bytes 20000000000 | tf_op jit(solution)/shard_map/y_solve/pallas_call | solution.py:435
  26.2 1.0 %collective-permute-done.2.wr_ref = f32[6,192,128]{2,1,0:T(8,128)S(1)} collective-permute-done((f32[6,192,128]{2,1,0:T(8,128)S(1)}, f32[6,192,128]{2,1,0:T(8,128)S(1)}, u32[]{:S(2)}, u32[]{:S(2)}) %collective-permute-start.2) | collective-permute-done | bytes 589856 | tf_op jit(solution)/shard_map/ppermute | solution.py:677
  27.3 0.6 %x_face.1 = (f32[6,192,128]{2,1,0:T(8,128)S(1)}, f32[6,192,128]{2,1,0:T(8,128)S(1)}) custom-call(f32[89,8,128]{2,1,0:T(8,128)S(1)} %get-tuple-element.22.table_ref, f32[6,192,128]{2,1,0:T(8,128)S(1)} %collective-permute-done.2.wr_ref, f32[6,192,128]{2,1,0:T(8,128)S(1)} %get-tuple-element.25.after_ref.ws_ref, f32[6,192,128]{2,1,0:T(8,128)S(1)} %get-tuple-element.26.l_ref, ...), custom_call_target="tpu_custom_call" | custom-call | flops 1 | bytes 1 | tf_op jit(solution)/shard_map/x_face/pallas_call | solution.py:280
  27.8 0.1 collective-permute-start.3
  27.9 0.0 collective-permute-done.6.left_2_ref.right_2_ref
  27.9 0.0 collective-permute-done.4.left_ref
  27.9 0.0 collective-permute-done.5.right_ref
  27.9 4.6 %z_join.1 = (f32[3,3,16,192,128]{4,3,2,1,0:T(8,128)}, f32[3,16,192,128]{3,2,1,0:T(8,128)S(1)}) custom-call(f32[128,128]{1,0:T(8,128)S(1)} %get-tuple-element.29.inv_ref, f32[1,128]{1,0:T(1,128)S(1)} %get-tuple-element.30.m_ref, f32[3,16,192,128]{3,2,1,0:T(8,128)S(1)} %get-tuple-element.35.g_ref, ...), custom_call_target="tpu_custom_call", output_to_operand_aliasing={{1}: (3, {})} | custom-call | flops 20000000000 | bytes 20000000000 | tf_op jit(solution)/shard_map/z_join/pallas_call | solution.py:641
  32.6 0.0 collective-permute-done.3.r_ref
  32.6 6.4 %x_solve.1 = (f32[3,3,16,192,128]{4,3,2,1,0:T(8,128)}, f32[3,16,192,128]{3,2,1,0:T(8,128)}) custom-call(f32[89,8,128]{2,1,0:T(8,128)S(1)} %get-tuple-element.22.table_ref, f32[3,16,192,128]{3,2,1,0:T(8,128)S(1)} %copy-done, f32[592,128]{1,0:T(8,128)S(1)} %collective-permute-done.after_ref.near_ref, ...), custom_call_target="tpu_custom_call", output_to_operand_aliasing={{0}: (8, {})} | custom-call | flops 5 | bytes 5 | tf_op jit(solution)/shard_map/x_solve/pallas_call | solution.py:387
Async XLA Ops:
  0.6 6.9 %copy-start = (f32[3,16,192,128]{3,2,1,0:T(8,128)S(1)}, f32[3,16,192,128]{3,2,1,0:T(8,128)}, u32[]{:S(2)}) copy-start(f32[3,16,192,128]{3,2,1,0:T(8,128)} %v_ref.9) | copy-start | bytes 14155780
  2.3 5.2 %collective-permute-start.1 = (f32[1168,128]{1,0:T(8,128)S(1)}, f32[1168,128]{1,0:T(8,128)S(1)}, u32[]{:S(2)}, u32[]{:S(2)}) collective-permute-start(f32[1168,128]{1,0:T(8,128)S(1)} %get-tuple-element.24), channel_id=1, source_target_pairs={{0,1},{1,0},{2,3},{3,2},{4,5},{5,4},{6,7},{7,6},{8,9},{9,8},{10,11... | collective-permute-start | bytes 1794056 | tf_op jit(solution)/shard_map/ppermute | solution.py:673
  2.8 18.2 %collective-permute-start = (f32[592,128]{1,0:T(8,128)S(1)}, f32[592,128]{1,0:T(8,128)S(1)}, u32[]{:S(2)}, u32[]{:S(2)}) collective-permute-start(f32[592,128]{1,0:T(8,128)S(1)} %get-tuple-element.23.own_ref), channel_id=1, source_target_pairs={{1,8},{9,16},{17,24},{25,0},{8,1},{16,9},{24,17},{0,25},{3,10},{11... | collective-permute-start | bytes 909320 | tf_op jit(solution)/shard_map/ppermute | solution.py:672
  9.7 17.6 %collective-permute-start.2 = (f32[6,192,128]{2,1,0:T(8,128)S(1)}, f32[6,192,128]{2,1,0:T(8,128)S(1)}, u32[]{:S(2)}, u32[]{:S(2)}) collective-permute-start(f32[6,192,128]{2,1,0:T(8,128)S(1)} %get-tuple-element.25.after_ref.ws_ref), channel_id=1, source_target_pairs={{1,8},{9,16},{17,24},{25,0},{8,1},{16,9},{24,17},{0,25},{3,10},{11... | collective-permute-start | bytes 1769480 | tf_op jit(solution)/shard_map/ppermute | solution.py:677
  16.5 11.4 %collective-permute-start.6 = (f32[24,16,128]{2,1,0:T(8,128)S(1)}, f32[24,16,128]{2,1,0:T(8,128)S(1)}, u32[]{:S(2)}, u32[]{:S(2)}) collective-permute-start(f32[24,16,128]{2,1,0:T(8,128)S(1)} %get-tuple-element.38), channel_id=1, source_target_pairs={{0,4},{2,6},{4,0},{6,2},{1,5},{3,7},{5,1},{7,3},{8,12},{10,14},{12... | collective-permute-start | bytes 589832 | tf_op jit(solution)/shard_map/ppermute | solution.py:680
  18.1 9.8 %collective-permute-start.4 = (f32[24,16,128]{2,1,0:T(8,128)S(1)}, f32[24,16,128]{2,1,0:T(8,128)S(1)}, u32[]{:S(2)}, u32[]{:S(2)}) collective-permute-start(f32[24,16,128]{2,1,0:T(8,128)S(1)} %get-tuple-element.36.own_right_ref), channel_id=1, source_target_pairs={{0,2},{2,4},{4,6},{6,0},{1,3},{3,5},{5,7},{7,1},{8,10},{10,12},{12... | collective-permute-start | bytes 589832 | tf_op jit(solution)/shard_map/ppermute | solution.py:685
  19.6 8.4 %collective-permute-start.5 = (f32[24,16,128]{2,1,0:T(8,128)S(1)}, f32[24,16,128]{2,1,0:T(8,128)S(1)}, u32[]{:S(2)}, u32[]{:S(2)}) collective-permute-start(f32[24,16,128]{2,1,0:T(8,128)S(1)} %get-tuple-element.37.own_left_ref), channel_id=1, source_target_pairs={{0,6},{2,0},{4,2},{6,4},{1,7},{3,1},{5,3},{7,5},{8,14},{10,8},{12,... | collective-permute-start | bytes 589832 | tf_op jit(solution)/shard_map/ppermute | solution.py:686
  27.8 4.8 %collective-permute-start.3 = (f32[6,192,128]{2,1,0:T(8,128)S(1)}, f32[6,192,128]{2,1,0:T(8,128)S(1)}, u32[]{:S(2)}, u32[]{:S(2)}) collective-permute-start(f32[6,192,128]{2,1,0:T(8,128)S(1)} %get-tuple-element.34.after_ref.e_ref), channel_id=1, source_target_pairs={{0,1},{1,0},{2,3},{3,2},{4,5},{5,4},{6,7},{7,6},{8,9},{9,8},{10,11... | collective-permute-start | bytes 1769480 | tf_op jit(solution)/shard_map/ppermute | solution.py:693

commit v2 on v1

v2 whole, which is shorter than its diff:
```python
import functools

import jax
import jax.numpy as jnp
from jax import lax
from jax.experimental import pallas as pl
from jax.experimental.pallas import tpu as pltpu
from jax.sharding import PartitionSpec as P

COUPLING = 1.0 / 3.0
NEAR = 7.0 / 9.0
FAR = 1.0 / 36.0
F32 = jnp.float32
BF16 = jnp.bfloat16
SMEM = pltpu.SMEM
VMEM_LIMIT = 20 * 1024 * 1024
GROUP = 8
Y_COST = 20_000_000_000
Z_COST = 20_000_000_000


def split(values):
    high = values.astype(BF16)
    low = (values - high.astype(F32)).astype(BF16)
    return high, low


def dot(a, b):
    return lax.dot_general(a, b, (((1,), (0,)), ((), ())), preferred_element_type=F32)


def dot_nt(a, b):
    return lax.dot_general(a, b, (((1,), (1,)), ((), ())), preferred_element_type=F32)


def params():
    return pltpu.CompilerParams(vmem_limit_bytes=VMEM_LIMIT)


def six(velocity, direction):
    return list(velocity) + [velocity[i] * velocity[direction] for i in range(3)]


def times_stencil(inverse):
    rows, length = inverse.shape
    zeros = jnp.zeros((rows, 2), F32)
    wide = jnp.concatenate([zeros, inverse, zeros], axis=1)

    def column(offset):
        return wide[:, 2 + offset : 2 + offset + length]

    return NEAR * (column(-1) - column(1)) + FAR * (column(-2) - column(2))


def in_vmem(*shape):
    return pltpu.VMEM(shape, F32)


ANY = pl.BlockSpec(memory_space=pl.ANY)
WHOLE = pl.BlockSpec(memory_space=pltpu.VMEM)
SCALARS = pl.BlockSpec(memory_space=SMEM)


def cost(array, passes):
    return pl.CostEstimate(flops=passes, bytes_accessed=passes, transcendentals=0)


def layer_shape(*shape):
    return jax.ShapeDtypeStruct(shape, F32)


class Ends:
    def __init__(self, n):
        self.first = lax.axis_index("gy") == 0
        self.n = n
        self.o = jnp.where(self.first, 0, n - 1)
        self.o1 = jnp.where(self.first, 1, n - 2)
        self.q = jnp.where(self.first, n - 1, 0)
        self.q1 = jnp.where(self.first, n - 2, 1)
        self.sign_o = jnp.where(self.first, -1.0, 1.0).astype(F32)
        self.sign_q = -self.sign_o


class Table:
    def __init__(self, n):
        self.source, self.forward, self.backward = 0, n, 2 * n
        self.send, self.last = 3 * n, 4 * n + 2
        self.oo, self.oo1, self.qo, self.qo1, self.qq = range(5 * n + 4, 5 * n + 9)
        self.size = 5 * n + 9


def prepare_kernel(n, v_ref, own_ref, halo_ref, sem):
    ends = Ends(n)
    copies = []
    for i in range(3):
        copies.append(pltpu.make_async_copy(v_ref.at[i, ends.o], own_ref.at[i], sem.at[3 * i]))
        for j in range(2):
            plane = jnp.where(ends.first, n - 2 + j, j)
            copies.append(pltpu.make_async_copy(v_ref.at[i, plane], halo_ref.at[i, j], sem.at[3 * i + 1 + j]))
    for copy in copies:
        copy.start()
    for copy in copies:
        copy.wait()


def prepare(velocity):
    _, n, ny, nz = velocity.shape
    return pl.pallas_call(
        functools.partial(prepare_kernel, n),
        in_specs=[ANY],
        out_specs=[WHOLE] * 2,
        out_shape=[layer_shape(3, ny, nz), layer_shape(3, 2, ny, nz)],
        scratch_shapes=[pltpu.SemaphoreType.DMA((9,))],
        compiler_params=params(),
        name="prepare",
    )(pltpu.with_memory_space_constraint(velocity, pltpu.HBM))


def tables_kernel(
    n, xi_ref, mx_ref, yi_ref, my_ref, zi_ref, mz_ref, after_ref,
    table_ref, y_ref, y_metric_ref, z_ref, z_metric_ref, x_ref, m_ref, sem,
):
    ends = Ends(n)
    nz = table_ref.shape[2]
    small = [pltpu.make_async_copy(xi_ref, x_ref, sem.at[0]), pltpu.make_async_copy(mx_ref, m_ref, sem.at[1])]
    copies = [
        pltpu.make_async_copy(zi_ref, z_ref, sem.at[2]),
        pltpu.make_async_copy(mz_ref, z_metric_ref, sem.at[3]),
        pltpu.make_async_copy(yi_ref, y_ref, sem.at[4]),
        pltpu.make_async_copy(my_ref, y_metric_ref, sem.at[5]),
    ]
    for copy in small + copies:
        copy.start()
    for copy in small:
        copy.wait()

    table = Table(n)
    first = ends.first

    def spread(value):
        return jnp.broadcast_to(value, (8, nz))

    def entry(i, j):
        return spread(x_ref[i : i + 1, j : j + 1])

    metric = [spread(m_ref[0:1, k : k + 1]) for k in range(n)]
    above = [entry(i, i + 1) for i in range(n - 1)]
    diagonal = [entry(i, i) for i in range(n)]
    ratio = [-above[i] / diagonal[i + 1] for i in range(n - 1)]
    ratio.append(-entry(n - 1, n - 2) / diagonal[n - 2] * diagonal[n - 1])
    for k in range(n):
        if k == 0:
            source = metric[k]
        elif k == n - 1:
            source = diagonal[k] * metric[k]
        else:
            source = (1.0 + ratio[k] * ratio[k - 1]) * metric[k]
        table_ref[table.source + k] = FAR * source
        table_ref[table.forward + k] = ratio[k] * metric[k] / metric[k - 1] if k > 0 else metric[k]
        table_ref[table.backward + k] = ratio[k] * metric[k] / metric[k + 1] if k < n - 1 else metric[k]

    top = [entry(0, k) for k in range(n)]
    bottom = [entry(n - 1, k) for k in range(n)]
    outer = [jnp.where(first, top[k], bottom[k]) for k in range(n)]
    inner = [jnp.where(first, bottom[k], top[k]) for k in range(n)]
    sign_o, sign_q = ends.sign_o, ends.sign_q
    for base, row, factor in ((table.send, outer, -COUPLING), (table.last, inner, 1.0)):

        def at(k):
            return row[k] if 0 <= k < n else jnp.zeros_like(row[0])

        for k in range(n):
            value = factor * (NEAR * (at(k - 1) - at(k + 1)) + FAR * (at(k - 2) - at(k + 2)))
            if base == table.send:
                if k == 0:
                    value = value + jnp.where(first, NEAR, 0.0)
                elif k == 1:
                    value = value + jnp.where(first, FAR, 0.0)
                elif k == n - 2:
                    value = value - jnp.where(first, 0.0, FAR)
                elif k == n - 1:
                    value = value - jnp.where(first, 0.0, NEAR)
            table_ref[base + k] = value
        at_q = jnp.where(first, row[n - 1], row[0])
        at_q1 = jnp.where(first, row[n - 2], row[1])
        near = factor * sign_q * (NEAR * at_q + FAR * at_q1)
        far = factor * sign_q * FAR * at_q
        table_ref[base + n] = jnp.where(first, near, far)
        table_ref[base + n + 1] = jnp.where(first, far, near)
    table_ref[table.oo] = jnp.where(first, outer[0], outer[n - 1])
    table_ref[table.oo1] = jnp.where(first, outer[1], outer[n - 2])
    table_ref[table.qo] = jnp.where(first, inner[0], inner[n - 1])
    table_ref[table.qo1] = jnp.where(first, inner[1], inner[n - 2])
    table_ref[table.qq] = jnp.where(first, inner[n - 1], inner[0])
    for copy in copies:
        copy.wait()


def tables(x_inverse, metric_x, y_inverse, metric_y, z_inverse, metric_z, after):
    n, ny, nz = x_inverse.shape[0], y_inverse.shape[0], z_inverse.shape[0]
    inputs = (x_inverse, metric_x, y_inverse, metric_y, z_inverse, metric_z)
    return pl.pallas_call(
        functools.partial(tables_kernel, n),
        in_specs=[ANY] * 7,
        out_specs=[WHOLE] * 5,
        out_shape=[
            in_vmem(Table(n).size, 8, nz),
            in_vmem(ny, ny),
            in_vmem(1, ny),
            in_vmem(nz, nz),
            in_vmem(1, nz),
        ],
        scratch_shapes=[pltpu.VMEM((n, n), F32), pltpu.VMEM((1, n), F32), pltpu.SemaphoreType.DMA((6,))],
        compiler_params=params(),
        name="tables",
    )(*(pltpu.with_memory_space_constraint(value, pltpu.HBM) for value in inputs), after)


def x_ends_kernel(n, ny, table_ref, v_ref, halo_ref, w_ref, l_ref):
    table = Table(n)

    def tile(index, carry):
        start = pl.multiple_of(index * 8, 8)
        rows = pl.ds(start, 8)
        w = [None] * 6
        l = [None] * 6
        for k in range(n + 2):
            if k < n:
                fields = six([v_ref[i, k, rows, :] for i in range(3)], 0)
            else:
                fields = six([halo_ref[i, k - n, rows, :] for i in range(3)], 0)
            a, b = table_ref[table.send + k], table_ref[table.last + k]
            for f in range(6):
                w[f] = a * fields[f] if k == 0 else w[f] + a * fields[f]
                l[f] = b * fields[f] if k == 0 else l[f] + b * fields[f]
        for f in range(6):
            w_ref[pl.ds(f * ny + start, 8), :] = w[f]
            l_ref[f, rows, :] = l[f]
        return carry

    lax.fori_loop(0, ny // 8, tile, 0)
    index = lax.broadcasted_iota(jnp.int32, (8, w_ref.shape[1]), 0)
    w_ref[6 * ny : 6 * ny + 8, :] = jnp.where(index == 0, table_ref[table.oo], table_ref[table.oo1])


def x_ends(table, velocity, halo):
    _, n, ny, nz = velocity.shape
    return pl.pallas_call(
        functools.partial(x_ends_kernel, n, ny),
        in_specs=[WHOLE] * 3,
        out_specs=[WHOLE, WHOLE],
        out_shape=[layer_shape(6 * ny + 8, nz), layer_shape(6, ny, nz)],
        compiler_params=params(),
        cost_estimate=cost(velocity, 3),
        name="x_ends",
    )(table, velocity, halo)


def x_face_kernel(n, ny, table_ref, wr_ref, ws_ref, l_ref, own_ref, near_ref, after_ref, w_ref, e_ref):
    ends = Ends(n)
    table = Table(n)
    shape = (8, wr_ref.shape[1])
    p_oo = jnp.broadcast_to(wr_ref[6 * ny : 6 * ny + 1, :], shape)
    p_oo1 = jnp.broadcast_to(wr_ref[6 * ny + 1 : 6 * ny + 2, :], shape)
    x_qo = table_ref[table.qo]
    inverse_den = 1.0 / (1.0 - COUPLING * COUPLING * table_ref[table.oo] * p_oo)
    sent_weight = COUPLING * p_oo
    own_weight = COUPLING * FAR * ends.sign_o * p_oo1
    near_weight = COUPLING * FAR * ends.sign_o * COUPLING * table_ref[table.oo1] * p_oo
    end_weight = ends.sign_o * FAR * table_ref[table.qo1]

    def tile(index, carry):
        start = pl.multiple_of(index * 8, 8)
        rows = pl.ds(start, 8)
        own = six([own_ref[i, rows, :] for i in range(3)], 0)
        near = six([near_ref[i, rows, :] for i in range(3)], 0)
        for f in range(6):
            field = pl.ds(f * ny + start, 8)
            w = wr_ref[field, :] - sent_weight * ws_ref[field, :]
            w = (w + own_weight * own[f] + near_weight * near[f]) * inverse_den
            w_ref[f, rows, :] = 36.0 * w
            e_ref[field, :] = l_ref[f, rows, :] + x_qo * w + end_weight * near[f]
        return carry

    lax.fori_loop(0, ny // 8, tile, 0)
    e_ref[6 * ny : 6 * ny + 8, :] = table_ref[table.qq]


def x_face(table, received, sent, partial, own, near, after, n):
    _, ny, nz = own.shape
    return pl.pallas_call(
        functools.partial(x_face_kernel, n, ny),
        in_specs=[WHOLE] * 6 + [ANY],
        out_specs=[WHOLE, WHOLE],
        out_shape=[layer_shape(6, ny, nz), layer_shape(6 * ny + 8, nz)],
        compiler_params=params(),
        cost_estimate=cost(received, 1),
        name="x_face",
    )(table, received, sent, partial, own, near, after)


def x_solve_kernel(
    n, ny, table_ref, v_ref, near_ref, halo_ref, w_ref, e_ref, r_ref, part_ref, z_ref, held_ref,
    gradient_ref, convection_ref, g_ref, c_ref, sem,
):
    table = Table(n)
    parts = sem.shape[1]
    share = ny // parts
    z_copy = pltpu.make_async_copy(z_ref, gradient_ref.at[:, 2], sem.at[2, 0])
    z_copy.start()
    p_qq = r_ref[6 * ny : 6 * ny + 8, :]
    weight = COUPLING * p_qq
    scale = -36.0 * COUPLING / (1.0 - COUPLING * COUPLING * table_ref[table.qq] * p_qq)

    def copies(part):
        rows = pl.ds(pl.multiple_of(part * share, 8), share)
        return (
            pltpu.make_async_copy(g_ref.at[:, :, rows], gradient_ref.at[:, 0, :, rows], sem.at[0, part]),
            pltpu.make_async_copy(c_ref.at[:, :, rows], convection_ref.at[:, :, rows], sem.at[1, part]),
        )

    def run(first):
        sign_o = -1.0 if first else 1.0
        near_j, far_j = (0, 1) if first else (1, 0)

        def tile(index, carry):
            start = pl.multiple_of(index * 8, 8)
            rows = pl.ds(start, 8)
            near = six([near_ref[i, rows, :] for i in range(3)], 0)
            inner_near = six([halo_ref[i, near_j, rows, :] for i in range(3)], 0)
            inner_far = six([halo_ref[i, far_j, rows, :] for i in range(3)], 0)
            for f in range(6):
                if f < 3:
                    line = [v_ref[f, k, rows, :] for k in range(n)]
                else:
                    line = [v_ref[f - 3, k, rows, :] * v_ref[0, k, rows, :] for k in range(n)]
                field = pl.ds(f * ny + start, 8)
                inner = -sign_o * (28.0 * inner_near[f] + inner_far[f])
                inner = inner + scale * (r_ref[field, :] - weight * e_ref[field, :])
                outer = w_ref[f, rows, :]
                forward = []
                for k in range(n):
                    if k == 0:
                        source = 28.0 * line[1] + line[2] + (outer if first else inner)
                    elif k == 1:
                        source = 28.0 * (line[2] - line[0]) + (line[3] - (near[f] if first else inner_near[f]))
                    elif k == n - 1:
                        source = (inner if first else outer) - 28.0 * line[n - 2] - line[n - 3]
                    elif k == n - 2:
                        source = 28.0 * (line[n - 1] - line[n - 3]) + (
                            (inner_near[f] if first else near[f]) - line[n - 4]
                        )
                    else:
                        source = 28.0 * (line[k + 1] - line[k - 1]) + (line[k + 2] - line[k - 2])
                    value = table_ref[table.source + k] * source
                    if k > 0:
                        value = value - table_ref[table.forward + k] * forward[k - 1]
                    forward.append(value)
                solved = None
                for k in reversed(range(n)):
                    solved = forward[k] if k == n - 1 else forward[k] - table_ref[table.backward + k] * solved
                    if f < 3:
                        g_ref[f, k, rows, :] = solved
                    else:
                        c_ref[f - 3, k, rows, :] = solved + part_ref[f - 3, k, rows, :]
            return carry

        def step(part, carry):
            lax.fori_loop(part * (share // 8), (part + 1) * (share // 8), tile, 0)
            for copy in copies(part):
                copy.start()
            return carry

        lax.fori_loop(0, parts, step, 0)

    is_first = lax.axis_index("gy") == 0
    pl.when(is_first)(functools.partial(run, True))
    pl.when(jnp.logical_not(is_first))(functools.partial(run, False))

    def drain(part, carry):
        for copy in copies(part):
            copy.wait()
        return carry

    z_copy.wait()
    lax.fori_loop(0, parts, drain, 0)


def x_solve(table, velocity, near, halo, outer, ends, received, partial, z_gradient, gradient, parts=12):
    _, n, ny, nz = velocity.shape
    return pl.pallas_call(
        functools.partial(x_solve_kernel, n, ny),
        in_specs=[WHOLE] * 9 + [ANY],
        out_specs=[ANY, ANY],
        out_shape=[layer_shape(*gradient.shape), layer_shape(3, n, ny, nz)],
        scratch_shapes=[
            pltpu.VMEM((3, n, ny, nz), F32),
            pltpu.VMEM((3, n, ny, nz), F32),
            pltpu.SemaphoreType.DMA((3, parts)),
        ],
        input_output_aliases={9: 0},
        compiler_params=params(),
        cost_estimate=cost(velocity, 5),
        name="x_solve",
    )(table, velocity, near, halo, outer, ends, received, partial, z_gradient, gradient)


def y_kernel(n, inv_ref, m_ref, v_ref, part_ref, after_ref, g_ref, c_ref, high_ref, low_ref):
    ny = inv_ref.shape[0]
    nz = v_ref.shape[3]
    row = lax.broadcasted_iota(jnp.int32, (ny, ny), 0)
    column = lax.broadcasted_iota(jnp.int32, (ny, ny), 1)
    metric = jnp.sum(jnp.where(row == column, m_ref[...], 0.0), axis=1, keepdims=True)
    high, low = split(times_stencil(inv_ref[...]) * metric)
    high_ref[...] = high
    low_ref[...] = low

    def step(group, carry):
        for u in range(GROUP):
            p = group * GROUP + u
            fields = six([v_ref[i, p] for i in range(3)], 1)
            for a in (0, 2, 4):
                high, low = split(jnp.concatenate(fields[a : a + 2], axis=1))
                result = dot(high_ref[...], high) + dot(low_ref[...], high) + dot(high_ref[...], low)
                for j in range(2):
                    f = a + j
                    value = result[:, j * nz : (j + 1) * nz]
                    if f < 3:
                        g_ref[f, p] = value
                    else:
                        c_ref[f - 3, p] = value + part_ref[f - 3, p]
        return carry

    lax.fori_loop(0, n // GROUP, step, 0)


def y_solve(y_inverse, metric, velocity, partial, after):
    _, n, ny, nz = velocity.shape
    return pl.pallas_call(
        functools.partial(y_kernel, n),
        in_specs=[WHOLE] * 4 + [ANY],
        out_specs=[WHOLE, WHOLE],
        out_shape=[in_vmem(3, n, ny, nz), in_vmem(3, n, ny, nz)],
        scratch_shapes=[pltpu.VMEM((ny, ny), BF16), pltpu.VMEM((ny, ny), BF16)],
        input_output_aliases={3: 1},
        compiler_params=params(),
        cost_estimate=cost(velocity, Y_COST),
        name="y_solve",
    )(y_inverse, metric, velocity, partial, after)


LINES = 128
PACK = 4


def z_own_kernel(
    n, inv_ref, m_ref, v_ref, after_ref, g_ref, c_ref, right_ref, left_ref, far_ref, main_ref, turned_ref
):
    nz = inv_ref.shape[0]
    ny = v_ref.shape[2]
    high, low = split(times_stencil(inv_ref[...]).T * m_ref[...])
    both = jnp.concatenate([high, low], axis=1)
    main_ref[...] = jnp.concatenate([both, both], axis=0)
    first_scale = 1.0 / m_ref[0:1, 0:1]
    last_scale = 1.0 / m_ref[0:1, nz - 1 : nz]
    lane = lax.broadcasted_iota(jnp.int32, (ny, nz), 1)

    m = nz - 1
    index = lax.broadcasted_iota(jnp.int32, right_ref.shape[1:], 0)
    for ref, corners in ((right_ref, ((m, m), (m, m - 1), (m, 0), (m, 1))), (left_ref, ((0, 0), (0, 1), (0, m), (0, m - 1)))):
        row = jnp.zeros(right_ref.shape[1:], F32)
        for position, (i, j) in enumerate(corners):
            row = jnp.where(index == position, inv_ref[i : i + 1, j : j + 1], row)
        ref[12] = row

    def segments(u):
        start = u * ny
        while start < (u + 1) * ny:
            stop = min((start // LINES + 1) * LINES, (u + 1) * ny)
            yield start // LINES, start - u * ny, stop - u * ny
            start = stop

    def step(group, carry):
        pieces = [[] for _ in range(GROUP * ny // LINES)]
        for u in range(GROUP):
            p = group * GROUP + u
            velocities = [v_ref[i, p] for i in range(3)]
            values = []
            for f, field in enumerate(six(velocities, 2)):
                high, low = split(field)
                both = dot(jnp.concatenate([high, low], axis=1), main_ref[...])
                value = both[:, :nz] + both[:, nz:]
                if f < 3:
                    g_ref[f, p] = value
                else:
                    c_ref[f - 3, p] = value
                values.append(value)
            for block, start, stop in segments(u):
                base = block % PACK * 32
                columns = pltpu.roll(values[0][start:stop], base + 1, axis=1)
                for f in range(1, 6):
                    moved = pltpu.roll(values[f][start:stop], (base + 1 + 2 * f) % nz, axis=1)
                    columns = jnp.where(lane[start:stop] // 2 == base // 2 + f, moved, columns)
                for i in range(3):
                    moved = pltpu.roll(velocities[i][start:stop], (base + 14 + 4 * i) % nz, axis=1)
                    columns = jnp.where(lane[start:stop] // 4 == base // 4 + 3 + i, moved, columns)
                pieces[block].append(columns)
        for j, parts in enumerate(pieces):
            if j % PACK == 0:
                packed = jnp.concatenate(parts, axis=0)
                for other in range(1, PACK):
                    columns = jnp.concatenate(pieces[j + other], axis=0)
                    packed = jnp.where(lane[0:LINES] // 32 == other, columns, packed)
                turned_ref[j // PACK] = packed.T
                blocks = pl.ds(group * len(pieces) + j, PACK)

                def rows(position):
                    return turned_ref[j // PACK, pl.ds(position, PACK, stride=32), :]

                for f in range(6):
                    right_ref[f, blocks, :] = rows(2 * f) * last_scale
                    left_ref[f, blocks, :] = rows(2 * f + 1) * first_scale
                for column in range(4):
                    for i in range(3):
                        values = rows(12 + 4 * i + column)
                        ref = right_ref if column < 2 else left_ref
                        ref[6 + 3 * (column % 2) + i, blocks, :] = values
                        far_ref[3 * column + i, blocks, :] = values
        return carry

    lax.fori_loop(0, n // GROUP, step, 0)


def z_own(z_inverse, metric, velocity, after):
    _, n, ny, nz = velocity.shape
    return pl.pallas_call(
        functools.partial(z_own_kernel, n),
        in_specs=[WHOLE, WHOLE, WHOLE, ANY],
        out_specs=[WHOLE] * 5,
        out_shape=[in_vmem(3, n, ny, nz)] * 2 + [layer_shape(13, n * ny // LINES, LINES)] * 2
        + [layer_shape(12, n * ny // LINES, LINES)],
        scratch_shapes=[
            pltpu.VMEM((2 * nz, 2 * nz), BF16),
            pltpu.VMEM((GROUP * ny // LINES // PACK, LINES, LINES), F32),
        ],
        compiler_params=params(),
        cost_estimate=cost(velocity, 3),
        name="z_own",
    )(z_inverse, metric, velocity, after)


def z_side(own_right, own_left, left, right, left_2, right_2, out_ref):
    blocks = own_left.shape[1]
    shape = own_left.shape[1:]

    def pair(ref, start):
        return six([ref[start + i] for i in range(3)], 2), six([ref[start + 3 + i] for i in range(3)], 2)

    def from_left(ref, start):
        far, near = pair(ref, start)
        return [(-NEAR * near[f] - FAR * far[f], -FAR * near[f]) for f in range(6)]

    def from_right(ref, start):
        near, far = pair(ref, start)
        return [(NEAR * near[f] + FAR * far[f], FAR * near[f]) for f in range(6)]

    def entries(ref):
        return [jnp.broadcast_to(ref[12, i : i + 1], shape) for i in range(4)]

    def first_value(ref, corners, f, at_left, at_right):
        x_00, x_01, x_0m, x_0l = corners
        return ref[f] + x_00 * at_left[f][0] + x_01 * at_left[f][1] + x_0m * at_right[f][0] + x_0l * at_right[f][1]

    def last_value(ref, corners, f, at_left, at_right):
        x_mm, x_ml, x_m0, x_m1 = corners
        return ref[f] + x_m0 * at_left[f][0] + x_m1 * at_left[f][1] + x_mm * at_right[f][0] + x_ml * at_right[f][1]

    own_first_row, own_last_row, left_row, right_row = (entries(ref) for ref in (own_left, own_right, left, right))
    at_left, at_right = from_left(left, 6), from_right(right, 6)
    left_at_left, left_at_right = from_left(left_2, 0), from_right(own_left, 6)
    right_at_left, right_at_right = from_left(own_right, 6), from_right(right_2, 6)
    left_den = 1.0 / (1.0 - COUPLING * COUPLING * left_row[0] * own_first_row[0])
    right_den = 1.0 / (1.0 - COUPLING * COUPLING * right_row[0] * own_last_row[0])
    for f in range(8):
        if f < 6:
            own_first = first_value(own_left, own_first_row, f, at_left, at_right)
            own_last = last_value(own_right, own_last_row, f, at_left, at_right)
            left_value = last_value(left, left_row, f, left_at_left, left_at_right)
            right_value = first_value(right, right_row, f, right_at_left, right_at_right)
            left_final = (left_value - COUPLING * left_row[0] * own_first) * left_den
            right_start = (right_value - COUPLING * right_row[0] * own_last) * right_den
            kinds = (
                at_left[f][0] - COUPLING * left_final,
                at_left[f][1],
                at_right[f][0] - COUPLING * right_start,
                at_right[f][1],
            )
        else:
            kinds = (jnp.zeros(shape, F32),) * 4
        for kind, values in enumerate(kinds):
            start = (8 * kind + f) * blocks
            out_ref[start : start + blocks, :] = values


def z_gradient_kernel(
    n, inv_ref, m_ref, g_ref, own_right_ref, own_left_ref, left_ref, right_ref, left_2_ref, right_2_ref, y_ref,
    gradient_ref, out_ref, lines_ref, side_ref, beside_ref, sem,
):
    nz = inv_ref.shape[0]
    ny = g_ref.shape[2]
    y_copy = pltpu.make_async_copy(y_ref, gradient_ref.at[:, 1], sem)
    y_copy.start()
    columns = inv_ref[...].T * m_ref[...]
    index = lax.broadcasted_iota(jnp.int32, (32, nz), 0)
    kind = index // 8
    picked = jnp.where(
        kind == 0,
        columns[0:1],
        jnp.where(kind == 1, columns[1:2], jnp.where(kind == 2, columns[nz - 1 : nz], columns[nz - 2 : nz - 1])),
    )
    wide = jnp.concatenate([jnp.where(index % 8 == f, picked, 0.0) for f in range(6)], axis=1)
    high, low = split(wide)
    side_ref[...] = jnp.concatenate([high, high, low], axis=0)
    blocks = GROUP * ny // LINES
    all_blocks = n * ny // LINES
    z_side(own_right_ref, own_left_ref, left_ref, right_ref, left_2_ref, right_2_ref, beside_ref)

    def step(group, carry):
        sides = []
        for j in range(blocks):
            beside = beside_ref[pl.ds(group * blocks + j, 32, stride=all_blocks), :]
            high, low = split(beside.T)
            sides.append(jnp.concatenate([high, low, high], axis=1))
        for pair in range(GROUP // 2):
            half = blocks // (GROUP // 2)
            lines = jnp.concatenate(sides[pair * half : (pair + 1) * half], axis=0)
            lines_ref[group * (GROUP // 2) + pair] = lines
            for f in range(0, 3):
                added = dot(lines, side_ref[:, f * nz : (f + 1) * nz])
                for u in range(2):
                    p = group * GROUP + 2 * pair + u
                    out_ref[f, p] = added[u * ny : (u + 1) * ny] + g_ref[f, p]
        return carry

    lax.fori_loop(0, n // GROUP, step, 0)
    y_copy.wait()


def z_gradient_join(z_inverse, metric, own, lines, y_gradient):
    _, n, ny, nz = own.shape
    return pl.pallas_call(
        functools.partial(z_gradient_kernel, n),
        in_specs=[WHOLE] * 10,
        out_specs=[ANY, WHOLE, WHOLE, WHOLE],
        out_shape=[
            layer_shape(3, 3, n, ny, nz),
            in_vmem(3, n, ny, nz),
            pltpu.VMEM((n // 2, 2 * ny, 96), BF16),
            pltpu.VMEM((96, 6 * nz), BF16),
        ],
        scratch_shapes=[pltpu.VMEM((32 * (n * ny // LINES), LINES), F32), pltpu.SemaphoreType.DMA],
        input_output_aliases={2: 1},
        compiler_params=params(),
        cost_estimate=cost(own, Z_COST),
        name="z_gradient_join",
    )(z_inverse, metric, own, *lines, y_gradient)


def z_convection_kernel(n, part_ref, lines_ref, side_ref, after_ref, c_ref):
    _, _, ny, nz = part_ref.shape

    def step(group, carry):
        for pair in range(GROUP // 2):
            lines = lines_ref[group * (GROUP // 2) + pair]
            for f in range(3):
                added = dot(lines, side_ref[:, (3 + f) * nz : (4 + f) * nz])
                for u in range(2):
                    p = group * GROUP + 2 * pair + u
                    c_ref[f, p] = added[u * ny : (u + 1) * ny] + part_ref[f, p]
        return carry

    lax.fori_loop(0, n // GROUP, step, 0)


def z_convection_join(partial, lines, side, after):
    _, n, ny, nz = partial.shape
    return pl.pallas_call(
        functools.partial(z_convection_kernel, n),
        in_specs=[WHOLE] * 3 + [ANY],
        out_specs=WHOLE,
        out_shape=in_vmem(3, n, ny, nz),
        input_output_aliases={0: 0},
        compiler_params=params(),
        cost_estimate=cost(partial, Z_COST),
        name="z_convection_join",
    )(partial, lines, side, after)


def on_device(mesh, velocity, metric_x, metric_y, metric_z, x_inverse, y_inverse, z_inverse):
    n = velocity.shape[1]
    blocks = mesh.shape["gx"] * 2
    across = [(i, (i + 1) % blocks) for i in range(1, blocks, 2)]
    across = across + [(j, i) for i, j in across]
    beside = [(0, 1), (1, 0)]
    count = mesh.shape["gz"]

    def shift(by):
        return [(i, (i + by) % count) for i in range(count)]

    own, inner = prepare(velocity)
    near = lax.ppermute(own, ("gx", "gy"), across)
    halo = lax.ppermute(inner, "gy", beside)
    held = pltpu.with_memory_space_constraint(velocity, pltpu.VMEM)
    table, y_inverse, metric_y, z_inverse, metric_z = tables(
        x_inverse, metric_x[None], y_inverse, metric_y[None], z_inverse, metric_z[None], own
    )

    x_sent, x_partial = x_ends(table, held, halo)
    x_received = lax.ppermute(x_sent, ("gx", "gy"), across)

    z_gradient, convection, to_right, to_left, to_far = z_own(z_inverse, metric_z, held, x_sent)
    left_far = lax.ppermute(to_far, "gz", shift(2))
    right_far = left_far if shift(2) == shift(-2) else lax.ppermute(to_far, "gz", shift(-2))
    z_lines = (
        to_right,
        to_left,
        lax.ppermute(to_right, "gz", shift(1)),
        lax.ppermute(to_left, "gz", shift(-1)),
        left_far,
        right_far,
    )

    y_gradient, convection = y_solve(y_inverse, metric_y, held, convection, near)
    gradient, z_gradient, lines, side = z_gradient_join(z_inverse, metric_z, z_gradient, z_lines, y_gradient)
    outer, x_end = x_face(table, x_received, x_sent, x_partial, own, near, z_gradient, n)
    x_other = lax.ppermute(x_end, "gy", beside)

    convection = z_convection_join(convection, lines, side, x_end)
    return tuple(
        x_solve(table, held, near, halo, outer, x_end, x_other, convection, z_gradient, gradient)
    )


def solution(mesh):
    return jax.shard_map(
        functools.partial(on_device, mesh),
        mesh=mesh,
        in_specs=(
            P(None, ("gx", "gy"), None, "gz"),
            P(("gx", "gy")),
            P(),
            P("gz"),
            P(("gx", "gy"), None),
            P(),
            P("gz", None),
        ),
        out_specs=(P(None, None, ("gx", "gy"), None, "gz"), P(None, ("gx", "gy"), None, "gz")),
        check_vma=False,
    )
```

time: 39.2 us -> 36.6 us (0.934)
  Pallas kernels: 25.7 us -> 24.2 us
  starting transfers between devices: 11.5 us -> 10.4 us
    ppermute x1, starting transfers between devices: 1.7 us -> 0.61 us  [on_device(): x_received = lax.ppermute(x_sent, ('gx', 'gy'), across)]
    ppermute x1, waiting for transfers between devices: 1.04 us -> 0.01 us  [on_device(): x_received = lax.ppermute(x_sent, ('gx', 'gy'), across)]
    ppermute x1, waiting for transfers between devices: 0.01 us -> 0.98 us  [on_device(): x_other = lax.ppermute(x_end, 'gy', beside)]
    pallas_call x1, Pallas kernels: 6.39 us -> 5.73 us  [x_solve(): pl.pallas_call(functools.partial(x_solve_kernel, n, ny), in_specs=[WHOLE]...]
    pallas_call x2 -> x4, Pallas kernels: 6.29 us -> 5.75 us  [the longest x1 2.21 us: z_gradient_join(): pl.pallas_call(functools.partial(z_gradient_kernel, n), in_specs=[WHOLE]...]
where the time goes in v2:
time: 36.6 us; the launch traced here: 36.4 us
  Pallas kernels  24.2 us (66%)
  starting transfers between devices  10.4 us (28%)
  waiting for transfers between devices  1 us (3%)
  between operations  0.76 us (2%)
    pallas_call x1, Pallas kernels, x_solve(): pl.pallas_call(functools.partial(x_solve_kernel, n, ny), in_specs=[WHOLE]...  5.73 us
    pallas_call x1, Pallas kernels, z_own(): pl.pallas_call(functools.partial(z_own_kernel, n), in_specs=[WHOLE, WHOLE...  5.11 us
    pallas_call x1, Pallas kernels, y_solve(): pl.pallas_call(functools.partial(y_kernel, n), in_specs=[WHOLE] * 4 + [AN...  4.95 us
    ppermute x1, starting transfers between devices, on_device(): near = lax.ppermute(own, ('gx', 'gy'), across)  4.71 us
    pallas_call x1, Pallas kernels, z_gradient_join(): pl.pallas_call(functools.partial(z_gradient_kernel, n), in_specs=[WHOLE]...  2.21 us
    pallas_call x1, Pallas kernels, x_ends(): pl.pallas_call(functools.partial(x_ends_kernel, n, ny), in_specs=[WHOLE]...  2.2 us
    ppermute x1, starting transfers between devices, on_device(): left_far = lax.ppermute(to_far, 'gz', shift(2))  1.58 us
    ppermute x1, starting transfers between devices, on_device(): lax.ppermute(to_right, 'gz', shift(1))  1.49 us
  transfers between devices with their start and end apart: 7, of which 1 were waited for; matrix products, arithmetic and copies ran while one was open for 0% of the time, Pallas kernels for 45%

profile of v2, /device:TPU:0, one launch (start us, length us, event | category | flops | bytes accessed | tf_op | source)
XLA Modules:
  0.0 36.4 jit_solution(1011281117989191181)
XLA Ops:
  0.6 0.0 copy-start
  0.6 1.5 %prepare.1 = (f32[3,192,128]{2,1,0:T(8,128)S(1)}, f32[3,2,192,128]{3,2,1,0:T(8,128)S(1)}) custom-call(f32[3,16,192,128]{3,2,1,0:T(8,128)} %v_ref.9), custom_call_target="tpu_custom_call" | custom-call | tf_op jit(solution)/shard_map/prepare/pallas_call | solution.py:108
  2.1 0.5 %collective-permute-start.1 = (f32[3,2,192,128]{3,2,1,0:T(8,128)S(1)}, f32[3,2,192,128]{3,2,1,0:T(8,128)S(1)}, u32[]{:S(2)}, u32[]{:S(2)}) collective-permute-start(f32[3,2,192,128]{3,2,1,0:T(8,128)S(1)} %get-tuple-element.26), channel_id=1, source_target_pairs={{0,1},{1,0},{2,3},{3,2},{4,5},{5,4},{6,7},{7,6},{8,9},{9,8},{10,11... | collective-permute-start | bytes 1769480 | tf_op jit(solution)/shard_map/ppermute | solution.py:712
  2.6 4.7 %collective-permute-start = (f32[3,192,128]{2,1,0:T(8,128)S(1)}, f32[3,192,128]{2,1,0:T(8,128)S(1)}, u32[]{:S(2)}, u32[]{:S(2)}) collective-permute-start(f32[3,192,128]{2,1,0:T(8,128)S(1)} %get-tuple-element.24.after_ref.own_ref), channel_id=1, source_target_pairs={{1,8},{9,16},{17,24},{25,0},{8,1},{16,9},{24,17},{0,25},{3,10},{11... | collective-permute-start | bytes 884744 | tf_op jit(solution)/shard_map/ppermute | solution.py:711
  7.3 1.1 %tables.1 = (f32[89,8,128]{2,1,0:T(8,128)S(1)}, f32[192,192]{1,0:T(8,128)S(1)}, f32[1,192]{1,0:T(1,128)S(1)}, f32[128,128]{1,0:T(8,128)S(1)}, f32[1,128]{1,0:T(1,128)S(1)}) custom-call(f32[16,16]{1,0:T(8,128)} %xi_ref.1, f32[1,16]{1,0:T(1,128)} %bitcast.4, f32[192,192]{1,0:T(8,128)} %yi_ref.1, f32[1,192]{1,0:T(1,128)} %bitcast.3, f32[128,128]{1,0:T(8,128)} %zi_ref.1, ...), custom_call_target="tpu_custom_call" | custom-call | tf_op jit(solution)/shard_map/tables/pallas_call | solution.py:202
  8.4 0.0 collective-permute-done.1.halo_ref
  8.4 0.0 copy-done
  8.4 2.2 %x_ends.1 = (f32[1160,128]{1,0:T(8,128)S(1)}, f32[6,192,128]{2,1,0:T(8,128)S(1)}) custom-call(f32[89,8,128]{2,1,0:T(8,128)S(1)} %get-tuple-element.25.table_ref, f32[3,16,192,128]{3,2,1,0:T(8,128)S(1)} %copy-done, f32[3,2,192,128]{3,2,1,0:T(8,128)S(1)} %collective-permute-done.1.halo_ref), custom_call_target="tpu_custom_call" | custom-call | flops 3 | bytes 3 | tf_op jit(solution)/shard_map/x_ends/pallas_call | solution.py:248
  10.6 0.6 %collective-permute-start.2 = (f32[1160,128]{1,0:T(8,128)S(1)}, f32[1160,128]{1,0:T(8,128)S(1)}, u32[]{:S(2)}, u32[]{:S(2)}) collective-permute-start(f32[1160,128]{1,0:T(8,128)S(1)} %get-tuple-element.27.after_ref.ws_ref), channel_id=1, source_target_pairs={{1,8},{9,16},{17,24},{25,0},{8,1},{16,9},{24,17},{0,25},{3,10},{11... | collective-permute-start | bytes 1781768 | tf_op jit(solution)/shard_map/ppermute | solution.py:719
  11.2 5.1 %z_own.1 = (f32[3,16,192,128]{3,2,1,0:T(8,128)S(1)}, f32[3,16,192,128]{3,2,1,0:T(8,128)S(1)}, f32[13,24,128]{2,1,0:T(8,128)S(1)}, f32[13,24,128]{2,1,0:T(8,128)S(1)}, f32[12,24,128]{2,1,0:T(8,128)S(1)}) custom-call(f32[128,128]{1,0:T(8,128)S(1)} %get-tuple-element.29.inv_ref, f32[1,128]{1,0:T(1,128)S(1)} %get-tuple-element.30.m_ref, ...), custom_call_target="tpu_custom_call" | custom-call | flops 3 | bytes 3 | tf_op jit(solution)/shard_map/z_own/pallas_call | solution.py:536
  16.4 1.6 %collective-permute-start.5 = (f32[12,24,128]{2,1,0:T(8,128)S(1)}, f32[12,24,128]{2,1,0:T(8,128)S(1)}, u32[]{:S(2)}, u32[]{:S(2)}) collective-permute-start(f32[12,24,128]{2,1,0:T(8,128)S(1)} %get-tuple-element.34), channel_id=1, source_target_pairs={{0,4},{2,6},{4,0},{6,2},{1,5},{3,7},{5,1},{7,3},{8,12},{10,14},{12... | collective-permute-start | bytes 442376 | tf_op jit(solution)/shard_map/ppermute | solution.py:722
  17.9 1.5 %collective-permute-start.3 = (f32[13,24,128]{2,1,0:T(8,128)S(1)}, f32[13,24,128]{2,1,0:T(8,128)S(1)}, u32[]{:S(2)}, u32[]{:S(2)}) collective-permute-start(f32[13,24,128]{2,1,0:T(8,128)S(1)} %get-tuple-element.32.own_right_ref), channel_id=1, source_target_pairs={{0,2},{2,4},{4,6},{6,0},{1,3},{3,5},{5,7},{7,1},{8,10},{10,12},{12... | collective-permute-start | bytes 479240 | tf_op jit(solution)/shard_map/ppermute | solution.py:727
  19.4 1.4 %collective-permute-start.4 = (f32[13,24,128]{2,1,0:T(8,128)S(1)}, f32[13,24,128]{2,1,0:T(8,128)S(1)}, u32[]{:S(2)}, u32[]{:S(2)}) collective-permute-start(f32[13,24,128]{2,1,0:T(8,128)S(1)} %get-tuple-element.33.own_left_ref), channel_id=1, source_target_pairs={{0,6},{2,0},{4,2},{6,4},{1,7},{3,1},{5,3},{7,5},{8,14},{10,8},{12,... | collective-permute-start | bytes 479240 | tf_op jit(solution)/shard_map/ppermute | solution.py:728
  20.9 0.0 collective-permute-done.after_ref.near_ref
  20.9 4.9 %y_solve.1 = (f32[3,16,192,128]{3,2,1,0:T(8,128)S(1)}, f32[3,16,192,128]{3,2,1,0:T(8,128)S(1)}) custom-call(f32[192,192]{1,0:T(8,128)S(1)} %get-tuple-element.35.inv_ref, f32[1,192]{1,0:T(1,128)S(1)} %get-tuple-element.36.m_ref, f32[3,16,192,128]{3,2,1,0:T(8,128)S(1)} %copy-done, ...), custom_call_target="tpu_custom_call", output_to_operand_aliasing={{1}: (3, {})} | custom-call | flops 20000000000 | bytes 20000000000 | tf_op jit(solution)/shard_map/y_solve/pallas_call | solution.py:439
  25.8 0.0 collective-permute-done.5.left_2_ref.right_2_ref
  25.8 0.0 collective-permute-done.3.left_ref
  25.9 0.0 collective-permute-done.4.right_ref
  25.9 2.2 %z_gradient_join.1 = (f32[3,3,16,192,128]{4,3,2,1,0:T(8,128)}, f32[3,16,192,128]{3,2,1,0:T(8,128)S(1)}, bf16[8,384,96]{2,1,0:T(8,128)(2,1)S(1)}, bf16[96,768]{1,0:T(8,128)(2,1)S(1)}) custom-call(f32[128,128]{1,0:T(8,128)S(1)} %get-tuple-element.29.inv_ref, f32[1,128]{1,0:T(1,128)S(1)} %get-tuple-element.30.m_ref, ...), custom_call_target="tpu_custom_call", output_to_operand_aliasing={{1}: (2, {})} | custom-call | flops 20000000000 | bytes 20000000000 | tf_op jit(solution)/shard_map/z_gradient_join/pallas_call | solution.py:651
  28.1 0.0 collective-permute-done.2.wr_ref
  28.1 0.5 %x_face.1 = (f32[6,192,128]{2,1,0:T(8,128)S(1)}, f32[1160,128]{1,0:T(8,128)S(1)}) custom-call(f32[89,8,128]{2,1,0:T(8,128)S(1)} %get-tuple-element.25.table_ref, f32[1160,128]{1,0:T(8,128)S(1)} %collective-permute-done.2.wr_ref, f32[1160,128]{1,0:T(8,128)S(1)} %get-tuple-element.27.after_ref.ws_ref, f32[6,192,128]{2,1,0:T(8,128)S(1)} %get-tuple-element.28.l_ref, ...), custom_call_target="tpu_custom_call" | custom-call | flops 1 | bytes 1 | tf_op jit(solution)/shard_map/x_face/pallas_call | solution.py:291
  28.6 0.1 collective-permute-start.6
  28.6 1.0 %z_convection_join.1.part_ref = f32[3,16,192,128]{3,2,1,0:T(8,128)S(1)} custom-call(f32[3,16,192,128]{3,2,1,0:T(8,128)S(1)} %get-tuple-element.42.part_ref, bf16[8,384,96]{2,1,0:T(8,128)(2,1)S(1)} %get-tuple-element.43.lines_ref, bf16[96,768]{1,0:T(8,128)(2,1)S(1)} %get-tuple-element.44.side_ref, ...), custom_call_target="tpu_custom_call", output_to_operand_aliasing={{}: (0, {})} | custom-call | flops 20000000000 | bytes 20000000000 | tf_op jit(solution)/shard_map/z_convection_join/pallas_call | solution.py:687
  29.7 1.0 %collective-permute-done.6.r_ref = f32[1160,128]{1,0:T(8,128)S(1)} collective-permute-done((f32[1160,128]{1,0:T(8,128)S(1)}, f32[1160,128]{1,0:T(8,128)S(1)}, u32[]{:S(2)}, u32[]{:S(2)}) %collective-permute-start.6) | collective-permute-done | bytes 593952 | tf_op jit(solution)/shard_map/ppermute | solution.py:736
  30.6 5.7 %x_solve.1 = (f32[3,3,16,192,128]{4,3,2,1,0:T(8,128)}, f32[3,16,192,128]{3,2,1,0:T(8,128)}) custom-call(f32[89,8,128]{2,1,0:T(8,128)S(1)} %get-tuple-element.25.table_ref, f32[3,16,192,128]{3,2,1,0:T(8,128)S(1)} %copy-done, f32[3,192,128]{2,1,0:T(8,128)S(1)} %collective-permute-done.after_ref.near_ref, ...), custom_call_target="tpu_custom_call", output_to_operand_aliasing={{0}: (9, {})} | custom-call | flops 5 | bytes 5 | tf_op jit(solution)/shard_map/x_solve/pallas_call | solution.py:391
Async XLA Ops:
  0.6 7.8 %copy-start = (f32[3,16,192,128]{3,2,1,0:T(8,128)S(1)}, f32[3,16,192,128]{3,2,1,0:T(8,128)}, u32[]{:S(2)}) copy-start(f32[3,16,192,128]{3,2,1,0:T(8,128)} %v_ref.9) | copy-start | bytes 14155780
  2.1 6.3 %collective-permute-start.1 = (f32[3,2,192,128]{3,2,1,0:T(8,128)S(1)}, f32[3,2,192,128]{3,2,1,0:T(8,128)S(1)}, u32[]{:S(2)}, u32[]{:S(2)}) collective-permute-start(f32[3,2,192,128]{3,2,1,0:T(8,128)S(1)} %get-tuple-element.26), channel_id=1, source_target_pairs={{0,1},{1,0},{2,3},{3,2},{4,5},{5,4},{6,7},{7,6},{8,9},{9,8},{10,11... | collective-permute-start | bytes 1769480 | tf_op jit(solution)/shard_map/ppermute | solution.py:712
  2.6 18.2 %collective-permute-start = (f32[3,192,128]{2,1,0:T(8,128)S(1)}, f32[3,192,128]{2,1,0:T(8,128)S(1)}, u32[]{:S(2)}, u32[]{:S(2)}) collective-permute-start(f32[3,192,128]{2,1,0:T(8,128)S(1)} %get-tuple-element.24.after_ref.own_ref), channel_id=1, source_target_pairs={{1,8},{9,16},{17,24},{25,0},{8,1},{16,9},{24,17},{0,25},{3,10},{11... | collective-permute-start | bytes 884744 | tf_op jit(solution)/shard_map/ppermute | solution.py:711
  10.6 17.4 %collective-permute-start.2 = (f32[1160,128]{1,0:T(8,128)S(1)}, f32[1160,128]{1,0:T(8,128)S(1)}, u32[]{:S(2)}, u32[]{:S(2)}) collective-permute-start(f32[1160,128]{1,0:T(8,128)S(1)} %get-tuple-element.27.after_ref.ws_ref), channel_id=1, source_target_pairs={{1,8},{9,16},{17,24},{25,0},{8,1},{16,9},{24,17},{0,25},{3,10},{11... | collective-permute-start | bytes 1781768 | tf_op jit(solution)/shard_map/ppermute | solution.py:719
  16.4 9.5 %collective-permute-start.5 = (f32[12,24,128]{2,1,0:T(8,128)S(1)}, f32[12,24,128]{2,1,0:T(8,128)S(1)}, u32[]{:S(2)}, u32[]{:S(2)}) collective-permute-start(f32[12,24,128]{2,1,0:T(8,128)S(1)} %get-tuple-element.34), channel_id=1, source_target_pairs={{0,4},{2,6},{4,0},{6,2},{1,5},{3,7},{5,1},{7,3},{8,12},{10,14},{12... | collective-permute-start | bytes 442376 | tf_op jit(solution)/shard_map/ppermute | solution.py:722
  17.9 7.9 %collective-permute-start.3 = (f32[13,24,128]{2,1,0:T(8,128)S(1)}, f32[13,24,128]{2,1,0:T(8,128)S(1)}, u32[]{:S(2)}, u32[]{:S(2)}) collective-permute-start(f32[13,24,128]{2,1,0:T(8,128)S(1)} %get-tuple-element.32.own_right_ref), channel_id=1, source_target_pairs={{0,2},{2,4},{4,6},{6,0},{1,3},{3,5},{5,7},{7,1},{8,10},{10,12},{12... | collective-permute-start | bytes 479240 | tf_op jit(solution)/shard_map/ppermute | solution.py:727
  19.4 6.4 %collective-permute-start.4 = (f32[13,24,128]{2,1,0:T(8,128)S(1)}, f32[13,24,128]{2,1,0:T(8,128)S(1)}, u32[]{:S(2)}, u32[]{:S(2)}) collective-permute-start(f32[13,24,128]{2,1,0:T(8,128)S(1)} %get-tuple-element.33.own_left_ref), channel_id=1, source_target_pairs={{0,6},{2,0},{4,2},{6,4},{1,7},{3,1},{5,3},{7,5},{8,14},{10,8},{12,... | collective-permute-start | bytes 479240 | tf_op jit(solution)/shard_map/ppermute | solution.py:728
  28.6 2.1 %collective-permute-start.6 = (f32[1160,128]{1,0:T(8,128)S(1)}, f32[1160,128]{1,0:T(8,128)S(1)}, u32[]{:S(2)}, u32[]{:S(2)}) collective-permute-start(f32[1160,128]{1,0:T(8,128)S(1)} %get-tuple-element.41.after_ref.e_ref), channel_id=1, source_target_pairs={{0,1},{1,0},{2,3},{3,2},{4,5},{5,4},{6,7},{7,6},{8,9},{9,8},{10,11... | collective-permute-start | bytes 1781768 | tf_op jit(solution)/shard_map/ppermute | solution.py:736

commit v3 on v2

--- a/solution.py
+++ b/solution.py
@@ -15,8 +15,8 @@
 SMEM = pltpu.SMEM
 VMEM_LIMIT = 20 * 1024 * 1024
 GROUP = 8
-Y_COST = 20_000_000_000
-Z_COST = 20_000_000_000
+EARLY = 3
+SHORT, LONG = 4, 20_000_000_000
 
 
 def split(values):
@@ -61,8 +61,8 @@
 SCALARS = pl.BlockSpec(memory_space=SMEM)
 
 
-def cost(array, passes):
-    return pl.CostEstimate(flops=passes, bytes_accessed=passes, transcendentals=0)
+def cost(flops):
+    return pl.CostEstimate(flops=flops, bytes_accessed=1, transcendentals=0)
 
 
 def layer_shape(*shape):
@@ -85,8 +85,9 @@
     def __init__(self, n):
         self.source, self.forward, self.backward = 0, n, 2 * n
         self.send, self.last = 3 * n, 4 * n + 2
-        self.oo, self.oo1, self.qo, self.qo1, self.qq = range(5 * n + 4, 5 * n + 9)
-        self.size = 5 * n + 9
+        self.outer, self.inner = 5 * n + 4, 6 * n + 4
+        self.oo, self.oo1, self.qo, self.qo1, self.qq = range(7 * n + 4, 7 * n + 9)
+        self.size = 7 * n + 9
 
 
 def prepare_kernel(n, v_ref, own_ref, halo_ref, sem):
@@ -118,7 +119,7 @@
 
 def tables_kernel(
     n, xi_ref, mx_ref, yi_ref, my_ref, zi_ref, mz_ref, after_ref,
-    table_ref, y_ref, y_metric_ref, z_ref, z_metric_ref, x_ref, m_ref, sem,
+    table_ref, y_high_ref, y_low_ref, z_main_ref, z_ref, z_metric_ref, x_ref, m_ref, y_ref, y_metric_ref, sem,
 ):
     ends = Ends(n)
     nz = table_ref.shape[2]
@@ -187,6 +188,10 @@
         far = factor * sign_q * FAR * at_q
         table_ref[base + n] = jnp.where(first, near, far)
         table_ref[base + n + 1] = jnp.where(first, far, near)
+    for k in range(n):
+        left, right = FAR * metric[k] * entry(k, 0), FAR * metric[k] * entry(k, n - 1)
+        table_ref[table.outer + k] = jnp.where(first, left, right)
+        table_ref[table.inner + k] = jnp.where(first, right, left)
     table_ref[table.oo] = jnp.where(first, outer[0], outer[n - 1])
     table_ref[table.oo1] = jnp.where(first, outer[1], outer[n - 2])
     table_ref[table.qo] = jnp.where(first, inner[0], inner[n - 1])
@@ -194,6 +199,14 @@
     table_ref[table.qq] = jnp.where(first, inner[n - 1], inner[0])
     for copy in copies:
         copy.wait()
+    ny = y_ref.shape[0]
+    row = lax.broadcasted_iota(jnp.int32, (ny, ny), 0)
+    column = lax.broadcasted_iota(jnp.int32, (ny, ny), 1)
+    y_metric = jnp.sum(jnp.where(row == column, y_metric_ref[...], 0.0), axis=1, keepdims=True)
+    y_high_ref[...], y_low_ref[...] = split(times_stencil(y_ref[...]) * y_metric)
+    high, low = split(times_stencil(z_ref[...]).T * z_metric_ref[...])
+    both = jnp.concatenate([high, low], axis=1)
+    z_main_ref[...] = jnp.concatenate([both, both], axis=0)
 
 
 def tables(x_inverse, metric_x, y_inverse, metric_y, z_inverse, metric_z, after):
@@ -202,16 +215,24 @@
     return pl.pallas_call(
         functools.partial(tables_kernel, n),
         in_specs=[ANY] * 7,
-        out_specs=[WHOLE] * 5,
+        out_specs=[WHOLE] * 6,
         out_shape=[
             in_vmem(Table(n).size, 8, nz),
-            in_vmem(ny, ny),
-            in_vmem(1, ny),
+            pltpu.VMEM((ny, ny), BF16),
+            pltpu.VMEM((ny, ny), BF16),
+            pltpu.VMEM((2 * nz, 2 * nz), BF16),
             in_vmem(nz, nz),
             in_vmem(1, nz),
         ],
-        scratch_shapes=[pltpu.VMEM((n, n), F32), pltpu.VMEM((1, n), F32), pltpu.SemaphoreType.DMA((6,))],
+        scratch_shapes=[
+            pltpu.VMEM((n, n), F32),
+            pltpu.VMEM((1, n), F32),
+            pltpu.VMEM((ny, ny), F32),
+            pltpu.VMEM((1, ny), F32),
+            pltpu.SemaphoreType.DMA((6,)),
+        ],
         compiler_params=params(),
+        cost_estimate=cost(LONG),
         name="tables",
     )(*(pltpu.with_memory_space_constraint(value, pltpu.HBM) for value in inputs), after)
 
@@ -251,7 +272,7 @@
         out_specs=[WHOLE, WHOLE],
         out_shape=[layer_shape(6 * ny + 8, nz), layer_shape(6, ny, nz)],
         compiler_params=params(),
-        cost_estimate=cost(velocity, 3),
+        cost_estimate=cost(SHORT),
         name="x_ends",
     )(table, velocity, halo)
 
@@ -294,16 +315,88 @@
         out_specs=[WHOLE, WHOLE],
         out_shape=[layer_shape(6, ny, nz), layer_shape(6 * ny + 8, nz)],
         compiler_params=params(),
-        cost_estimate=cost(received, 1),
+        cost_estimate=cost(SHORT),
         name="x_face",
     )(table, received, sent, partial, own, near, after)
 
 
+def x_sweeps(n, table, table_ref, line, at_first, at_second, at_last_but_one, at_last):
+    forward = []
+    for k in range(n):
+        if k == 0:
+            source = 28.0 * line[1] + (line[2] + at_first)
+        elif k == 1:
+            source = 28.0 * (line[2] - line[0]) + (line[3] + at_second)
+        elif k == n - 1:
+            source = (at_last - line[n - 3]) - 28.0 * line[n - 2]
+        elif k == n - 2:
+            source = 28.0 * (line[n - 1] - line[n - 3]) + (at_last_but_one - line[n - 4])
+        else:
+            source = 28.0 * (line[k + 1] - line[k - 1]) + (line[k + 2] - line[k - 2])
+        value = table_ref[table.source + k] * source
+        if k > 0:
+            value = value - table_ref[table.forward + k] * forward[k - 1]
+        forward.append(value)
+    solved = [None] * (n - 1) + [forward[n - 1]]
+    for k in reversed(range(n - 1)):
+        solved[k] = forward[k] - table_ref[table.backward + k] * solved[k + 1]
+    return solved
+
+
+def each_side(run):
+    first = lax.axis_index("gy") == 0
+    pl.when(first)(functools.partial(run, True))
+    pl.when(jnp.logical_not(first))(functools.partial(run, False))
+
+
+def x_gradient_kernel(n, ny, table_ref, v_ref, near_ref, halo_ref, y_ref, gradient_ref, g_ref, sem):
+    table = Table(n)
+    y_copy = pltpu.make_async_copy(y_ref, gradient_ref.at[:, 1], sem)
+    y_copy.start()
+
+    def run(first):
+        sign = -1.0 if first else 1.0
+        near_j, far_j = (0, 1) if first else (1, 0)
+
+        def tile(index, carry):
+            rows = pl.ds(pl.multiple_of(index * 8, 8), 8)
+            for f in range(3):
+                line = [v_ref[f, k, rows, :] for k in range(n)]
+                inner_near = -sign * halo_ref[f, near_j, rows, :]
+                inner = 28.0 * inner_near - sign * halo_ref[f, far_j, rows, :]
+                near = sign * near_ref[f, rows, :]
+                zero = jnp.zeros_like(near)
+                ends = (zero, near, inner_near, inner) if first else (inner, inner_near, near, zero)
+                for k, value in enumerate(x_sweeps(n, table, table_ref, line, *ends)):
+                    g_ref[f, k, rows, :] = value
+            return carry
+
+        lax.fori_loop(0, ny // 8, tile, 0)
+
+    each_side(run)
+    y_copy.wait()
+
+
+def x_gradient_own(table, velocity, near, halo, y_gradient):
+    _, n, ny, nz = velocity.shape
+    return pl.pallas_call(
+        functools.partial(x_gradient_kernel, n, ny),
+        in_specs=[WHOLE] * 5,
+        out_specs=[ANY, WHOLE],
+        out_shape=[layer_shape(3, 3, n, ny, nz), in_vmem(3, n, ny, nz)],
+        scratch_shapes=[pltpu.SemaphoreType.DMA],
+        compiler_params=params(),
+        cost_estimate=cost(SHORT),
+        name="x_gradient_own",
+    )(table, velocity, near, halo, y_gradient)
+
+
 def x_solve_kernel(
-    n, ny, table_ref, v_ref, near_ref, halo_ref, w_ref, e_ref, r_ref, part_ref, z_ref, held_ref,
-    gradient_ref, convection_ref, g_ref, c_ref, sem,
+    n, ny, table_ref, v_ref, near_ref, halo_ref, w_ref, e_ref, r_ref, own_ref, part_ref, lines_ref, side_ref, z_ref, held_ref,
+    gradient_ref, convection_ref, g_ref, c_ref, beside_ref, sem,
 ):
     table = Table(n)
+    nz = v_ref.shape[3]
     parts = sem.shape[1]
     share = ny // parts
     z_copy = pltpu.make_async_copy(z_ref, gradient_ref.at[:, 2], sem.at[2, 0])
@@ -320,62 +413,46 @@
         )
 
     def run(first):
-        sign_o = -1.0 if first else 1.0
+        sign = -1.0 if first else 1.0
         near_j, far_j = (0, 1) if first else (1, 0)
 
-        def tile(index, carry):
-            start = pl.multiple_of(index * 8, 8)
-            rows = pl.ds(start, 8)
-            near = six([near_ref[i, rows, :] for i in range(3)], 0)
-            inner_near = six([halo_ref[i, near_j, rows, :] for i in range(3)], 0)
-            inner_far = six([halo_ref[i, far_j, rows, :] for i in range(3)], 0)
-            for f in range(6):
-                if f < 3:
-                    line = [v_ref[f, k, rows, :] for k in range(n)]
-                else:
+        def step(part, carry):
+            base = pl.multiple_of(part * share, 16)
+            lines = lines_ref[:, pl.ds(base, share), :].reshape(n * share, lines_ref.shape[2])
+            beside_ref[...] = dot(lines, side_ref[:, 3 * nz :])
+            for offset in range(0, share, 8):
+                start = base + offset
+                rows = pl.ds(start, 8)
+                near = six([near_ref[i, rows, :] for i in range(3)], 0)
+                inner_near = six([halo_ref[i, near_j, rows, :] for i in range(3)], 0)
+                inner_far = six([halo_ref[i, far_j, rows, :] for i in range(3)], 0)
+                for f in range(6):
+                    field = pl.ds(f * ny + start, 8)
+                    outer = w_ref[f, rows, :]
+                    inner = scale * (r_ref[field, :] - weight * e_ref[field, :])
+                    if f < 3:
+                        for k in range(n):
+                            g_ref[f, k, rows, :] = (
+                                own_ref[f, k, rows, :]
+                                + table_ref[table.outer + k] * outer
+                                + table_ref[table.inner + k] * inner
+                            )
+                        continue
                     line = [v_ref[f - 3, k, rows, :] * v_ref[0, k, rows, :] for k in range(n)]
-                field = pl.ds(f * ny + start, 8)
-                inner = -sign_o * (28.0 * inner_near[f] + inner_far[f])
-                inner = inner + scale * (r_ref[field, :] - weight * e_ref[field, :])
-                outer = w_ref[f, rows, :]
-                forward = []
-                for k in range(n):
-                    if k == 0:
-                        source = 28.0 * line[1] + line[2] + (outer if first else inner)
-                    elif k == 1:
-                        source = 28.0 * (line[2] - line[0]) + (line[3] - (near[f] if first else inner_near[f]))
-                    elif k == n - 1:
-                        source = (inner if first else outer) - 28.0 * line[n - 2] - line[n - 3]
-                    elif k == n - 2:
-                        source = 28.0 * (line[n - 1] - line[n - 3]) + (
-                            (inner_near[f] if first else near[f]) - line[n - 4]
-                        )
-                    else:
-                        source = 28.0 * (line[k + 1] - line[k - 1]) + (line[k + 2] - line[k - 2])
-                    value = table_ref[table.source + k] * source
-                    if k > 0:
-                        value = value - table_ref[table.forward + k] * forward[k - 1]
-                    forward.append(value)
-                solved = None
-                for k in reversed(range(n)):
-                    solved = forward[k] if k == n - 1 else forward[k] - table_ref[table.backward + k] * solved
-                    if f < 3:
-                        g_ref[f, k, rows, :] = solved
-                    else:
-                        c_ref[f - 3, k, rows, :] = solved + part_ref[f - 3, k, rows, :]
-            return carry
-
-        def step(part, carry):
-            lax.fori_loop(part * (share // 8), (part + 1) * (share // 8), tile, 0)
+                    inner = inner - sign * (28.0 * inner_near[f] + inner_far[f])
+                    ends = (outer, sign * near[f], -sign * inner_near[f], inner)
+                    ends = ends if first else ends[::-1]
+                    for k, value in enumerate(x_sweeps(n, table, table_ref, line, *ends)):
+                        row = k * share + offset
+                        beside = beside_ref[row : row + 8, (f - 3) * nz : (f - 2) * nz]
+                        c_ref[f - 3, k, rows, :] = value + (part_ref[f - 3, k, rows, :] + beside)
             for copy in copies(part):
                 copy.start()
             return carry
 
         lax.fori_loop(0, parts, step, 0)
 
-    is_first = lax.axis_index("gy") == 0
-    pl.when(is_first)(functools.partial(run, True))
-    pl.when(jnp.logical_not(is_first))(functools.partial(run, False))
+    each_side(run)
 
     def drain(part, carry):
         for copy in copies(part):
@@ -386,67 +463,62 @@
     lax.fori_loop(0, parts, drain, 0)
 
 
-def x_solve(table, velocity, near, halo, outer, ends, received, partial, z_gradient, gradient, parts=12):
+def x_solve(table, velocity, near, halo, outer, ends, received, own, partial, lines, side, z_gradient, gradient, share=16):
     _, n, ny, nz = velocity.shape
     return pl.pallas_call(
         functools.partial(x_solve_kernel, n, ny),
-        in_specs=[WHOLE] * 9 + [ANY],
+        in_specs=[WHOLE] * 12 + [ANY],
         out_specs=[ANY, ANY],
         out_shape=[layer_shape(*gradient.shape), layer_shape(3, n, ny, nz)],
         scratch_shapes=[
             pltpu.VMEM((3, n, ny, nz), F32),
             pltpu.VMEM((3, n, ny, nz), F32),
-            pltpu.SemaphoreType.DMA((3, parts)),
+            pltpu.VMEM((n * share, 3 * nz), F32),
+            pltpu.SemaphoreType.DMA((3, ny // share)),
         ],
-        input_output_aliases={9: 0},
+        input_output_aliases={12: 0},
         compiler_params=params(),
-        cost_estimate=cost(velocity, 5),
+        cost_estimate=cost(SHORT),
         name="x_solve",
-    )(table, velocity, near, halo, outer, ends, received, partial, z_gradient, gradient)
-
-
-def y_kernel(n, inv_ref, m_ref, v_ref, part_ref, after_ref, g_ref, c_ref, high_ref, low_ref):
-    ny = inv_ref.shape[0]
-    nz = v_ref.shape[3]
-    row = lax.broadcasted_iota(jnp.int32, (ny, ny), 0)
-    column = lax.broadcasted_iota(jnp.int32, (ny, ny), 1)
-    metric = jnp.sum(jnp.where(row == column, m_ref[...], 0.0), axis=1, keepdims=True)
-    high, low = split(times_stencil(inv_ref[...]) * metric)
-    high_ref[...] = high
-    low_ref[...] = low
-
+    )(table, velocity, near, halo, outer, ends, received, own, partial, lines, side, z_gradient, gradient)
+
+
+def y_plane(velocities, high_ref, low_ref):
+    fields = six(velocities, 1)
+    nz = fields[0].shape[1]
+    values = []
+    for a in (0, 2, 4):
+        high, low = split(jnp.concatenate(fields[a : a + 2], axis=1))
+        result = dot(high_ref[...], high) + dot(low_ref[...], high) + dot(high_ref[...], low)
+        values = values + [result[:, :nz], result[:, nz:]]
+    return values
+
+
+def y_kernel(n, high_ref, low_ref, v_ref, held_ref, part_ref, after_ref, g_ref, c_ref):
     def step(group, carry):
-        for u in range(GROUP):
+        for u in range(EARLY, GROUP):
             p = group * GROUP + u
-            fields = six([v_ref[i, p] for i in range(3)], 1)
-            for a in (0, 2, 4):
-                high, low = split(jnp.concatenate(fields[a : a + 2], axis=1))
-                result = dot(high_ref[...], high) + dot(low_ref[...], high) + dot(high_ref[...], low)
-                for j in range(2):
-                    f = a + j
-                    value = result[:, j * nz : (j + 1) * nz]
-                    if f < 3:
-                        g_ref[f, p] = value
-                    else:
-                        c_ref[f - 3, p] = value + part_ref[f - 3, p]
+            values = y_plane([v_ref[i, p] for i in range(3)], high_ref, low_ref)
+            for f in range(3):
+                g_ref[f, p] = values[f]
+                c_ref[f, p] = values[3 + f] + part_ref[f, p]
         return carry
 
     lax.fori_loop(0, n // GROUP, step, 0)
 
 
-def y_solve(y_inverse, metric, velocity, partial, after):
+def y_solve(high, low, velocity, early, partial, after):
     _, n, ny, nz = velocity.shape
     return pl.pallas_call(
         functools.partial(y_kernel, n),
-        in_specs=[WHOLE] * 4 + [ANY],
+        in_specs=[WHOLE] * 5 + [ANY],
         out_specs=[WHOLE, WHOLE],
         out_shape=[in_vmem(3, n, ny, nz), in_vmem(3, n, ny, nz)],
-        scratch_shapes=[pltpu.VMEM((ny, ny), BF16), pltpu.VMEM((ny, ny), BF16)],
-        input_output_aliases={3: 1},
+        input_output_aliases={3: 0, 4: 1},
         compiler_params=params(),
-        cost_estimate=cost(velocity, Y_COST),
+        cost_estimate=cost(LONG),
         name="y_solve",
-    )(y_inverse, metric, velocity, partial, after)
+    )(high, low, velocity, early, partial, after)
 
 
 LINES = 128
@@ -454,13 +526,11 @@
 
 
 def z_own_kernel(
-    n, inv_ref, m_ref, v_ref, after_ref, g_ref, c_ref, right_ref, left_ref, far_ref, main_ref, turned_ref
+    n, inv_ref, m_ref, main_ref, high_ref, low_ref, v_ref, after_ref,
+    g_ref, c_ref, y_ref, right_ref, left_ref, far_ref, turned_ref,
 ):
     nz = inv_ref.shape[0]
     ny = v_ref.shape[2]
-    high, low = split(times_stencil(inv_ref[...]).T * m_ref[...])
-    both = jnp.concatenate([high, low], axis=1)
-    main_ref[...] = jnp.concatenate([both, both], axis=0)
     first_scale = 1.0 / m_ref[0:1, 0:1]
     last_scale = 1.0 / m_ref[0:1, nz - 1 : nz]
     lane = lax.broadcasted_iota(jnp.int32, (ny, nz), 1)
@@ -486,6 +556,11 @@
             p = group * GROUP + u
             velocities = [v_ref[i, p] for i in range(3)]
             values = []
+            y_values = [None] * 6
+            if u < EARLY:
+                y_values = y_plane(velocities, high_ref, low_ref)
+                for f in range(3):
+                    y_ref[f, p] = y_values[f]
             for f, field in enumerate(six(velocities, 2)):
                 high, low = split(field)
                 both = dot(jnp.concatenate([high, low], axis=1), main_ref[...])
@@ -493,7 +568,7 @@
                 if f < 3:
                     g_ref[f, p] = value
                 else:
-                    c_ref[f - 3, p] = value
+                    c_ref[f - 3, p] = value if u >= EARLY else value + y_values[f]
                 values.append(value)
             for block, start, stop in segments(u):
                 base = block % PACK * 32
@@ -531,22 +606,19 @@
     lax.fori_loop(0, n // GROUP, step, 0)
 
 
-def z_own(z_inverse, metric, velocity, after):
+def z_own(z_inverse, metric, main, high, low, velocity, after):
     _, n, ny, nz = velocity.shape
     return pl.pallas_call(
         functools.partial(z_own_kernel, n),
-        in_specs=[WHOLE, WHOLE, WHOLE, ANY],
-        out_specs=[WHOLE] * 5,
-        out_shape=[in_vmem(3, n, ny, nz)] * 2 + [layer_shape(13, n * ny // LINES, LINES)] * 2
+        in_specs=[WHOLE] * 6 + [ANY],
+        out_specs=[WHOLE] * 6,
+        out_shape=[in_vmem(3, n, ny, nz)] * 3 + [layer_shape(13, n * ny // LINES, LINES)] * 2
         + [layer_shape(12, n * ny // LINES, LINES)],
-        scratch_shapes=[
-            pltpu.VMEM((2 * nz, 2 * nz), BF16),
-            pltpu.VMEM((GROUP * ny // LINES // PACK, LINES, LINES), F32),
-        ],
+        scratch_shapes=[pltpu.VMEM((GROUP * ny // LINES // PACK, LINES, LINES), F32)],
         compiler_params=params(),
-        cost_estimate=cost(velocity, 3),
+        cost_estimate=cost(SHORT),
         name="z_own",
-    )(z_inverse, metric, velocity, after)
+    )(z_inverse, metric, main, high, low, velocity, after)
 
 
 def z_side(own_right, own_left, left, right, left_2, right_2, out_ref):
@@ -603,13 +675,11 @@
 
 
 def z_gradient_kernel(
-    n, inv_ref, m_ref, g_ref, own_right_ref, own_left_ref, left_ref, right_ref, left_2_ref, right_2_ref, y_ref,
-    gradient_ref, out_ref, lines_ref, side_ref, beside_ref, sem,
+    n, inv_ref, m_ref, g_ref, own_right_ref, own_left_ref, left_ref, right_ref, left_2_ref, right_2_ref,
+    after_ref, out_ref, lines_ref, side_ref, beside_ref,
 ):
     nz = inv_ref.shape[0]
     ny = g_ref.shape[2]
-    y_copy = pltpu.make_async_copy(y_ref, gradient_ref.at[:, 1], sem)
-    y_copy.start()
     columns = inv_ref[...].T * m_ref[...]
     index = lax.broadcasted_iota(jnp.int32, (32, nz), 0)
     kind = index // 8
@@ -621,7 +691,8 @@
     wide = jnp.concatenate([jnp.where(index % 8 == f, picked, 0.0) for f in range(6)], axis=1)
     high, low = split(wide)
     side_ref[...] = jnp.concatenate([high, high, low], axis=0)
-    blocks = GROUP * ny // LINES
+    planes = GROUP
+    blocks = planes * ny // LINES
     all_blocks = n * ny // LINES
     z_side(own_right_ref, own_left_ref, left_ref, right_ref, left_2_ref, right_2_ref, beside_ref)
 
@@ -631,69 +702,38 @@
             beside = beside_ref[pl.ds(group * blocks + j, 32, stride=all_blocks), :]
             high, low = split(beside.T)
             sides.append(jnp.concatenate([high, low, high], axis=1))
-        for pair in range(GROUP // 2):
-            half = blocks // (GROUP // 2)
+        for pair in range(planes // 2):
+            half = blocks // (planes // 2)
             lines = jnp.concatenate(sides[pair * half : (pair + 1) * half], axis=0)
-            lines_ref[group * (GROUP // 2) + pair] = lines
+            for u in range(2):
+                lines_ref[group * planes + 2 * pair + u] = lines[u * ny : (u + 1) * ny]
             for f in range(0, 3):
                 added = dot(lines, side_ref[:, f * nz : (f + 1) * nz])
                 for u in range(2):
-                    p = group * GROUP + 2 * pair + u
+                    p = group * planes + 2 * pair + u
                     out_ref[f, p] = added[u * ny : (u + 1) * ny] + g_ref[f, p]
         return carry
 
-    lax.fori_loop(0, n // GROUP, step, 0)
-    y_copy.wait()
-
-
-def z_gradient_join(z_inverse, metric, own, lines, y_gradient):
+    lax.fori_loop(0, n // planes, step, 0)
+
+
+def z_gradient_join(z_inverse, metric, own, lines, after):
     _, n, ny, nz = own.shape
     return pl.pallas_call(
         functools.partial(z_gradient_kernel, n),
-        in_specs=[WHOLE] * 10,
-        out_specs=[ANY, WHOLE, WHOLE, WHOLE],
+        in_specs=[WHOLE] * 9 + [ANY],
+        out_specs=[WHOLE, WHOLE, WHOLE],
         out_shape=[
-            layer_shape(3, 3, n, ny, nz),
             in_vmem(3, n, ny, nz),
-            pltpu.VMEM((n // 2, 2 * ny, 96), BF16),
+            pltpu.VMEM((n, ny, 96), BF16),
             pltpu.VMEM((96, 6 * nz), BF16),
         ],
-        scratch_shapes=[pltpu.VMEM((32 * (n * ny // LINES), LINES), F32), pltpu.SemaphoreType.DMA],
-        input_output_aliases={2: 1},
+        scratch_shapes=[pltpu.VMEM((32 * (n * ny // LINES), LINES), F32)],
+        input_output_aliases={2: 0},
         compiler_params=params(),
-        cost_estimate=cost(own, Z_COST),
+        cost_estimate=cost(LONG),
         name="z_gradient_join",
-    )(z_inverse, metric, own, *lines, y_gradient)
-
-
-def z_convection_kernel(n, part_ref, lines_ref, side_ref, after_ref, c_ref):
-    _, _, ny, nz = part_ref.shape
-
-    def step(group, carry):
-        for pair in range(GROUP // 2):
-            lines = lines_ref[group * (GROUP // 2) + pair]
-            for f in range(3):
-                added = dot(lines, side_ref[:, (3 + f) * nz : (4 + f) * nz])
-                for u in range(2):
-                    p = group * GROUP + 2 * pair + u
-                    c_ref[f, p] = added[u * ny : (u + 1) * ny] + part_ref[f, p]
-        return carry
-
-    lax.fori_loop(0, n // GROUP, step, 0)
-
-
-def z_convection_join(partial, lines, side, after):
-    _, n, ny, nz = partial.shape
-    return pl.pallas_call(
-        functools.partial(z_convection_kernel, n),
-        in_specs=[WHOLE] * 3 + [ANY],
-        out_specs=WHOLE,
-        out_shape=in_vmem(3, n, ny, nz),
-        input_output_aliases={0: 0},
-        compiler_params=params(),
-        cost_estimate=cost(partial, Z_COST),
-        name="z_convection_join",
-    )(partial, lines, side, after)
+    )(z_inverse, metric, own, *lines, after)
 
 
 def on_device(mesh, velocity, metric_x, metric_y, metric_z, x_inverse, y_inverse, z_inverse):
@@ -711,14 +751,16 @@
     near = lax.ppermute(own, ("gx", "gy"), across)
     halo = lax.ppermute(inner, "gy", beside)
     held = pltpu.with_memory_space_constraint(velocity, pltpu.VMEM)
-    table, y_inverse, metric_y, z_inverse, metric_z = tables(
+    table, y_high, y_low, z_main, z_inverse, metric_z = tables(
         x_inverse, metric_x[None], y_inverse, metric_y[None], z_inverse, metric_z[None], own
     )
 
     x_sent, x_partial = x_ends(table, held, halo)
     x_received = lax.ppermute(x_sent, ("gx", "gy"), across)
 
-    z_gradient, convection, to_right, to_left, to_far = z_own(z_inverse, metric_z, held, x_sent)
+    z_gradient, convection, y_gradient, to_right, to_left, to_far = z_own(
+        z_inverse, metric_z, z_main, y_high, y_low, held, x_sent
+    )
     left_far = lax.ppermute(to_far, "gz", shift(2))
     right_far = left_far if shift(2) == shift(-2) else lax.ppermute(to_far, "gz", shift(-2))
     z_lines = (
@@ -730,14 +772,15 @@
         right_far,
     )
 
-    y_gradient, convection = y_solve(y_inverse, metric_y, held, convection, near)
-    gradient, z_gradient, lines, side = z_gradient_join(z_inverse, metric_z, z_gradient, z_lines, y_gradient)
-    outer, x_end = x_face(table, x_received, x_sent, x_partial, own, near, z_gradient, n)
+    y_gradient, convection = y_solve(y_high, y_low, held, y_gradient, convection, near)
+    gradient, x_gradient = x_gradient_own(table, held, near, halo, y_gradient)
+    outer, x_end = x_face(table, x_received, x_sent, x_partial, own, near, x_gradient, n)
     x_other = lax.ppermute(x_end, "gy", beside)
-
-    convection = z_convection_join(convection, lines, side, x_end)
+    z_gradient, lines, side = z_gradient_join(z_inverse, metric_z, z_gradient, z_lines, x_end)
     return tuple(
-        x_solve(table, held, near, halo, outer, x_end, x_other, convection, z_gradient, gradient)
+        x_solve(
+            table, held, near, halo, outer, x_end, x_other, x_gradient, convection, lines, side, z_gradient, gradient
+        )
     )
 
 

time: 36.6 us -> 35.7 us (0.975)
  starting transfers between devices: 10.4 us -> 9.83 us
    ppermute x1, waiting for transfers between devices: 0.98 us -> 0.01 us  [on_device(): x_other = lax.ppermute(x_end, 'gy', beside)]
    pallas_call x1, Pallas kernels: 1.06 us -> 1.83 us  [tables(): pl.pallas_call(functools.partial(tables_kernel, n), in_specs=[ANY] * 7, o...]
    ppermute x1, waiting for transfers between devices: 0.01 us -> 0.77 us  [on_device(): x_received = lax.ppermute(x_sent, ('gx', 'gy'), across)]
    ppermute x1, starting transfers between devices: 0.52 us -> 0.01 us  [on_device(): halo = lax.ppermute(inner, 'gy', beside)]
    pallas_call x3, Pallas kernels: 11.1 us -> 10.6 us  [the longest x1 5.34 us: z_own(): pl.pallas_call(functools.partial(z_own_kernel, n), in_specs=[WHOLE] * 6 +...]
  transfers between devices with their start and end apart: 7 -> 7, of which waited for: 1 -> 2; matrix products, arithmetic and copies ran while one was open for 0% -> 0% of each run, Pallas kernels for 45% -> 48%
where the time goes in v3:
time: 35.7 us; the launch traced here: 35.6 us
  Pallas kernels  24.1 us (68%)
  starting transfers between devices  9.83 us (28%)
  waiting for transfers between devices  0.94 us (3%)
  between operations  0.74 us (2%)
    pallas_call x1, Pallas kernels, x_solve(): pl.pallas_call(functools.partial(x_solve_kernel, n, ny), in_specs=[WHOLE]...  5.43 us
    pallas_call x1, Pallas kernels, z_own(): pl.pallas_call(functools.partial(z_own_kernel, n), in_specs=[WHOLE] * 6 +...  5.34 us
    ppermute x1, starting transfers between devices, on_device(): near = lax.ppermute(own, ('gx', 'gy'), across)  4.55 us
    pallas_call x1, Pallas kernels, y_solve(): pl.pallas_call(functools.partial(y_kernel, n), in_specs=[WHOLE] * 5 + [AN...  2.93 us
    pallas_call x1, Pallas kernels, x_gradient_own(): pl.pallas_call(functools.partial(x_gradient_kernel, n, ny), in_specs=[WHO...  2.37 us
    pallas_call x1, Pallas kernels, x_ends(): pl.pallas_call(functools.partial(x_ends_kernel, n, ny), in_specs=[WHOLE]...  2.17 us
    pallas_call x1, Pallas kernels, z_gradient_join(): pl.pallas_call(functools.partial(z_gradient_kernel, n), in_specs=[WHOLE]...  2.06 us
    pallas_call x1, Pallas kernels, tables(): pl.pallas_call(functools.partial(tables_kernel, n), in_specs=[ANY] * 7, o...  1.83 us
  transfers between devices with their start and end apart: 7, of which 2 were waited for; matrix products, arithmetic and copies ran while one was open for 0% of the time, Pallas kernels for 48%

profile of v3, /device:TPU:0, one launch (start us, length us, event | category | flops | bytes accessed | tf_op | source)
XLA Modules:
  0.0 35.6 jit_solution(9220004946583337717)
XLA Ops:
  0.6 0.0 slice-start
  0.6 1.5 %prepare.1 = (f32[3,192,128]{2,1,0:T(8,128)S(1)}, f32[3,2,192,128]{3,2,1,0:T(8,128)S(1)}) custom-call(f32[3,16,192,128]{3,2,1,0:T(8,128)} %v_ref.11), custom_call_target="tpu_custom_call" | custom-call | tf_op jit(solution)/shard_map/prepare/pallas_call | solution.py:109
  2.1 4.6 %collective-permute-start = (f32[3,192,128]{2,1,0:T(8,128)S(1)}, f32[3,192,128]{2,1,0:T(8,128)S(1)}, u32[]{:S(2)}, u32[]{:S(2)}) collective-permute-start(f32[3,192,128]{2,1,0:T(8,128)S(1)} %get-tuple-element.27.after_ref.own_ref), channel_id=1, source_target_pairs={{1,8},{9,16},{17,24},{25,0},{8,1},{16,9},{24,17},{0,25},{3,10},{11... | collective-permute-start | bytes 884744 | tf_op jit(solution)/shard_map/ppermute | solution.py:751
  6.7 0.0 collective-permute-start.1
  6.7 0.0 slice-start.1
  6.7 1.8 %tables.1 = (f32[121,8,128]{2,1,0:T(8,128)S(1)}, bf16[192,192]{1,0:T(8,128)(2,1)S(1)}, bf16[192,192]{1,0:T(8,128)(2,1)S(1)}, bf16[256,256]{1,0:T(8,128)(2,1)S(1)...) custom-call(f32[16,16]{1,0:T(8,128)} %xi_ref.1, f32[1,16]{1,0:T(1,128)} %bitcast.6, f32[192,192]{1,0:T(8,128)} %yi_ref.1, ...), custom_call_target="tpu_custom_call" | custom-call | flops 20000000000 | bytes 1 | tf_op jit(solution)/shard_map/tables/pallas_call | solution.py:215
  8.5 0.2 collective-permute-done.1.halo_ref
  8.7 0.0 slice-done
  8.7 0.0 slice-done.1
  8.7 2.2 %x_ends.1 = (f32[1160,128]{1,0:T(8,128)S(1)}, f32[6,192,128]{2,1,0:T(8,128)S(1)}) custom-call(f32[121,8,128]{2,1,0:T(8,128)S(1)} %get-tuple-element.28.table_ref, f32[3,16,192,128]{3,2,1,0:T(8,128)S(1)} %bitcast.4, f32[3,2,192,128]{3,2,1,0:T(8,128)S(1)} %collective-permute-done.1.halo_ref), custom_call_target="tpu_custom_call" | custom-call | flops 4 | bytes 1 | tf_op jit(solution)/shard_map/x_ends/pallas_call | solution.py:269
  10.9 0.7 %collective-permute-start.2 = (f32[1160,128]{1,0:T(8,128)S(1)}, f32[1160,128]{1,0:T(8,128)S(1)}, u32[]{:S(2)}, u32[]{:S(2)}) collective-permute-start(f32[1160,128]{1,0:T(8,128)S(1)} %get-tuple-element.30.after_ref.ws_ref), channel_id=1, source_target_pairs={{1,8},{9,16},{17,24},{25,0},{8,1},{16,9},{24,17},{0,25},{3,10},{11... | collective-permute-start | bytes 1781768 | tf_op jit(solution)/shard_map/ppermute | solution.py:759
  11.6 5.3 %z_own.1 = (f32[3,16,192,128]{3,2,1,0:T(8,128)S(1)}, f32[3,16,192,128]{3,2,1,0:T(8,128)S(1)}, f32[3,16,192,128]{3,2,1,0:T(8,128)S(1)}, f32[13,24,128]{2,1,0:T(8,...) custom-call(f32[128,128]{1,0:T(8,128)S(1)} %get-tuple-element.34.inv_ref, ...), custom_call_target="tpu_custom_call" | custom-call | flops 4 | bytes 1 | tf_op jit(solution)/shard_map/z_own/pallas_call | solution.py:611
  16.9 1.6 %collective-permute-start.6 = (f32[12,24,128]{2,1,0:T(8,128)S(1)}, f32[12,24,128]{2,1,0:T(8,128)S(1)}, u32[]{:S(2)}, u32[]{:S(2)}) collective-permute-start(f32[12,24,128]{2,1,0:T(8,128)S(1)} %get-tuple-element.47), channel_id=1, source_target_pairs={{0,4},{2,6},{4,0},{6,2},{1,5},{3,7},{5,1},{7,3},{8,12},{10,14},{12... | collective-permute-start | bytes 442376 | tf_op jit(solution)/shard_map/ppermute | solution.py:764
  18.5 1.5 %collective-permute-start.4 = (f32[13,24,128]{2,1,0:T(8,128)S(1)}, f32[13,24,128]{2,1,0:T(8,128)S(1)}, u32[]{:S(2)}, u32[]{:S(2)}) collective-permute-start(f32[13,24,128]{2,1,0:T(8,128)S(1)} %get-tuple-element.45.own_right_ref), channel_id=1, source_target_pairs={{0,2},{2,4},{4,6},{6,0},{1,3},{3,5},{5,7},{7,1},{8,10},{10,12},{12... | collective-permute-start | bytes 479240 | tf_op jit(solution)/shard_map/ppermute | solution.py:769
  20.0 1.4 %collective-permute-start.5 = (f32[13,24,128]{2,1,0:T(8,128)S(1)}, f32[13,24,128]{2,1,0:T(8,128)S(1)}, u32[]{:S(2)}, u32[]{:S(2)}) collective-permute-start(f32[13,24,128]{2,1,0:T(8,128)S(1)} %get-tuple-element.46.own_left_ref), channel_id=1, source_target_pairs={{0,6},{2,0},{4,2},{6,4},{1,7},{3,1},{5,3},{7,5},{8,14},{10,8},{12,... | collective-permute-start | bytes 479240 | tf_op jit(solution)/shard_map/ppermute | solution.py:770
  21.4 0.0 collective-permute-done.after_ref.near_ref
  21.4 2.9 %y_solve.1 = (f32[3,16,192,128]{3,2,1,0:T(8,128)S(1)}, f32[3,16,192,128]{3,2,1,0:T(8,128)S(1)}) custom-call(bf16[192,192]{1,0:T(8,128)(2,1)S(1)} %get-tuple-element.32.high_ref, bf16[192,192]{1,0:T(8,128)(2,1)S(1)} %get-tuple-element.33.low_ref, f32[3,16,192,128]{3,2,1,0:T(8,128)S(1)} %bitcast.4, ...), custom_call_target="tpu_custom_call", output_to_operand_aliasing={{0}: (3, {}), {1}: (4, {})} | custom-call | flops 20000000000 | bytes 1 | tf_op jit(solution)/shard_map/y_solve/pallas_call | solution.py:512
  24.4 2.4 %x_gradient_own.1 = (f32[3,3,16,192,128]{4,3,2,1,0:T(8,128)}, f32[3,16,192,128]{3,2,1,0:T(8,128)S(1)}) custom-call(f32[121,8,128]{2,1,0:T(8,128)S(1)} %get-tuple-element.28.table_ref, f32[3,16,192,128]{3,2,1,0:T(8,128)S(1)} %bitcast.4, f32[3,192,128]{2,1,0:T(8,128)S(1)} %collective-permute-done.after_ref.near_ref, ...), custom_call_target="tpu_custom_call" | custom-call | flops 4 | bytes 1 | tf_op jit(solution)/shard_map/x_gradient_own/pallas_call | solution.py:382
  26.7 0.8 %collective-permute-done.2.wr_ref = f32[1160,128]{1,0:T(8,128)S(1)} collective-permute-done((f32[1160,128]{1,0:T(8,128)S(1)}, f32[1160,128]{1,0:T(8,128)S(1)}, u32[]{:S(2)}, u32[]{:S(2)}) %collective-permute-start.2) | collective-permute-done | bytes 593952 | tf_op jit(solution)/shard_map/ppermute | solution.py:759
  27.5 0.5 %x_face.1 = (f32[6,192,128]{2,1,0:T(8,128)S(1)}, f32[1160,128]{1,0:T(8,128)S(1)}) custom-call(f32[121,8,128]{2,1,0:T(8,128)S(1)} %get-tuple-element.28.table_ref, f32[1160,128]{1,0:T(8,128)S(1)} %collective-permute-done.2.wr_ref, f32[1160,128]{1,0:T(8,128)S(1)} %get-tuple-element.30.after_ref.ws_ref, f32[6,192,128]{2,1,0:T(8,128)S(1)} %get-tuple-element.31.l_ref, ...), custom_call_target="tpu_custom_call" | custom-call | flops 4 | bytes 1 | tf_op jit(solution)/shard_map/x_face/pallas_call | solution.py:312
  28.0 0.1 collective-permute-start.3
  28.1 0.0 collective-permute-done.6.left_2_ref.right_2_ref
  28.1 0.0 collective-permute-done.4.left_ref
  28.1 0.0 collective-permute-done.5.right_ref
  28.1 2.1 %z_gradient_join.1 = (f32[3,16,192,128]{3,2,1,0:T(8,128)S(1)}, bf16[16,192,96]{2,1,0:T(8,128)(2,1)S(1)}, bf16[96,768]{1,0:T(8,128)(2,1)S(1)}) custom-call(f32[128,128]{1,0:T(8,128)S(1)} %get-tuple-element.34.inv_ref, f32[1,128]{1,0:T(1,128)S(1)} %get-tuple-element.35.m_ref, ...), custom_call_target="tpu_custom_call", output_to_operand_aliasing={{0}: (2, {})} | custom-call | flops 20000000000 | bytes 1 | tf_op jit(solution)/shard_map/z_gradient_join/pallas_call | solution.py:722
  30.2 0.0 collective-permute-done.3.r_ref
  30.2 5.4 %x_solve.1 = (f32[3,3,16,192,128]{4,3,2,1,0:T(8,128)}, f32[3,16,192,128]{3,2,1,0:T(8,128)}) custom-call(f32[121,8,128]{2,1,0:T(8,128)S(1)} %get-tuple-element.28.table_ref, f32[3,16,192,128]{3,2,1,0:T(8,128)S(1)} %bitcast.4, f32[3,192,128]{2,1,0:T(8,128)S(1)} %collective-permute-done.after_ref.near_ref, ...), custom_call_target="tpu_custom_call", output_to_operand_aliasing={{0}: (12, {})} | custom-call | flops 4 | bytes 1 | tf_op jit(solution)/shard_map/x_solve/pallas_call | solution.py:468
  (1 shorter events, 0.0 us)
Async XLA Ops:
  0.6 8.1 %slice-start = ((s8[4718592]{0:T(1024)(128)(4,1)}), s8[4194304]{0:T(1024)(128)(4,1)S(1)}, s32[]{:S(2)}) async-start(s8[4718592]{0:T(1024)(128)(4,1)} %bitcast.3), calls=%async_computation | async-start | bytes 8388608
  2.1 19.3 %collective-permute-start = (f32[3,192,128]{2,1,0:T(8,128)S(1)}, f32[3,192,128]{2,1,0:T(8,128)S(1)}, u32[]{:S(2)}, u32[]{:S(2)}) collective-permute-start(f32[3,192,128]{2,1,0:T(8,128)S(1)} %get-tuple-element.27.after_ref.own_ref), channel_id=1, source_target_pairs={{1,8},{9,16},{17,24},{25,0},{8,1},{16,9},{24,17},{0,25},{3,10},{11... | collective-permute-start | bytes 884744 | tf_op jit(solution)/shard_map/ppermute | solution.py:751
  6.7 2.0 %collective-permute-start.1 = (f32[3,2,192,128]{3,2,1,0:T(8,128)S(1)}, f32[3,2,192,128]{3,2,1,0:T(8,128)S(1)}, u32[]{:S(2)}, u32[]{:S(2)}) collective-permute-start(f32[3,2,192,128]{3,2,1,0:T(8,128)S(1)} %get-tuple-element.29), channel_id=1, source_target_pairs={{0,1},{1,0},{2,3},{3,2},{4,5},{5,4},{6,7},{7,6},{8,9},{9,8},{10,11... | collective-permute-start | bytes 1769480 | tf_op jit(solution)/shard_map/ppermute | solution.py:752
  6.7 2.0 %slice-start.1 = ((s8[4718592]{0:T(1024)(128)(4,1)}), s8[524288]{0:T(1024)(128)(4,1)S(1)}, s32[]{:S(2)}) async-start(s8[4718592]{0:T(1024)(128)(4,1)} %bitcast.3), calls=%async_computation.1 | async-start | bytes 1048576
  10.9 16.6 %collective-permute-start.2 = (f32[1160,128]{1,0:T(8,128)S(1)}, f32[1160,128]{1,0:T(8,128)S(1)}, u32[]{:S(2)}, u32[]{:S(2)}) collective-permute-start(f32[1160,128]{1,0:T(8,128)S(1)} %get-tuple-element.30.after_ref.ws_ref), channel_id=1, source_target_pairs={{1,8},{9,16},{17,24},{25,0},{8,1},{16,9},{24,17},{0,25},{3,10},{11... | collective-permute-start | bytes 1781768 | tf_op jit(solution)/shard_map/ppermute | solution.py:759
  16.9 11.2 %collective-permute-start.6 = (f32[12,24,128]{2,1,0:T(8,128)S(1)}, f32[12,24,128]{2,1,0:T(8,128)S(1)}, u32[]{:S(2)}, u32[]{:S(2)}) collective-permute-start(f32[12,24,128]{2,1,0:T(8,128)S(1)} %get-tuple-element.47), channel_id=1, source_target_pairs={{0,4},{2,6},{4,0},{6,2},{1,5},{3,7},{5,1},{7,3},{8,12},{10,14},{12... | collective-permute-start | bytes 442376 | tf_op jit(solution)/shard_map/ppermute | solution.py:764
  18.5 9.6 %collective-permute-start.4 = (f32[13,24,128]{2,1,0:T(8,128)S(1)}, f32[13,24,128]{2,1,0:T(8,128)S(1)}, u32[]{:S(2)}, u32[]{:S(2)}) collective-permute-start(f32[13,24,128]{2,1,0:T(8,128)S(1)} %get-tuple-element.45.own_right_ref), channel_id=1, source_target_pairs={{0,2},{2,4},{4,6},{6,0},{1,3},{3,5},{5,7},{7,1},{8,10},{10,12},{12... | collective-permute-start | bytes 479240 | tf_op jit(solution)/shard_map/ppermute | solution.py:769
  20.0 8.1 %collective-permute-start.5 = (f32[13,24,128]{2,1,0:T(8,128)S(1)}, f32[13,24,128]{2,1,0:T(8,128)S(1)}, u32[]{:S(2)}, u32[]{:S(2)}) collective-permute-start(f32[13,24,128]{2,1,0:T(8,128)S(1)} %get-tuple-element.46.own_left_ref), channel_id=1, source_target_pairs={{0,6},{2,0},{4,2},{6,4},{1,7},{3,1},{5,3},{7,5},{8,14},{10,8},{12,... | collective-permute-start | bytes 479240 | tf_op jit(solution)/shard_map/ppermute | solution.py:770
  28.0 2.2 %collective-permute-start.3 = (f32[1160,128]{1,0:T(8,128)S(1)}, f32[1160,128]{1,0:T(8,128)S(1)}, u32[]{:S(2)}, u32[]{:S(2)}) collective-permute-start(f32[1160,128]{1,0:T(8,128)S(1)} %get-tuple-element.42.after_ref.e_ref), channel_id=1, source_target_pairs={{0,1},{1,0},{2,3},{3,2},{4,5},{5,4},{6,7},{7,6},{8,9},{9,8},{10,11... | collective-permute-start | bytes 1781768 | tf_op jit(solution)/shard_map/ppermute | solution.py:778

commit v4 on v3

--- a/solution.py
+++ b/solution.py
@@ -15,7 +15,7 @@
 SMEM = pltpu.SMEM
 VMEM_LIMIT = 20 * 1024 * 1024
 GROUP = 8
-EARLY = 3
+EARLY = 4
 SHORT, LONG = 4, 20_000_000_000
 
 
@@ -119,7 +119,7 @@
 
 def tables_kernel(
     n, xi_ref, mx_ref, yi_ref, my_ref, zi_ref, mz_ref, after_ref,
-    table_ref, y_high_ref, y_low_ref, z_main_ref, z_ref, z_metric_ref, x_ref, m_ref, y_ref, y_metric_ref, sem,
+    table_ref, y_ref, y_metric_ref, z_ref, z_metric_ref, x_ref, m_ref, sem,
 ):
     ends = Ends(n)
     nz = table_ref.shape[2]
@@ -199,14 +199,6 @@
     table_ref[table.qq] = jnp.where(first, inner[n - 1], inner[0])
     for copy in copies:
         copy.wait()
-    ny = y_ref.shape[0]
-    row = lax.broadcasted_iota(jnp.int32, (ny, ny), 0)
-    column = lax.broadcasted_iota(jnp.int32, (ny, ny), 1)
-    y_metric = jnp.sum(jnp.where(row == column, y_metric_ref[...], 0.0), axis=1, keepdims=True)
-    y_high_ref[...], y_low_ref[...] = split(times_stencil(y_ref[...]) * y_metric)
-    high, low = split(times_stencil(z_ref[...]).T * z_metric_ref[...])
-    both = jnp.concatenate([high, low], axis=1)
-    z_main_ref[...] = jnp.concatenate([both, both], axis=0)
 
 
 def tables(x_inverse, metric_x, y_inverse, metric_y, z_inverse, metric_z, after):
@@ -215,22 +207,15 @@
     return pl.pallas_call(
         functools.partial(tables_kernel, n),
         in_specs=[ANY] * 7,
-        out_specs=[WHOLE] * 6,
+        out_specs=[WHOLE] * 5,
         out_shape=[
             in_vmem(Table(n).size, 8, nz),
-            pltpu.VMEM((ny, ny), BF16),
-            pltpu.VMEM((ny, ny), BF16),
-            pltpu.VMEM((2 * nz, 2 * nz), BF16),
+            in_vmem(ny, ny),
+            in_vmem(1, ny),
             in_vmem(nz, nz),
             in_vmem(1, nz),
         ],
-        scratch_shapes=[
-            pltpu.VMEM((n, n), F32),
-            pltpu.VMEM((1, n), F32),
-            pltpu.VMEM((ny, ny), F32),
-            pltpu.VMEM((1, ny), F32),
-            pltpu.SemaphoreType.DMA((6,)),
-        ],
+        scratch_shapes=[pltpu.VMEM((n, n), F32), pltpu.VMEM((1, n), F32), pltpu.SemaphoreType.DMA((6,))],
         compiler_params=params(),
         cost_estimate=cost(LONG),
         name="tables",
@@ -420,24 +405,28 @@
             base = pl.multiple_of(part * share, 16)
             lines = lines_ref[:, pl.ds(base, share), :].reshape(n * share, lines_ref.shape[2])
             beside_ref[...] = dot(lines, side_ref[:, 3 * nz :])
+            def inner_end(f, start):
+                field = pl.ds(f * ny + start, 8)
+                return scale * (r_ref[field, :] - weight * e_ref[field, :])
+
+            added = []
+            for offset in range(0, share, 8):
+                rows = pl.ds(base + offset, 8)
+                for f in range(3):
+                    added.append((f, rows, w_ref[f, rows, :], inner_end(f, base + offset)))
+            for k in range(n):
+                a, b = table_ref[table.outer + k], table_ref[table.inner + k]
+                for f, rows, outer, inner in added:
+                    g_ref[f, k, rows, :] = own_ref[f, k, rows, :] + a * outer + b * inner
             for offset in range(0, share, 8):
                 start = base + offset
                 rows = pl.ds(start, 8)
                 near = six([near_ref[i, rows, :] for i in range(3)], 0)
                 inner_near = six([halo_ref[i, near_j, rows, :] for i in range(3)], 0)
                 inner_far = six([halo_ref[i, far_j, rows, :] for i in range(3)], 0)
-                for f in range(6):
-                    field = pl.ds(f * ny + start, 8)
+                for f in range(3, 6):
                     outer = w_ref[f, rows, :]
-                    inner = scale * (r_ref[field, :] - weight * e_ref[field, :])
-                    if f < 3:
-                        for k in range(n):
-                            g_ref[f, k, rows, :] = (
-                                own_ref[f, k, rows, :]
-                                + table_ref[table.outer + k] * outer
-                                + table_ref[table.inner + k] * inner
-                            )
-                        continue
+                    inner = inner_end(f, start)
                     line = [v_ref[f - 3, k, rows, :] * v_ref[0, k, rows, :] for k in range(n)]
                     inner = inner - sign * (28.0 * inner_near[f] + inner_far[f])
                     ends = (outer, sign * near[f], -sign * inner_near[f], inner)
@@ -526,11 +515,18 @@
 
 
 def z_own_kernel(
-    n, inv_ref, m_ref, main_ref, high_ref, low_ref, v_ref, after_ref,
-    g_ref, c_ref, y_ref, right_ref, left_ref, far_ref, turned_ref,
+    n, y_inv_ref, y_m_ref, inv_ref, m_ref, v_ref, after_ref,
+    g_ref, c_ref, y_ref, high_ref, low_ref, right_ref, left_ref, far_ref, main_ref, turned_ref,
 ):
     nz = inv_ref.shape[0]
     ny = v_ref.shape[2]
+    row = lax.broadcasted_iota(jnp.int32, (ny, ny), 0)
+    column = lax.broadcasted_iota(jnp.int32, (ny, ny), 1)
+    y_metric = jnp.sum(jnp.where(row == column, y_m_ref[...], 0.0), axis=1, keepdims=True)
+    high_ref[...], low_ref[...] = split(times_stencil(y_inv_ref[...]) * y_metric)
+    high, low = split(times_stencil(inv_ref[...]).T * m_ref[...])
+    both = jnp.concatenate([high, low], axis=1)
+    main_ref[...] = jnp.concatenate([both, both], axis=0)
     first_scale = 1.0 / m_ref[0:1, 0:1]
     last_scale = 1.0 / m_ref[0:1, nz - 1 : nz]
     lane = lax.broadcasted_iota(jnp.int32, (ny, nz), 1)
@@ -586,7 +582,7 @@
                 for other in range(1, PACK):
                     columns = jnp.concatenate(pieces[j + other], axis=0)
                     packed = jnp.where(lane[0:LINES] // 32 == other, columns, packed)
-                turned_ref[j // PACK] = packed.T
+                turned_ref[j // PACK, 0:LINES, :] = packed.T
                 blocks = pl.ds(group * len(pieces) + j, PACK)
 
                 def rows(position):
@@ -606,19 +602,24 @@
     lax.fori_loop(0, n // GROUP, step, 0)
 
 
-def z_own(z_inverse, metric, main, high, low, velocity, after):
+def z_own(y_inverse, y_metric, z_inverse, metric, velocity, after):
     _, n, ny, nz = velocity.shape
     return pl.pallas_call(
         functools.partial(z_own_kernel, n),
-        in_specs=[WHOLE] * 6 + [ANY],
-        out_specs=[WHOLE] * 6,
-        out_shape=[in_vmem(3, n, ny, nz)] * 3 + [layer_shape(13, n * ny // LINES, LINES)] * 2
+        in_specs=[WHOLE] * 5 + [ANY],
+        out_specs=[WHOLE] * 8,
+        out_shape=[in_vmem(3, n, ny, nz)] * 3
+        + [pltpu.VMEM((ny, ny), BF16)] * 2
+        + [layer_shape(13, n * ny // LINES, LINES)] * 2
         + [layer_shape(12, n * ny // LINES, LINES)],
-        scratch_shapes=[pltpu.VMEM((GROUP * ny // LINES // PACK, LINES, LINES), F32)],
+        scratch_shapes=[
+            pltpu.VMEM((2 * nz, 2 * nz), BF16),
+            pltpu.VMEM((GROUP * ny // LINES // PACK, LINES + 32, LINES), F32),
+        ],
         compiler_params=params(),
         cost_estimate=cost(SHORT),
         name="z_own",
-    )(z_inverse, metric, main, high, low, velocity, after)
+    )(y_inverse, y_metric, z_inverse, metric, velocity, after)
 
 
 def z_side(own_right, own_left, left, right, left_2, right_2, out_ref):
@@ -728,7 +729,7 @@
             pltpu.VMEM((n, ny, 96), BF16),
             pltpu.VMEM((96, 6 * nz), BF16),
         ],
-        scratch_shapes=[pltpu.VMEM((32 * (n * ny // LINES), LINES), F32)],
+        scratch_shapes=[pltpu.VMEM((33 * (n * ny // LINES), LINES), F32)],
         input_output_aliases={2: 0},
         compiler_params=params(),
         cost_estimate=cost(LONG),
@@ -751,15 +752,15 @@
     near = lax.ppermute(own, ("gx", "gy"), across)
     halo = lax.ppermute(inner, "gy", beside)
     held = pltpu.with_memory_space_constraint(velocity, pltpu.VMEM)
-    table, y_high, y_low, z_main, z_inverse, metric_z = tables(
+    table, y_inverse, metric_y, z_inverse, metric_z = tables(
         x_inverse, metric_x[None], y_inverse, metric_y[None], z_inverse, metric_z[None], own
     )
 
     x_sent, x_partial = x_ends(table, held, halo)
     x_received = lax.ppermute(x_sent, ("gx", "gy"), across)
 
-    z_gradient, convection, y_gradient, to_right, to_left, to_far = z_own(
-        z_inverse, metric_z, z_main, y_high, y_low, held, x_sent
+    z_gradient, convection, y_gradient, y_high, y_low, to_right, to_left, to_far = z_own(
+        y_inverse, metric_y, z_inverse, metric_z, held, x_sent
     )
     left_far = lax.ppermute(to_far, "gz", shift(2))
     right_far = left_far if shift(2) == shift(-2) else lax.ppermute(to_far, "gz", shift(-2))

time: 35.7 us -> 35.7 us (level)
  waiting for transfers between devices: 0.94 us -> 1.42 us
  Pallas kernels: 24.1 us -> 23.7 us
    pallas_call x1, Pallas kernels: 5.34 us -> 6.32 us  [z_own(): pl.pallas_call(functools.partial(z_own_kernel, n), in_specs=[WHOLE] * 5 +...]
    ppermute x1, waiting for transfers between devices: 0.16 us -> 0.87 us  [on_device(): halo = lax.ppermute(inner, 'gy', beside)]
    pallas_call x1, Pallas kernels: 1.83 us -> 1.12 us  [tables(): pl.pallas_call(functools.partial(tables_kernel, n), in_specs=[ANY] * 7, o...]
    pallas_call x1, Pallas kernels: 2.93 us -> 2.38 us  [y_solve(): pl.pallas_call(functools.partial(y_kernel, n), in_specs=[WHOLE] * 5 + [AN...]
  transfers between devices with their start and end apart: 7 -> 7, of which waited for: 2 -> 3; matrix products, arithmetic and copies ran while one was open for 0% -> 0% of each run, Pallas kernels for 48% -> 47%
where the time goes in v4:
time: 35.7 us; the launch traced here: 35.6 us
  Pallas kernels  23.7 us (66%)
  starting transfers between devices  9.7 us (27%)
  waiting for transfers between devices  1.42 us (4%)
  between operations  0.74 us (2%)
    pallas_call x1, Pallas kernels, z_own(): pl.pallas_call(functools.partial(z_own_kernel, n), in_specs=[WHOLE] * 5 +...  6.32 us
    pallas_call x1, Pallas kernels, x_solve(): pl.pallas_call(functools.partial(x_solve_kernel, n, ny), in_specs=[WHOLE]...  5.34 us
    ppermute x1, starting transfers between devices, on_device(): near = lax.ppermute(own, ('gx', 'gy'), across)  4.55 us
    pallas_call x1, Pallas kernels, y_solve(): pl.pallas_call(functools.partial(y_kernel, n), in_specs=[WHOLE] * 5 + [AN...  2.38 us
    pallas_call x1, Pallas kernels, x_gradient_own(): pl.pallas_call(functools.partial(x_gradient_kernel, n, ny), in_specs=[WHO...  2.37 us
    pallas_call x1, Pallas kernels, x_ends(): pl.pallas_call(functools.partial(x_ends_kernel, n, ny), in_specs=[WHOLE]...  2.17 us
    pallas_call x1, Pallas kernels, z_gradient_join(): pl.pallas_call(functools.partial(z_gradient_kernel, n), in_specs=[WHOLE]...  2.06 us
    ppermute x1, starting transfers between devices, on_device(): left_far = lax.ppermute(to_far, 'gz', shift(2))  1.7 us
  transfers between devices with their start and end apart: 7, of which 3 were waited for; matrix products, arithmetic and copies ran while one was open for 0% of the time, Pallas kernels for 47%

profile of v4, /device:TPU:0, one launch (start us, length us, event | category | flops | bytes accessed | tf_op | source)
XLA Modules:
  0.0 35.6 jit_solution(1237397044143551659)
XLA Ops:
  0.6 0.0 slice-start
  0.6 1.5 %prepare.1 = (f32[3,192,128]{2,1,0:T(8,128)S(1)}, f32[3,2,192,128]{3,2,1,0:T(8,128)S(1)}) custom-call(f32[3,16,192,128]{3,2,1,0:T(8,128)} %v_ref.11), custom_call_target="tpu_custom_call" | custom-call | tf_op jit(solution)/shard_map/prepare/pallas_call | solution.py:109
  2.1 4.6 %collective-permute-start = (f32[3,192,128]{2,1,0:T(8,128)S(1)}, f32[3,192,128]{2,1,0:T(8,128)S(1)}, u32[]{:S(2)}, u32[]{:S(2)}) collective-permute-start(f32[3,192,128]{2,1,0:T(8,128)S(1)} %get-tuple-element.28.after_ref.own_ref), channel_id=1, source_target_pairs={{1,8},{9,16},{17,24},{25,0},{8,1},{16,9},{24,17},{0,25},{3,10},{11... | collective-permute-start | bytes 884744 | tf_op jit(solution)/shard_map/ppermute | solution.py:752
  6.7 0.0 collective-permute-start.1
  6.7 0.0 slice-start.1
  6.7 1.1 %tables.1 = (f32[121,8,128]{2,1,0:T(8,128)S(1)}, f32[192,192]{1,0:T(8,128)S(1)}, f32[1,192]{1,0:T(1,128)S(1)}, f32[128,128]{1,0:T(8,128)S(1)}, f32[1,128]{1,0:T(1,128)S(1)}) custom-call(f32[16,16]{1,0:T(8,128)} %xi_ref.1, f32[1,16]{1,0:T(1,128)} %bitcast.6, f32[192,192]{1,0:T(8,128)} %yi_ref.1, f32[1,192]{1,0:T(1,128)} %bitcast.5, f32[128,128]{1,0:T(8,128)} %zi_ref.1, ...), custom_call_target="tpu_custom_call" | custom-call | flops 20000000000 | bytes 1 | tf_op jit(solution)/shard_map/tables/pallas_call | solution.py:207
  7.8 0.9 %collective-permute-done.1.halo_ref = f32[3,2,192,128]{3,2,1,0:T(8,128)S(1)} collective-permute-done((f32[3,2,192,128]{3,2,1,0:T(8,128)S(1)}, f32[3,2,192,128]{3,2,1,0:T(8,128)S(1)}, u32[]{:S(2)}, u32[]{:S(2)}) %collective-permute-start.1) | collective-permute-done | bytes 589856 | tf_op jit(solution)/shard_map/ppermute | solution.py:753
  8.7 0.0 slice-done
  8.7 0.0 slice-done.1
  8.7 2.2 %x_ends.1 = (f32[1160,128]{1,0:T(8,128)S(1)}, f32[6,192,128]{2,1,0:T(8,128)S(1)}) custom-call(f32[121,8,128]{2,1,0:T(8,128)S(1)} %get-tuple-element.29.table_ref, f32[3,16,192,128]{3,2,1,0:T(8,128)S(1)} %bitcast.4, f32[3,2,192,128]{3,2,1,0:T(8,128)S(1)} %collective-permute-done.1.halo_ref), custom_call_target="tpu_custom_call" | custom-call | flops 4 | bytes 1 | tf_op jit(solution)/shard_map/x_ends/pallas_call | solution.py:254
  10.9 0.4 %collective-permute-start.2 = (f32[1160,128]{1,0:T(8,128)S(1)}, f32[1160,128]{1,0:T(8,128)S(1)}, u32[]{:S(2)}, u32[]{:S(2)}) collective-permute-start(f32[1160,128]{1,0:T(8,128)S(1)} %get-tuple-element.31.after_ref.ws_ref), channel_id=1, source_target_pairs={{1,8},{9,16},{17,24},{25,0},{8,1},{16,9},{24,17},{0,25},{3,10},{11... | collective-permute-start | bytes 1781768 | tf_op jit(solution)/shard_map/ppermute | solution.py:760
  11.3 6.3 %z_own.1 = (f32[3,16,192,128]{3,2,1,0:T(8,128)S(1)}, f32[3,16,192,128]{3,2,1,0:T(8,128)S(1)}, f32[3,16,192,128]{3,2,1,0:T(8,128)S(1)}, bf16[192,192]{1,0:T(8,128...) custom-call(f32[192,192]{1,0:T(8,128)S(1)} %get-tuple-element.33.y_i, ...), custom_call_target="tpu_custom_call" | custom-call | flops 4 | bytes 1 | tf_op jit(solution)/shard_map/z_own/pallas_call | solution.py:607
  17.6 1.7 %collective-permute-start.6 = (f32[12,24,128]{2,1,0:T(8,128)S(1)}, f32[12,24,128]{2,1,0:T(8,128)S(1)}, u32[]{:S(2)}, u32[]{:S(2)}) collective-permute-start(f32[12,24,128]{2,1,0:T(8,128)S(1)} %get-tuple-element.49), channel_id=1, source_target_pairs={{0,4},{2,6},{4,0},{6,2},{1,5},{3,7},{5,1},{7,3},{8,12},{10,14},{12... | collective-permute-start | bytes 442376 | tf_op jit(solution)/shard_map/ppermute | solution.py:765
  19.3 1.5 %collective-permute-start.4 = (f32[13,24,128]{2,1,0:T(8,128)S(1)}, f32[13,24,128]{2,1,0:T(8,128)S(1)}, u32[]{:S(2)}, u32[]{:S(2)}) collective-permute-start(f32[13,24,128]{2,1,0:T(8,128)S(1)} %get-tuple-element.47.own_right_ref), channel_id=1, source_target_pairs={{0,2},{2,4},{4,6},{6,0},{1,3},{3,5},{5,7},{7,1},{8,10},{10,12},{12... | collective-permute-start | bytes 479240 | tf_op jit(solution)/shard_map/ppermute | solution.py:770
  20.8 1.4 %collective-permute-start.5 = (f32[13,24,128]{2,1,0:T(8,128)S(1)}, f32[13,24,128]{2,1,0:T(8,128)S(1)}, u32[]{:S(2)}, u32[]{:S(2)}) collective-permute-start(f32[13,24,128]{2,1,0:T(8,128)S(1)} %get-tuple-element.48.own_left_ref), channel_id=1, source_target_pairs={{0,6},{2,0},{4,2},{6,4},{1,7},{3,1},{5,3},{7,5},{8,14},{10,8},{12,... | collective-permute-start | bytes 479240 | tf_op jit(solution)/shard_map/ppermute | solution.py:771
  22.3 0.0 collective-permute-done.after_ref.near_ref
  22.3 2.4 %y_solve.1 = (f32[3,16,192,128]{3,2,1,0:T(8,128)S(1)}, f32[3,16,192,128]{3,2,1,0:T(8,128)S(1)}) custom-call(bf16[192,192]{1,0:T(8,128)(2,1)S(1)} %get-tuple-element.37.high_ref, bf16[192,192]{1,0:T(8,128)(2,1)S(1)} %get-tuple-element.38.low_ref, f32[3,16,192,128]{3,2,1,0:T(8,128)S(1)} %bitcast.4, ...), custom_call_target="tpu_custom_call", output_to_operand_aliasing={{0}: (3, {}), {1}: (4, {})} | custom-call | flops 20000000000 | bytes 1 | tf_op jit(solution)/shard_map/y_solve/pallas_call | solution.py:501
  24.7 2.4 %x_gradient_own.1 = (f32[3,3,16,192,128]{4,3,2,1,0:T(8,128)}, f32[3,16,192,128]{3,2,1,0:T(8,128)S(1)}) custom-call(f32[121,8,128]{2,1,0:T(8,128)S(1)} %get-tuple-element.29.table_ref, f32[3,16,192,128]{3,2,1,0:T(8,128)S(1)} %bitcast.4, f32[3,192,128]{2,1,0:T(8,128)S(1)} %collective-permute-done.after_ref.near_ref, ...), custom_call_target="tpu_custom_call" | custom-call | flops 4 | bytes 1 | tf_op jit(solution)/shard_map/x_gradient_own/pallas_call | solution.py:367
  27.0 0.5 %collective-permute-done.2.wr_ref = f32[1160,128]{1,0:T(8,128)S(1)} collective-permute-done((f32[1160,128]{1,0:T(8,128)S(1)}, f32[1160,128]{1,0:T(8,128)S(1)}, u32[]{:S(2)}, u32[]{:S(2)}) %collective-permute-start.2) | collective-permute-done | bytes 593952 | tf_op jit(solution)/shard_map/ppermute | solution.py:760
  27.5 0.5 %x_face.1 = (f32[6,192,128]{2,1,0:T(8,128)S(1)}, f32[1160,128]{1,0:T(8,128)S(1)}) custom-call(f32[121,8,128]{2,1,0:T(8,128)S(1)} %get-tuple-element.29.table_ref, f32[1160,128]{1,0:T(8,128)S(1)} %collective-permute-done.2.wr_ref, f32[1160,128]{1,0:T(8,128)S(1)} %get-tuple-element.31.after_ref.ws_ref, f32[6,192,128]{2,1,0:T(8,128)S(1)} %get-tuple-element.32.l_ref, ...), custom_call_target="tpu_custom_call" | custom-call | flops 4 | bytes 1 | tf_op jit(solution)/shard_map/x_face/pallas_call | solution.py:297
  28.0 0.1 collective-permute-start.3
  28.1 0.0 collective-permute-done.6.left_2_ref.right_2_ref
  28.1 0.0 collective-permute-done.4.left_ref
  28.1 0.1 collective-permute-done.5.right_ref
  28.1 2.1 %z_gradient_join.1 = (f32[3,16,192,128]{3,2,1,0:T(8,128)S(1)}, bf16[16,192,96]{2,1,0:T(8,128)(2,1)S(1)}, bf16[96,768]{1,0:T(8,128)(2,1)S(1)}) custom-call(f32[128,128]{1,0:T(8,128)S(1)} %get-tuple-element.35.inv_ref, f32[1,128]{1,0:T(1,128)S(1)} %get-tuple-element.36.m_ref, ...), custom_call_target="tpu_custom_call", output_to_operand_aliasing={{0}: (2, {})} | custom-call | flops 20000000000 | bytes 1 | tf_op jit(solution)/shard_map/z_gradient_join/pallas_call | solution.py:723
  30.2 0.0 collective-permute-done.3.r_ref
  30.2 5.3 %x_solve.1 = (f32[3,3,16,192,128]{4,3,2,1,0:T(8,128)}, f32[3,16,192,128]{3,2,1,0:T(8,128)}) custom-call(f32[121,8,128]{2,1,0:T(8,128)S(1)} %get-tuple-element.29.table_ref, f32[3,16,192,128]{3,2,1,0:T(8,128)S(1)} %bitcast.4, f32[3,192,128]{2,1,0:T(8,128)S(1)} %collective-permute-done.after_ref.near_ref, ...), custom_call_target="tpu_custom_call", output_to_operand_aliasing={{0}: (12, {})} | custom-call | flops 4 | bytes 1 | tf_op jit(solution)/shard_map/x_solve/pallas_call | solution.py:457
  (1 shorter events, 0.0 us)
Async XLA Ops:
  0.6 8.1 %slice-start = ((s8[4718592]{0:T(1024)(128)(4,1)}), s8[4194304]{0:T(1024)(128)(4,1)S(1)}, s32[]{:S(2)}) async-start(s8[4718592]{0:T(1024)(128)(4,1)} %bitcast.3), calls=%async_computation | async-start | bytes 8388608
  2.1 20.2 %collective-permute-start = (f32[3,192,128]{2,1,0:T(8,128)S(1)}, f32[3,192,128]{2,1,0:T(8,128)S(1)}, u32[]{:S(2)}, u32[]{:S(2)}) collective-permute-start(f32[3,192,128]{2,1,0:T(8,128)S(1)} %get-tuple-element.28.after_ref.own_ref), channel_id=1, source_target_pairs={{1,8},{9,16},{17,24},{25,0},{8,1},{16,9},{24,17},{0,25},{3,10},{11... | collective-permute-start | bytes 884744 | tf_op jit(solution)/shard_map/ppermute | solution.py:752
  6.7 2.0 %collective-permute-start.1 = (f32[3,2,192,128]{3,2,1,0:T(8,128)S(1)}, f32[3,2,192,128]{3,2,1,0:T(8,128)S(1)}, u32[]{:S(2)}, u32[]{:S(2)}) collective-permute-start(f32[3,2,192,128]{3,2,1,0:T(8,128)S(1)} %get-tuple-element.30), channel_id=1, source_target_pairs={{0,1},{1,0},{2,3},{3,2},{4,5},{5,4},{6,7},{7,6},{8,9},{9,8},{10,11... | collective-permute-start | bytes 1769480 | tf_op jit(solution)/shard_map/ppermute | solution.py:753
  6.7 2.0 %slice-start.1 = ((s8[4718592]{0:T(1024)(128)(4,1)}), s8[524288]{0:T(1024)(128)(4,1)S(1)}, s32[]{:S(2)}) async-start(s8[4718592]{0:T(1024)(128)(4,1)} %bitcast.3), calls=%async_computation.1 | async-start | bytes 1048576
  10.9 16.6 %collective-permute-start.2 = (f32[1160,128]{1,0:T(8,128)S(1)}, f32[1160,128]{1,0:T(8,128)S(1)}, u32[]{:S(2)}, u32[]{:S(2)}) collective-permute-start(f32[1160,128]{1,0:T(8,128)S(1)} %get-tuple-element.31.after_ref.ws_ref), channel_id=1, source_target_pairs={{1,8},{9,16},{17,24},{25,0},{8,1},{16,9},{24,17},{0,25},{3,10},{11... | collective-permute-start | bytes 1781768 | tf_op jit(solution)/shard_map/ppermute | solution.py:760
  17.6 10.4 %collective-permute-start.6 = (f32[12,24,128]{2,1,0:T(8,128)S(1)}, f32[12,24,128]{2,1,0:T(8,128)S(1)}, u32[]{:S(2)}, u32[]{:S(2)}) collective-permute-start(f32[12,24,128]{2,1,0:T(8,128)S(1)} %get-tuple-element.49), channel_id=1, source_target_pairs={{0,4},{2,6},{4,0},{6,2},{1,5},{3,7},{5,1},{7,3},{8,12},{10,14},{12... | collective-permute-start | bytes 442376 | tf_op jit(solution)/shard_map/ppermute | solution.py:765
  19.3 8.7 %collective-permute-start.4 = (f32[13,24,128]{2,1,0:T(8,128)S(1)}, f32[13,24,128]{2,1,0:T(8,128)S(1)}, u32[]{:S(2)}, u32[]{:S(2)}) collective-permute-start(f32[13,24,128]{2,1,0:T(8,128)S(1)} %get-tuple-element.47.own_right_ref), channel_id=1, source_target_pairs={{0,2},{2,4},{4,6},{6,0},{1,3},{3,5},{5,7},{7,1},{8,10},{10,12},{12... | collective-permute-start | bytes 479240 | tf_op jit(solution)/shard_map/ppermute | solution.py:770
  20.8 7.3 %collective-permute-start.5 = (f32[13,24,128]{2,1,0:T(8,128)S(1)}, f32[13,24,128]{2,1,0:T(8,128)S(1)}, u32[]{:S(2)}, u32[]{:S(2)}) collective-permute-start(f32[13,24,128]{2,1,0:T(8,128)S(1)} %get-tuple-element.48.own_left_ref), channel_id=1, source_target_pairs={{0,6},{2,0},{4,2},{6,4},{1,7},{3,1},{5,3},{7,5},{8,14},{10,8},{12,... | collective-permute-start | bytes 479240 | tf_op jit(solution)/shard_map/ppermute | solution.py:771
  28.0 2.2 %collective-permute-start.3 = (f32[1160,128]{1,0:T(8,128)S(1)}, f32[1160,128]{1,0:T(8,128)S(1)}, u32[]{:S(2)}, u32[]{:S(2)}) collective-permute-start(f32[1160,128]{1,0:T(8,128)S(1)} %get-tuple-element.44.after_ref.e_ref), channel_id=1, source_target_pairs={{0,1},{1,0},{2,3},{3,2},{4,5},{5,4},{6,7},{7,6},{8,9},{9,8},{10,11... | collective-permute-start | bytes 1781768 | tf_op jit(solution)/shard_map/ppermute | solution.py:779

commit v5 on v4

--- a/solution.py
+++ b/solution.py
@@ -27,10 +27,6 @@
 
 def dot(a, b):
     return lax.dot_general(a, b, (((1,), (0,)), ((), ())), preferred_element_type=F32)
-
-
-def dot_nt(a, b):
-    return lax.dot_general(a, b, (((1,), (1,)), ((), ())), preferred_element_type=F32)
 
 
 def params():

time: 35.7 us -> 35.7 us (level)
  no operation moved by 1% of the time
where the time goes in v5:
time: 35.7 us; the launch traced here: 35.6 us
  Pallas kernels  23.7 us (66%)
  starting transfers between devices  9.7 us (27%)
  waiting for transfers between devices  1.42 us (4%)
  between operations  0.74 us (2%)
    pallas_call x1, Pallas kernels, z_own(): pl.pallas_call(functools.partial(z_own_kernel, n), in_specs=[WHOLE] * 5 +...  6.32 us
    pallas_call x1, Pallas kernels, x_solve(): pl.pallas_call(functools.partial(x_solve_kernel, n, ny), in_specs=[WHOLE]...  5.34 us
    ppermute x1, starting transfers between devices, on_device(): near = lax.ppermute(own, ('gx', 'gy'), across)  4.55 us
    pallas_call x1, Pallas kernels, y_solve(): pl.pallas_call(functools.partial(y_kernel, n), in_specs=[WHOLE] * 5 + [AN...  2.38 us
    pallas_call x1, Pallas kernels, x_gradient_own(): pl.pallas_call(functools.partial(x_gradient_kernel, n, ny), in_specs=[WHO...  2.37 us
    pallas_call x1, Pallas kernels, x_ends(): pl.pallas_call(functools.partial(x_ends_kernel, n, ny), in_specs=[WHOLE]...  2.17 us
    pallas_call x1, Pallas kernels, z_gradient_join(): pl.pallas_call(functools.partial(z_gradient_kernel, n), in_specs=[WHOLE]...  2.06 us
    ppermute x1, starting transfers between devices, on_device(): left_far = lax.ppermute(to_far, 'gz', shift(2))  1.7 us
  transfers between devices with their start and end apart: 7, of which 3 were waited for; matrix products, arithmetic and copies ran while one was open for 0% of the time, Pallas kernels for 47%

profile of v5, /device:TPU:0, one launch (start us, length us, event | category | flops | bytes accessed | tf_op | source)
XLA Modules:
  0.0 35.6 jit_solution(1237397044143551659)
XLA Ops:
  0.6 0.0 slice-start
  0.6 1.5 %prepare.1 = (f32[3,192,128]{2,1,0:T(8,128)S(1)}, f32[3,2,192,128]{3,2,1,0:T(8,128)S(1)}) custom-call(f32[3,16,192,128]{3,2,1,0:T(8,128)} %v_ref.11), custom_call_target="tpu_custom_call" | custom-call | tf_op jit(solution)/shard_map/prepare/pallas_call | solution.py:105
  2.1 4.6 %collective-permute-start = (f32[3,192,128]{2,1,0:T(8,128)S(1)}, f32[3,192,128]{2,1,0:T(8,128)S(1)}, u32[]{:S(2)}, u32[]{:S(2)}) collective-permute-start(f32[3,192,128]{2,1,0:T(8,128)S(1)} %get-tuple-element.28.after_ref.own_ref), channel_id=1, source_target_pairs={{1,8},{9,16},{17,24},{25,0},{8,1},{16,9},{24,17},{0,25},{3,10},{11... | collective-permute-start | bytes 884744 | tf_op jit(solution)/shard_map/ppermute | solution.py:748
  6.7 0.0 collective-permute-start.1
  6.7 0.0 slice-start.1
  6.7 1.1 %tables.1 = (f32[121,8,128]{2,1,0:T(8,128)S(1)}, f32[192,192]{1,0:T(8,128)S(1)}, f32[1,192]{1,0:T(1,128)S(1)}, f32[128,128]{1,0:T(8,128)S(1)}, f32[1,128]{1,0:T(1,128)S(1)}) custom-call(f32[16,16]{1,0:T(8,128)} %xi_ref.1, f32[1,16]{1,0:T(1,128)} %bitcast.6, f32[192,192]{1,0:T(8,128)} %yi_ref.1, f32[1,192]{1,0:T(1,128)} %bitcast.5, f32[128,128]{1,0:T(8,128)} %zi_ref.1, ...), custom_call_target="tpu_custom_call" | custom-call | flops 20000000000 | bytes 1 | tf_op jit(solution)/shard_map/tables/pallas_call | solution.py:203
  7.8 0.9 %collective-permute-done.1.halo_ref = f32[3,2,192,128]{3,2,1,0:T(8,128)S(1)} collective-permute-done((f32[3,2,192,128]{3,2,1,0:T(8,128)S(1)}, f32[3,2,192,128]{3,2,1,0:T(8,128)S(1)}, u32[]{:S(2)}, u32[]{:S(2)}) %collective-permute-start.1) | collective-permute-done | bytes 589856 | tf_op jit(solution)/shard_map/ppermute | solution.py:749
  8.7 0.0 slice-done
  8.7 0.0 slice-done.1
  8.7 2.2 %x_ends.1 = (f32[1160,128]{1,0:T(8,128)S(1)}, f32[6,192,128]{2,1,0:T(8,128)S(1)}) custom-call(f32[121,8,128]{2,1,0:T(8,128)S(1)} %get-tuple-element.29.table_ref, f32[3,16,192,128]{3,2,1,0:T(8,128)S(1)} %bitcast.4, f32[3,2,192,128]{3,2,1,0:T(8,128)S(1)} %collective-permute-done.1.halo_ref), custom_call_target="tpu_custom_call" | custom-call | flops 4 | bytes 1 | tf_op jit(solution)/shard_map/x_ends/pallas_call | solution.py:250
  10.9 0.4 %collective-permute-start.2 = (f32[1160,128]{1,0:T(8,128)S(1)}, f32[1160,128]{1,0:T(8,128)S(1)}, u32[]{:S(2)}, u32[]{:S(2)}) collective-permute-start(f32[1160,128]{1,0:T(8,128)S(1)} %get-tuple-element.31.after_ref.ws_ref), channel_id=1, source_target_pairs={{1,8},{9,16},{17,24},{25,0},{8,1},{16,9},{24,17},{0,25},{3,10},{11... | collective-permute-start | bytes 1781768 | tf_op jit(solution)/shard_map/ppermute | solution.py:756
  11.3 6.3 %z_own.1 = (f32[3,16,192,128]{3,2,1,0:T(8,128)S(1)}, f32[3,16,192,128]{3,2,1,0:T(8,128)S(1)}, f32[3,16,192,128]{3,2,1,0:T(8,128)S(1)}, bf16[192,192]{1,0:T(8,128...) custom-call(f32[192,192]{1,0:T(8,128)S(1)} %get-tuple-element.33.y_i, ...), custom_call_target="tpu_custom_call" | custom-call | flops 4 | bytes 1 | tf_op jit(solution)/shard_map/z_own/pallas_call | solution.py:603
  17.6 1.7 %collective-permute-start.6 = (f32[12,24,128]{2,1,0:T(8,128)S(1)}, f32[12,24,128]{2,1,0:T(8,128)S(1)}, u32[]{:S(2)}, u32[]{:S(2)}) collective-permute-start(f32[12,24,128]{2,1,0:T(8,128)S(1)} %get-tuple-element.49), channel_id=1, source_target_pairs={{0,4},{2,6},{4,0},{6,2},{1,5},{3,7},{5,1},{7,3},{8,12},{10,14},{12... | collective-permute-start | bytes 442376 | tf_op jit(solution)/shard_map/ppermute | solution.py:761
  19.3 1.5 %collective-permute-start.4 = (f32[13,24,128]{2,1,0:T(8,128)S(1)}, f32[13,24,128]{2,1,0:T(8,128)S(1)}, u32[]{:S(2)}, u32[]{:S(2)}) collective-permute-start(f32[13,24,128]{2,1,0:T(8,128)S(1)} %get-tuple-element.47.own_right_ref), channel_id=1, source_target_pairs={{0,2},{2,4},{4,6},{6,0},{1,3},{3,5},{5,7},{7,1},{8,10},{10,12},{12... | collective-permute-start | bytes 479240 | tf_op jit(solution)/shard_map/ppermute | solution.py:766
  20.8 1.4 %collective-permute-start.5 = (f32[13,24,128]{2,1,0:T(8,128)S(1)}, f32[13,24,128]{2,1,0:T(8,128)S(1)}, u32[]{:S(2)}, u32[]{:S(2)}) collective-permute-start(f32[13,24,128]{2,1,0:T(8,128)S(1)} %get-tuple-element.48.own_left_ref), channel_id=1, source_target_pairs={{0,6},{2,0},{4,2},{6,4},{1,7},{3,1},{5,3},{7,5},{8,14},{10,8},{12,... | collective-permute-start | bytes 479240 | tf_op jit(solution)/shard_map/ppermute | solution.py:767
  22.3 0.0 collective-permute-done.after_ref.near_ref
  22.3 2.4 %y_solve.1 = (f32[3,16,192,128]{3,2,1,0:T(8,128)S(1)}, f32[3,16,192,128]{3,2,1,0:T(8,128)S(1)}) custom-call(bf16[192,192]{1,0:T(8,128)(2,1)S(1)} %get-tuple-element.37.high_ref, bf16[192,192]{1,0:T(8,128)(2,1)S(1)} %get-tuple-element.38.low_ref, f32[3,16,192,128]{3,2,1,0:T(8,128)S(1)} %bitcast.4, ...), custom_call_target="tpu_custom_call", output_to_operand_aliasing={{0}: (3, {}), {1}: (4, {})} | custom-call | flops 20000000000 | bytes 1 | tf_op jit(solution)/shard_map/y_solve/pallas_call | solution.py:497
  24.7 2.4 %x_gradient_own.1 = (f32[3,3,16,192,128]{4,3,2,1,0:T(8,128)}, f32[3,16,192,128]{3,2,1,0:T(8,128)S(1)}) custom-call(f32[121,8,128]{2,1,0:T(8,128)S(1)} %get-tuple-element.29.table_ref, f32[3,16,192,128]{3,2,1,0:T(8,128)S(1)} %bitcast.4, f32[3,192,128]{2,1,0:T(8,128)S(1)} %collective-permute-done.after_ref.near_ref, ...), custom_call_target="tpu_custom_call" | custom-call | flops 4 | bytes 1 | tf_op jit(solution)/shard_map/x_gradient_own/pallas_call | solution.py:363
  27.0 0.5 %collective-permute-done.2.wr_ref = f32[1160,128]{1,0:T(8,128)S(1)} collective-permute-done((f32[1160,128]{1,0:T(8,128)S(1)}, f32[1160,128]{1,0:T(8,128)S(1)}, u32[]{:S(2)}, u32[]{:S(2)}) %collective-permute-start.2) | collective-permute-done | bytes 593952 | tf_op jit(solution)/shard_map/ppermute | solution.py:756
  27.5 0.5 %x_face.1 = (f32[6,192,128]{2,1,0:T(8,128)S(1)}, f32[1160,128]{1,0:T(8,128)S(1)}) custom-call(f32[121,8,128]{2,1,0:T(8,128)S(1)} %get-tuple-element.29.table_ref, f32[1160,128]{1,0:T(8,128)S(1)} %collective-permute-done.2.wr_ref, f32[1160,128]{1,0:T(8,128)S(1)} %get-tuple-element.31.after_ref.ws_ref, f32[6,192,128]{2,1,0:T(8,128)S(1)} %get-tuple-element.32.l_ref, ...), custom_call_target="tpu_custom_call" | custom-call | flops 4 | bytes 1 | tf_op jit(solution)/shard_map/x_face/pallas_call | solution.py:293
  28.0 0.1 collective-permute-start.3
  28.1 0.0 collective-permute-done.6.left_2_ref.right_2_ref
  28.1 0.0 collective-permute-done.4.left_ref
  28.1 0.1 collective-permute-done.5.right_ref
  28.1 2.1 %z_gradient_join.1 = (f32[3,16,192,128]{3,2,1,0:T(8,128)S(1)}, bf16[16,192,96]{2,1,0:T(8,128)(2,1)S(1)}, bf16[96,768]{1,0:T(8,128)(2,1)S(1)}) custom-call(f32[128,128]{1,0:T(8,128)S(1)} %get-tuple-element.35.inv_ref, f32[1,128]{1,0:T(1,128)S(1)} %get-tuple-element.36.m_ref, ...), custom_call_target="tpu_custom_call", output_to_operand_aliasing={{0}: (2, {})} | custom-call | flops 20000000000 | bytes 1 | tf_op jit(solution)/shard_map/z_gradient_join/pallas_call | solution.py:719
  30.2 0.0 collective-permute-done.3.r_ref
  30.2 5.3 %x_solve.1 = (f32[3,3,16,192,128]{4,3,2,1,0:T(8,128)}, f32[3,16,192,128]{3,2,1,0:T(8,128)}) custom-call(f32[121,8,128]{2,1,0:T(8,128)S(1)} %get-tuple-element.29.table_ref, f32[3,16,192,128]{3,2,1,0:T(8,128)S(1)} %bitcast.4, f32[3,192,128]{2,1,0:T(8,128)S(1)} %collective-permute-done.after_ref.near_ref, ...), custom_call_target="tpu_custom_call", output_to_operand_aliasing={{0}: (12, {})} | custom-call | flops 4 | bytes 1 | tf_op jit(solution)/shard_map/x_solve/pallas_call | solution.py:453
  (1 shorter events, 0.0 us)
Async XLA Ops:
  0.6 8.1 %slice-start = ((s8[4718592]{0:T(1024)(128)(4,1)}), s8[4194304]{0:T(1024)(128)(4,1)S(1)}, s32[]{:S(2)}) async-start(s8[4718592]{0:T(1024)(128)(4,1)} %bitcast.3), calls=%async_computation | async-start | bytes 8388608
  2.1 20.2 %collective-permute-start = (f32[3,192,128]{2,1,0:T(8,128)S(1)}, f32[3,192,128]{2,1,0:T(8,128)S(1)}, u32[]{:S(2)}, u32[]{:S(2)}) collective-permute-start(f32[3,192,128]{2,1,0:T(8,128)S(1)} %get-tuple-element.28.after_ref.own_ref), channel_id=1, source_target_pairs={{1,8},{9,16},{17,24},{25,0},{8,1},{16,9},{24,17},{0,25},{3,10},{11... | collective-permute-start | bytes 884744 | tf_op jit(solution)/shard_map/ppermute | solution.py:748
  6.7 2.0 %collective-permute-start.1 = (f32[3,2,192,128]{3,2,1,0:T(8,128)S(1)}, f32[3,2,192,128]{3,2,1,0:T(8,128)S(1)}, u32[]{:S(2)}, u32[]{:S(2)}) collective-permute-start(f32[3,2,192,128]{3,2,1,0:T(8,128)S(1)} %get-tuple-element.30), channel_id=1, source_target_pairs={{0,1},{1,0},{2,3},{3,2},{4,5},{5,4},{6,7},{7,6},{8,9},{9,8},{10,11... | collective-permute-start | bytes 1769480 | tf_op jit(solution)/shard_map/ppermute | solution.py:749
  6.7 2.0 %slice-start.1 = ((s8[4718592]{0:T(1024)(128)(4,1)}), s8[524288]{0:T(1024)(128)(4,1)S(1)}, s32[]{:S(2)}) async-start(s8[4718592]{0:T(1024)(128)(4,1)} %bitcast.3), calls=%async_computation.1 | async-start | bytes 1048576
  10.9 16.6 %collective-permute-start.2 = (f32[1160,128]{1,0:T(8,128)S(1)}, f32[1160,128]{1,0:T(8,128)S(1)}, u32[]{:S(2)}, u32[]{:S(2)}) collective-permute-start(f32[1160,128]{1,0:T(8,128)S(1)} %get-tuple-element.31.after_ref.ws_ref), channel_id=1, source_target_pairs={{1,8},{9,16},{17,24},{25,0},{8,1},{16,9},{24,17},{0,25},{3,10},{11... | collective-permute-start | bytes 1781768 | tf_op jit(solution)/shard_map/ppermute | solution.py:756
  17.6 10.4 %collective-permute-start.6 = (f32[12,24,128]{2,1,0:T(8,128)S(1)}, f32[12,24,128]{2,1,0:T(8,128)S(1)}, u32[]{:S(2)}, u32[]{:S(2)}) collective-permute-start(f32[12,24,128]{2,1,0:T(8,128)S(1)} %get-tuple-element.49), channel_id=1, source_target_pairs={{0,4},{2,6},{4,0},{6,2},{1,5},{3,7},{5,1},{7,3},{8,12},{10,14},{12... | collective-permute-start | bytes 442376 | tf_op jit(solution)/shard_map/ppermute | solution.py:761
  19.3 8.7 %collective-permute-start.4 = (f32[13,24,128]{2,1,0:T(8,128)S(1)}, f32[13,24,128]{2,1,0:T(8,128)S(1)}, u32[]{:S(2)}, u32[]{:S(2)}) collective-permute-start(f32[13,24,128]{2,1,0:T(8,128)S(1)} %get-tuple-element.47.own_right_ref), channel_id=1, source_target_pairs={{0,2},{2,4},{4,6},{6,0},{1,3},{3,5},{5,7},{7,1},{8,10},{10,12},{12... | collective-permute-start | bytes 479240 | tf_op jit(solution)/shard_map/ppermute | solution.py:766
  20.8 7.3 %collective-permute-start.5 = (f32[13,24,128]{2,1,0:T(8,128)S(1)}, f32[13,24,128]{2,1,0:T(8,128)S(1)}, u32[]{:S(2)}, u32[]{:S(2)}) collective-permute-start(f32[13,24,128]{2,1,0:T(8,128)S(1)} %get-tuple-element.48.own_left_ref), channel_id=1, source_target_pairs={{0,6},{2,0},{4,2},{6,4},{1,7},{3,1},{5,3},{7,5},{8,14},{10,8},{12,... | collective-permute-start | bytes 479240 | tf_op jit(solution)/shard_map/ppermute | solution.py:767
  28.0 2.2 %collective-permute-start.3 = (f32[1160,128]{1,0:T(8,128)S(1)}, f32[1160,128]{1,0:T(8,128)S(1)}, u32[]{:S(2)}, u32[]{:S(2)}) collective-permute-start(f32[1160,128]{1,0:T(8,128)S(1)} %get-tuple-element.44.after_ref.e_ref), channel_id=1, source_target_pairs={{0,1},{1,0},{2,3},{3,2},{4,5},{5,4},{6,7},{7,6},{8,9},{9,8},{10,11... | collective-permute-start | bytes 1781768 | tf_op jit(solution)/shard_map/ppermute | solution.py:775

commit v6 on v5

--- a/solution.py
+++ b/solution.py
@@ -218,26 +218,23 @@
     )(*(pltpu.with_memory_space_constraint(value, pltpu.HBM) for value in inputs), after)
 
 
-def x_ends_kernel(n, ny, table_ref, v_ref, halo_ref, w_ref, l_ref):
+def x_ends_kernel(n, ny, table_ref, v_ref, halo_ref, w_ref):
     table = Table(n)
 
     def tile(index, carry):
         start = pl.multiple_of(index * 8, 8)
         rows = pl.ds(start, 8)
         w = [None] * 6
-        l = [None] * 6
         for k in range(n + 2):
             if k < n:
                 fields = six([v_ref[i, k, rows, :] for i in range(3)], 0)
             else:
                 fields = six([halo_ref[i, k - n, rows, :] for i in range(3)], 0)
-            a, b = table_ref[table.send + k], table_ref[table.last + k]
+            a = table_ref[table.send + k]
             for f in range(6):
                 w[f] = a * fields[f] if k == 0 else w[f] + a * fields[f]
-                l[f] = b * fields[f] if k == 0 else l[f] + b * fields[f]
         for f in range(6):
             w_ref[pl.ds(f * ny + start, 8), :] = w[f]
-            l_ref[f, rows, :] = l[f]
         return carry
 
     lax.fori_loop(0, ny // 8, tile, 0)
@@ -250,8 +247,8 @@
     return pl.pallas_call(
         functools.partial(x_ends_kernel, n, ny),
         in_specs=[WHOLE] * 3,
-        out_specs=[WHOLE, WHOLE],
-        out_shape=[layer_shape(6 * ny + 8, nz), layer_shape(6, ny, nz)],
+        out_specs=WHOLE,
+        out_shape=layer_shape(6 * ny + 8, nz),
         compiler_params=params(),
         cost_estimate=cost(SHORT),
         name="x_ends",
@@ -479,7 +476,22 @@
     return values
 
 
-def y_kernel(n, high_ref, low_ref, v_ref, held_ref, part_ref, after_ref, g_ref, c_ref):
+def y_kernel(n, high_ref, low_ref, v_ref, held_ref, part_ref, table_ref, halo_ref, after_ref, g_ref, c_ref, l_ref):
+    table = Table(n)
+    tiles = v_ref.shape[2] // 8 // (n // GROUP)
+    share = tiles // (GROUP - EARLY)
+
+    def inner_end(index):
+        rows = pl.ds(pl.multiple_of(index * 8, 8), 8)
+        l = [None] * 6
+        for k in range(n + 2):
+            fields = six([v_ref[i, k, rows, :] if k < n else halo_ref[i, k - n, rows, :] for i in range(3)], 0)
+            b = table_ref[table.last + k]
+            for f in range(6):
+                l[f] = b * fields[f] if k == 0 else l[f] + b * fields[f]
+        for f in range(6):
+            l_ref[f, rows, :] = l[f]
+
     def step(group, carry):
         for u in range(EARLY, GROUP):
             p = group * GROUP + u
@@ -487,23 +499,25 @@
             for f in range(3):
                 g_ref[f, p] = values[f]
                 c_ref[f, p] = values[3 + f] + part_ref[f, p]
+            for j in range(share):
+                inner_end(group * tiles + (u - EARLY) * share + j)
         return carry
 
     lax.fori_loop(0, n // GROUP, step, 0)
 
 
-def y_solve(high, low, velocity, early, partial, after):
+def y_solve(high, low, velocity, early, partial, table, halo, after):
     _, n, ny, nz = velocity.shape
     return pl.pallas_call(
         functools.partial(y_kernel, n),
-        in_specs=[WHOLE] * 5 + [ANY],
-        out_specs=[WHOLE, WHOLE],
-        out_shape=[in_vmem(3, n, ny, nz), in_vmem(3, n, ny, nz)],
+        in_specs=[WHOLE] * 7 + [ANY],
+        out_specs=[WHOLE] * 3,
+        out_shape=[in_vmem(3, n, ny, nz), in_vmem(3, n, ny, nz), layer_shape(6, ny, nz)],
         input_output_aliases={3: 0, 4: 1},
         compiler_params=params(),
         cost_estimate=cost(LONG),
         name="y_solve",
-    )(high, low, velocity, early, partial, after)
+    )(high, low, velocity, early, partial, table, halo, after)
 
 
 LINES = 128
@@ -752,7 +766,7 @@
         x_inverse, metric_x[None], y_inverse, metric_y[None], z_inverse, metric_z[None], own
     )
 
-    x_sent, x_partial = x_ends(table, held, halo)
+    x_sent = x_ends(table, held, halo)
     x_received = lax.ppermute(x_sent, ("gx", "gy"), across)
 
     z_gradient, convection, y_gradient, y_high, y_low, to_right, to_left, to_far = z_own(
@@ -769,7 +783,9 @@
         right_far,
     )
 
-    y_gradient, convection = y_solve(y_high, y_low, held, y_gradient, convection, near)
+    y_gradient, convection, x_partial = y_solve(
+        y_high, y_low, held, y_gradient, convection, table, halo, near
+    )
     gradient, x_gradient = x_gradient_own(table, held, near, halo, y_gradient)
     outer, x_end = x_face(table, x_received, x_sent, x_partial, own, near, x_gradient, n)
     x_other = lax.ppermute(x_end, "gy", beside)

time: 35.7 us -> 39.8 us (1.11)
  local copies, waits for them, and re-layouts: 0.01 us -> 4.53 us
  waiting for transfers between devices: 1.42 us -> 0.89 us
    unnamed x4 -> x8, local copies, waits for them, and re-layouts: 0.01 us -> 4.53 us
    pallas_call x1, Pallas kernels: 2.38 us -> 3.22 us  [y_solve(): pl.pallas_call(functools.partial(y_kernel, n), in_specs=[WHOLE] * 7 + [AN...]
    pallas_call x1, Pallas kernels: 2.17 us -> 1.48 us  [x_ends(): pl.pallas_call(functools.partial(x_ends_kernel, n, ny), in_specs=[WHOLE]...]
    ppermute x1, waiting for transfers between devices: 0.47 us -> 0.01 us  [on_device(): x_received = lax.ppermute(x_sent, ('gx', 'gy'), across)]
  transfers between devices with their start and end apart: 7 -> 7, of which waited for: 3 -> 1; matrix products, arithmetic and copies ran while one was open for 0% -> 0% of each run, Pallas kernels for 47% -> 43%
where the time goes in v6:
time: 39.8 us; the launch traced here: 39.6 us
  Pallas kernels  23.8 us (60%)
  starting transfers between devices  9.7 us (24%)
  local copies, waits for them, and re-layouts  4.53 us (11%)
  waiting for transfers between devices  0.89 us (2%)
  between operations  0.76 us (2%)
    pallas_call x1, Pallas kernels, z_own(): pl.pallas_call(functools.partial(z_own_kernel, n), in_specs=[WHOLE] * 5 +...  6.23 us
    pallas_call x1, Pallas kernels, x_solve(): pl.pallas_call(functools.partial(x_solve_kernel, n, ny), in_specs=[WHOLE]...  5.34 us
    ppermute x1, starting transfers between devices, on_device(): near = lax.ppermute(own, ('gx', 'gy'), across)  4.55 us
    unnamed x8, local copies, waits for them, and re-layouts  4.53 us
    pallas_call x1, Pallas kernels, y_solve(): pl.pallas_call(functools.partial(y_kernel, n), in_specs=[WHOLE] * 7 + [AN...  3.22 us
    pallas_call x1, Pallas kernels, x_gradient_own(): pl.pallas_call(functools.partial(x_gradient_kernel, n, ny), in_specs=[WHO...  2.35 us
    pallas_call x1, Pallas kernels, z_gradient_join(): pl.pallas_call(functools.partial(z_gradient_kernel, n), in_specs=[WHOLE]...  2.07 us
    ppermute x1, starting transfers between devices, on_device(): left_far = lax.ppermute(to_far, 'gz', shift(2))  1.71 us
  transfers between devices with their start and end apart: 7, of which 1 were waited for; matrix products, arithmetic and copies ran while one was open for 0% of the time, Pallas kernels for 43%

profile of v6, /device:TPU:0, one launch (start us, length us, event | category | flops | bytes accessed | tf_op | source)
XLA Modules:
  0.0 39.6 jit_solution(10151048319645139712)
XLA Ops:
  0.6 0.0 slice-start
  0.6 1.5 %prepare.1 = (f32[3,192,128]{2,1,0:T(8,128)S(1)}, f32[3,2,192,128]{3,2,1,0:T(8,128)S(1)}) custom-call(f32[3,16,192,128]{3,2,1,0:T(8,128)} %v_ref.11), custom_call_target="tpu_custom_call" | custom-call | tf_op jit(solution)/shard_map/prepare/pallas_call | solution.py:105
  2.1 4.6 %collective-permute-start = (f32[3,192,128]{2,1,0:T(8,128)S(1)}, f32[3,192,128]{2,1,0:T(8,128)S(1)}, u32[]{:S(2)}, u32[]{:S(2)}) collective-permute-start(f32[3,192,128]{2,1,0:T(8,128)S(1)} %get-tuple-element.27.after_ref.own_ref), channel_id=1, source_target_pairs={{1,8},{9,16},{17,24},{25,0},{8,1},{16,9},{24,17},{0,25},{3,10},{11... | collective-permute-start | bytes 884744 | tf_op jit(solution)/shard_map/ppermute | solution.py:762
  6.7 0.0 collective-permute-start.1
  6.7 0.0 slice-start.1
  6.7 1.1 %tables.1 = (f32[121,8,128]{2,1,0:T(8,128)S(1)}, f32[192,192]{1,0:T(8,128)S(1)}, f32[1,192]{1,0:T(1,128)S(1)}, f32[128,128]{1,0:T(8,128)S(1)}, f32[1,128]{1,0:T(1,128)S(1)}) custom-call(f32[16,16]{1,0:T(8,128)} %xi_ref.1, f32[1,16]{1,0:T(1,128)} %bitcast.6, f32[192,192]{1,0:T(8,128)} %yi_ref.1, f32[1,192]{1,0:T(1,128)} %bitcast.5, f32[128,128]{1,0:T(8,128)} %zi_ref.1, ...), custom_call_target="tpu_custom_call" | custom-call | flops 20000000000 | bytes 1 | tf_op jit(solution)/shard_map/tables/pallas_call | solution.py:203
  7.8 0.9 %collective-permute-done.1.halo_ref = f32[3,2,192,128]{3,2,1,0:T(8,128)S(1)} collective-permute-done((f32[3,2,192,128]{3,2,1,0:T(8,128)S(1)}, f32[3,2,192,128]{3,2,1,0:T(8,128)S(1)}, u32[]{:S(2)}, u32[]{:S(2)}) %collective-permute-start.1) | collective-permute-done | bytes 589856 | tf_op jit(solution)/shard_map/ppermute | solution.py:763
  8.7 0.0 slice-done
  8.7 0.0 slice-done.1
  8.7 1.5 %x_ends.1.after_ref.ws_ref = f32[1160,128]{1,0:T(8,128)S(1)} custom-call(f32[121,8,128]{2,1,0:T(8,128)S(1)} %get-tuple-element.28.table_ref, f32[3,16,192,128]{3,2,1,0:T(8,128)S(1)} %bitcast.4, f32[3,2,192,128]{3,2,1,0:T(8,128)S(1)} %collective-permute-done.1.halo_ref), custom_call_target="tpu_custom_call" | custom-call | flops 4 | bytes 1 | tf_op jit(solution)/shard_map/x_ends/pallas_call | solution.py:247
  10.2 0.4 %collective-permute-start.2 = (f32[1160,128]{1,0:T(8,128)S(1)}, f32[1160,128]{1,0:T(8,128)S(1)}, u32[]{:S(2)}, u32[]{:S(2)}) collective-permute-start(f32[1160,128]{1,0:T(8,128)S(1)} %x_ends.1.after_ref.ws_ref), channel_id=1, source_target_pairs={{1,8},{9,16},{17,24},{25,0},{8,1},{16,9},{24,17},{0,25},{3,10},{11... | collective-permute-start | bytes 1781768 | tf_op jit(solution)/shard_map/ppermute | solution.py:770
  10.6 6.2 %z_own.1 = (f32[3,16,192,128]{3,2,1,0:T(8,128)S(1)}, f32[3,16,192,128]{3,2,1,0:T(8,128)S(1)}, f32[3,16,192,128]{3,2,1,0:T(8,128)S(1)}, bf16[192,192]{1,0:T(8,128...) custom-call(f32[192,192]{1,0:T(8,128)S(1)} %get-tuple-element.30.y_i, ...), custom_call_target="tpu_custom_call" | custom-call | flops 4 | bytes 1 | tf_op jit(solution)/shard_map/z_own/pallas_call | solution.py:617
  16.9 1.7 %collective-permute-start.6 = (f32[12,24,128]{2,1,0:T(8,128)S(1)}, f32[12,24,128]{2,1,0:T(8,128)S(1)}, u32[]{:S(2)}, u32[]{:S(2)}) collective-permute-start(f32[12,24,128]{2,1,0:T(8,128)S(1)} %get-tuple-element.47), channel_id=1, source_target_pairs={{0,4},{2,6},{4,0},{6,2},{1,5},{3,7},{5,1},{7,3},{8,12},{10,14},{12... | collective-permute-start | bytes 442376 | tf_op jit(solution)/shard_map/ppermute | solution.py:775
  18.6 1.5 %collective-permute-start.4 = (f32[13,24,128]{2,1,0:T(8,128)S(1)}, f32[13,24,128]{2,1,0:T(8,128)S(1)}, u32[]{:S(2)}, u32[]{:S(2)}) collective-permute-start(f32[13,24,128]{2,1,0:T(8,128)S(1)} %get-tuple-element.45.own_right_ref), channel_id=1, source_target_pairs={{0,2},{2,4},{4,6},{6,0},{1,3},{3,5},{5,7},{7,1},{8,10},{10,12},{12... | collective-permute-start | bytes 479240 | tf_op jit(solution)/shard_map/ppermute | solution.py:780
  20.1 1.4 %collective-permute-start.5 = (f32[13,24,128]{2,1,0:T(8,128)S(1)}, f32[13,24,128]{2,1,0:T(8,128)S(1)}, u32[]{:S(2)}, u32[]{:S(2)}) collective-permute-start(f32[13,24,128]{2,1,0:T(8,128)S(1)} %get-tuple-element.46.own_left_ref), channel_id=1, source_target_pairs={{0,6},{2,0},{4,2},{6,4},{1,7},{3,1},{5,3},{7,5},{8,14},{10,8},{12,... | collective-permute-start | bytes 479240 | tf_op jit(solution)/shard_map/ppermute | solution.py:781
  21.5 0.0 collective-permute-done.after_ref.near_ref
  21.5 3.2 %y_solve.1 = (f32[3,16,192,128]{3,2,1,0:T(8,128)S(1)}, f32[3,16,192,128]{3,2,1,0:T(8,128)S(1)}, f32[6,192,128]{2,1,0:T(8,128)S(1)}) custom-call(bf16[192,192]{1,0:T(8,128)(2,1)S(1)} %get-tuple-element.34.high_ref, bf16[192,192]{1,0:T(8,128)(2,1)S(1)} %get-tuple-element.35.low_ref, ...), custom_call_target="tpu_custom_call", output_to_operand_aliasing={{0}: (3, {}), {1}: (4, {})} | custom-call | flops 20000000000 | bytes 1 | tf_op jit(solution)/shard_map/y_solve/pallas_call | solution.py:511
  24.7 0.0 copy-start
  24.7 2.2 %copy-done = f32[3,16,192,128]{3,2,1,0:T(8,128)} copy-done((f32[3,16,192,128]{3,2,1,0:T(8,128)}, f32[3,16,192,128]{3,2,1,0:T(8,128)S(1)}, u32[]{:S(2)}) %copy-start) | copy-done | bytes 4718616
  26.9 0.0 copy-start.1
  26.9 2.3 %copy-done.1 = f32[3,16,192,128]{3,2,1,0:T(8,128)S(1)} copy-done((f32[3,16,192,128]{3,2,1,0:T(8,128)S(1)}, f32[3,16,192,128]{3,2,1,0:T(8,128)}, u32[]{:S(2)}) %copy-start.1) | copy-done | bytes 4718616
  29.2 2.3 %x_gradient_own.1 = (f32[3,3,16,192,128]{4,3,2,1,0:T(8,128)}, f32[3,16,192,128]{3,2,1,0:T(8,128)S(1)}) custom-call(f32[121,8,128]{2,1,0:T(8,128)S(1)} %get-tuple-element.28.table_ref, f32[3,16,192,128]{3,2,1,0:T(8,128)S(1)} %bitcast.4, f32[3,192,128]{2,1,0:T(8,128)S(1)} %collective-permute-done.after_ref.near_ref, ...), custom_call_target="tpu_custom_call" | custom-call | flops 4 | bytes 1 | tf_op jit(solution)/shard_map/x_gradient_own/pallas_call | solution.py:360
  31.6 0.0 collective-permute-done.2.wr_ref
  31.6 0.5 %x_face.1 = (f32[6,192,128]{2,1,0:T(8,128)S(1)}, f32[1160,128]{1,0:T(8,128)S(1)}) custom-call(f32[121,8,128]{2,1,0:T(8,128)S(1)} %get-tuple-element.28.table_ref, f32[1160,128]{1,0:T(8,128)S(1)} %collective-permute-done.2.wr_ref, f32[1160,128]{1,0:T(8,128)S(1)} %x_ends.1.after_ref.ws_ref, f32[6,192,128]{2,1,0:T(8,128)S(1)} %get-tuple-element.38.l_ref, ...), custom_call_target="tpu_custom_call" | custom-call | flops 4 | bytes 1 | tf_op jit(solution)/shard_map/x_face/pallas_call | solution.py:290
  32.1 0.1 collective-permute-start.3
  32.2 0.0 collective-permute-done.6.left_2_ref.right_2_ref
  32.2 0.0 collective-permute-done.4.left_ref
  32.2 0.0 collective-permute-done.5.right_ref
  32.2 2.1 %z_gradient_join.1 = (f32[3,16,192,128]{3,2,1,0:T(8,128)S(1)}, bf16[16,192,96]{2,1,0:T(8,128)(2,1)S(1)}, bf16[96,768]{1,0:T(8,128)(2,1)S(1)}) custom-call(f32[128,128]{1,0:T(8,128)S(1)} %get-tuple-element.32.inv_ref, f32[1,128]{1,0:T(1,128)S(1)} %get-tuple-element.33.m_ref, ...), custom_call_target="tpu_custom_call", output_to_operand_aliasing={{0}: (2, {})} | custom-call | flops 20000000000 | bytes 1 | tf_op jit(solution)/shard_map/z_gradient_join/pallas_call | solution.py:733
  34.3 0.0 collective-permute-done.3.r_ref
  34.3 5.3 %x_solve.1 = (f32[3,3,16,192,128]{4,3,2,1,0:T(8,128)}, f32[3,16,192,128]{3,2,1,0:T(8,128)}) custom-call(f32[121,8,128]{2,1,0:T(8,128)S(1)} %get-tuple-element.28.table_ref, f32[3,16,192,128]{3,2,1,0:T(8,128)S(1)} %bitcast.4, f32[3,192,128]{2,1,0:T(8,128)S(1)} %collective-permute-done.after_ref.near_ref, ...), custom_call_target="tpu_custom_call", output_to_operand_aliasing={{0}: (12, {})} | custom-call | flops 4 | bytes 1 | tf_op jit(solution)/shard_map/x_solve/pallas_call | solution.py:450
  (1 shorter events, 0.0 us)
Async XLA Ops:
  0.6 8.1 %slice-start = ((s8[4718592]{0:T(1024)(128)(4,1)}), s8[4194304]{0:T(1024)(128)(4,1)S(1)}, s32[]{:S(2)}) async-start(s8[4718592]{0:T(1024)(128)(4,1)} %bitcast.3), calls=%async_computation | async-start | bytes 8388608
  2.1 19.4 %collective-permute-start = (f32[3,192,128]{2,1,0:T(8,128)S(1)}, f32[3,192,128]{2,1,0:T(8,128)S(1)}, u32[]{:S(2)}, u32[]{:S(2)}) collective-permute-start(f32[3,192,128]{2,1,0:T(8,128)S(1)} %get-tuple-element.27.after_ref.own_ref), channel_id=1, source_target_pairs={{1,8},{9,16},{17,24},{25,0},{8,1},{16,9},{24,17},{0,25},{3,10},{11... | collective-permute-start | bytes 884744 | tf_op jit(solution)/shard_map/ppermute | solution.py:762
  6.7 2.0 %collective-permute-start.1 = (f32[3,2,192,128]{3,2,1,0:T(8,128)S(1)}, f32[3,2,192,128]{3,2,1,0:T(8,128)S(1)}, u32[]{:S(2)}, u32[]{:S(2)}) collective-permute-start(f32[3,2,192,128]{3,2,1,0:T(8,128)S(1)} %get-tuple-element.29), channel_id=1, source_target_pairs={{0,1},{1,0},{2,3},{3,2},{4,5},{5,4},{6,7},{7,6},{8,9},{9,8},{10,11... | collective-permute-start | bytes 1769480 | tf_op jit(solution)/shard_map/ppermute | solution.py:763
  6.7 2.0 %slice-start.1 = ((s8[4718592]{0:T(1024)(128)(4,1)}), s8[524288]{0:T(1024)(128)(4,1)S(1)}, s32[]{:S(2)}) async-start(s8[4718592]{0:T(1024)(128)(4,1)} %bitcast.3), calls=%async_computation.1 | async-start | bytes 1048576
  10.2 21.4 %collective-permute-start.2 = (f32[1160,128]{1,0:T(8,128)S(1)}, f32[1160,128]{1,0:T(8,128)S(1)}, u32[]{:S(2)}, u32[]{:S(2)}) collective-permute-start(f32[1160,128]{1,0:T(8,128)S(1)} %x_ends.1.after_ref.ws_ref), channel_id=1, source_target_pairs={{1,8},{9,16},{17,24},{25,0},{8,1},{16,9},{24,17},{0,25},{3,10},{11... | collective-permute-start | bytes 1781768 | tf_op jit(solution)/shard_map/ppermute | solution.py:770
  16.9 15.3 %collective-permute-start.6 = (f32[12,24,128]{2,1,0:T(8,128)S(1)}, f32[12,24,128]{2,1,0:T(8,128)S(1)}, u32[]{:S(2)}, u32[]{:S(2)}) collective-permute-start(f32[12,24,128]{2,1,0:T(8,128)S(1)} %get-tuple-element.47), channel_id=1, source_target_pairs={{0,4},{2,6},{4,0},{6,2},{1,5},{3,7},{5,1},{7,3},{8,12},{10,14},{12... | collective-permute-start | bytes 442376 | tf_op jit(solution)/shard_map/ppermute | solution.py:775
  18.6 13.6 %collective-permute-start.4 = (f32[13,24,128]{2,1,0:T(8,128)S(1)}, f32[13,24,128]{2,1,0:T(8,128)S(1)}, u32[]{:S(2)}, u32[]{:S(2)}) collective-permute-start(f32[13,24,128]{2,1,0:T(8,128)S(1)} %get-tuple-element.45.own_right_ref), channel_id=1, source_target_pairs={{0,2},{2,4},{4,6},{6,0},{1,3},{3,5},{5,7},{7,1},{8,10},{10,12},{12... | collective-permute-start | bytes 479240 | tf_op jit(solution)/shard_map/ppermute | solution.py:780
  20.1 12.1 %collective-permute-start.5 = (f32[13,24,128]{2,1,0:T(8,128)S(1)}, f32[13,24,128]{2,1,0:T(8,128)S(1)}, u32[]{:S(2)}, u32[]{:S(2)}) collective-permute-start(f32[13,24,128]{2,1,0:T(8,128)S(1)} %get-tuple-element.46.own_left_ref), channel_id=1, source_target_pairs={{0,6},{2,0},{4,2},{6,4},{1,7},{3,1},{5,3},{7,5},{8,14},{10,8},{12,... | collective-permute-start | bytes 479240 | tf_op jit(solution)/shard_map/ppermute | solution.py:781
  24.7 2.2 %copy-start = (f32[3,16,192,128]{3,2,1,0:T(8,128)}, f32[3,16,192,128]{3,2,1,0:T(8,128)S(1)}, u32[]{:S(2)}) copy-start(f32[3,16,192,128]{3,2,1,0:T(8,128)S(1)} %get-tuple-element.39.y_ref) | copy-start | bytes 14155780
  26.9 2.3 %copy-start.1 = (f32[3,16,192,128]{3,2,1,0:T(8,128)S(1)}, f32[3,16,192,128]{3,2,1,0:T(8,128)}, u32[]{:S(2)}) copy-start(f32[3,16,192,128]{3,2,1,0:T(8,128)} %copy-done) | copy-start | bytes 14155780
  32.1 2.2 %collective-permute-start.3 = (f32[1160,128]{1,0:T(8,128)S(1)}, f32[1160,128]{1,0:T(8,128)S(1)}, u32[]{:S(2)}, u32[]{:S(2)}) collective-permute-start(f32[1160,128]{1,0:T(8,128)S(1)} %get-tuple-element.42.after_ref.e_ref), channel_id=1, source_target_pairs={{0,1},{1,0},{2,3},{3,2},{4,5},{5,4},{6,7},{7,6},{8,9},{9,8},{10,11... | collective-permute-start | bytes 1781768 | tf_op jit(solution)/shard_map/ppermute | solution.py:791
